TPU v7x, 32 devices: a whole 2x2x4 slice. The times are simulated.
32 devices in a mesh: ctx: 8 (over z, y), head: 4 (over x, core).
Axes of the slice: x: 2, y: 2, z: 4, core: 2. Of those that a mesh axis runs over, the one named last changes fastest.
Arguments:
- queries: bfloat16 [4096, 8192], P(('ctx', 'head')), may hold values from -7.5 to 7.5
- keys: bfloat16 [4096, 1024], P(('ctx', 'head')), may hold values from -6 to 6
- values: bfloat16 [4096, 1024], P(('ctx', 'head')), may hold values from -6 to 6
- out_grad: bfloat16 [4096, 8192], P(('ctx', 'head')), may hold values from -6 to 6
- segment_tiles: int32 [8], replicated, may hold values from 1 to 8, 32 in all
- parent_list: int32 [8], replicated, may hold values from 0 to 6, as said below
Outputs:
- attn_out: bfloat16 [4096, 8192], P(('ctx', 'head'))
- query_grad: bfloat16 [4096, 8192], P(('ctx', 'head'))
- key_grad: bfloat16 [4096, 1024], P(('ctx', 'head'))
- value_grad: bfloat16 [4096, 1024], P(('ctx', 'head'))
Inputs may be any that keep to these rules, and one draw needn't show every extreme that they name: parent_list[0] is 0, the root; the parent of every other segment comes before it, and no segment lies more than 3 levels below the root.
All inputs are finite; a program needn't handle non-finite values.
Results may differ from a plain program's by a relative error of at most 0.017.
Values may be sent and summed in bfloat16 or wider, within the bound.
No kernel may reach another device: no remote copies, remote signals or barrier semaphores. Data moves between devices by JAX's collectives and lax.ppermute only.
A program may use at most 128 MiB of HBM per device.

v0:
```python
import functools
import math

import jax
import jax.numpy as jnp
from jax import lax
from jax.experimental import pallas as pl
from jax.experimental.pallas import tpu as pltpu
from jax.sharding import PartitionSpec as P

HD = 128
TILE = 128
LEVELS = 4
MOST = 8
NEG = -1e30
SCALE = 1.0 / math.sqrt(HD)
LOG2E = 1.4426950408889634
bf16 = jnp.bfloat16
f32 = jnp.float32


def visible_lists(segment_tiles, parent_list, first, here, tiles, slot_of):
    count = segment_tiles.shape[0]
    ends = jnp.cumsum(segment_tiles, dtype=jnp.int32)
    numbers = jnp.arange(count, dtype=jnp.int32)
    key_tiles = jnp.arange(tiles, dtype=jnp.int32)
    key_seg = jnp.sum((key_tiles[:, None] >= ends[None, :]).astype(jnp.int32), axis=1)
    mine = first + jnp.arange(here, dtype=jnp.int32)
    seg = jnp.sum((mine[:, None] >= ends[None, :]).astype(jnp.int32), axis=1)
    seen = jnp.zeros((here, tiles), jnp.bool_)
    for level in range(LEVELS):
        seen = seen | (seg[:, None] == key_seg[None, :])
        seg = jnp.sum(jnp.where(seg[:, None] == numbers[None, :], parent_list[None, :], 0), axis=1)
    seen = seen & (key_tiles[None, :] <= mine[:, None])
    rank = jnp.cumsum(seen.astype(jnp.int32), axis=1) - 1
    most = min(tiles, LEVELS * MOST)
    places = jnp.arange(most, dtype=jnp.int32)
    chosen = seen[:, :, None] & (rank[:, :, None] == places[None, None, :])
    lists = jnp.sum(jnp.where(chosen, slot_of[None, :, None], 0), axis=1)
    return lists.astype(jnp.int32), jnp.sum(seen.astype(jnp.int32), axis=1)


def mm(a, b, ca=1, cb=0):
    return lax.dot_general(a, b, (((ca,), (cb,)), ((), ())), preferred_element_type=f32)


def attend_kernel(
    vis, cnt, q, do, k, v, o, dq, dkv, kt, vt, qt, dt, s_buf, p_buf, o_acc, q_acc, dka, dva, *, heads, last
):
    t = pl.program_id(1)
    part = pl.program_id(2)
    rows = heads * TILE
    tiles = k.shape[0]

    @pl.when((t == 0) & (part == 0))
    def _():
        def prepare(i, c):
            kt[i] = k[i].T
            vt[i] = v[i].T
            dka[i] = jnp.zeros((HD, TILE), f32)
            dva[i] = jnp.zeros((HD, TILE), f32)
            return c

        lax.fori_loop(0, tiles, prepare, 0)

    for h in range(heads):
        cols = pl.ds(h * HD, HD)
        qt[:, cols] = q[0, :, cols].T
        dt[:, cols] = do[0, :, cols].T
    n = cnt[t]
    blocks = (n + 1) // 2

    def pair(ref, b, axis):
        return jnp.concatenate([ref[vis[t, 2 * b]], ref[vis[t, 2 * b + 1]]], axis=axis)

    def scores(b, m8, masked):
        s = mm(pair(k, b, 0), qt[...])
        if masked:
            key = lax.broadcasted_iota(jnp.int32, (2 * TILE, rows), 0)
            token = lax.broadcasted_iota(jnp.int32, (2 * TILE, rows), 1) % TILE
            s = jnp.where(key <= token + (1 - n % 2) * TILE, s, NEG)
        s_buf[b] = s
        return jnp.maximum(m8, jnp.max(s.reshape(2 * TILE // 8, 8, rows), axis=0))

    m8 = jnp.full((8, rows), NEG, f32)
    m8 = lax.fori_loop(0, blocks - 1, lambda b, c: scores(b, c, False), m8)
    m8 = scores(blocks - 1, m8, True)
    m = jnp.max(m8, axis=0, keepdims=True)

    o_acc[...] = jnp.zeros_like(o_acc)

    def weigh(b, l8):
        p = jnp.exp2((s_buf[b] - m) * (SCALE * LOG2E))
        pb = p.astype(bf16)
        p_buf[b] = pb
        o_acc[...] += mm(pair(vt, b, 1), pb)
        return l8 + jnp.sum(p.reshape(2 * TILE // 8, 8, rows), axis=0)

    l8 = lax.fori_loop(0, blocks, weigh, jnp.zeros((8, rows), f32))
    inv = 1.0 / jnp.sum(l8, axis=0, keepdims=True)
    ob = (o_acc[...] * inv).astype(bf16)
    db = (dt[...].astype(f32) * inv).astype(bf16)
    dt[...] = db
    rowdot = jnp.sum(db.astype(f32) * ob.astype(f32), axis=0, keepdims=True)
    for h in range(heads):
        cols = slice(h * HD, (h + 1) * HD)
        o[0, :, cols] = ob[:, cols].T

    q_acc[...] = jnp.zeros_like(q_acc)

    def back(b, c):
        pb = p_buf[b]
        dp = mm(pair(v, b, 0), dt[...])
        ds = (pb.astype(f32) * (dp - rowdot)).astype(bf16)
        dvt = mm(dt[...], pb, 1, 1)
        dkt = mm(qt[...], ds, 1, 1)
        q_acc[...] += mm(pair(kt, b, 1), ds)
        one = vis[t, 2 * b]
        two = vis[t, 2 * b + 1]
        dva[one] += dvt[:, :TILE]
        dva[two] += dvt[:, TILE:]
        dka[one] += dkt[:, :TILE]
        dka[two] += dkt[:, TILE:]
        return c

    lax.fori_loop(0, blocks, back, 0)
    qb = (q_acc[...] * SCALE).astype(bf16)
    for h in range(heads):
        cols = slice(h * HD, (h + 1) * HD)
        dq[0, :, cols] = qb[:, cols].T

    @pl.when((t == last[0]) & (part == last[1]))
    def _():
        def finish(i, c):
            dkv[i, :, :HD] = (dka[i] * SCALE).astype(bf16).T
            dkv[i, :, HD:] = dva[i].astype(bf16).T
            return c

        lax.fori_loop(0, tiles, finish, 0)


def attend(vis, cnt, q, do, kv, heads):
    here, _, width = q.shape
    tiles = kv.shape[0]
    groups = width // (heads * TILE)
    most = vis.shape[1]
    parts = 1 if tiles <= 64 else 2
    heads = heads // parts
    rows = heads * TILE
    rowspec = pl.BlockSpec((1, TILE, rows), lambda g, t, p, *_: (t, 0, g * parts + p))
    keyspec = pl.BlockSpec((tiles, TILE, HD), lambda g, t, p, *_: (0, 0, 2 * g), pipeline_mode=pl.Buffered(1))
    valspec = pl.BlockSpec((tiles, TILE, HD), lambda g, t, p, *_: (0, 0, 2 * g + 1), pipeline_mode=pl.Buffered(1))
    gradspec = pl.BlockSpec((tiles, TILE, 2 * HD), lambda g, t, p, *_: (0, 0, g), pipeline_mode=pl.Buffered(1))
    return pl.pallas_call(
        functools.partial(attend_kernel, heads=heads, last=(here - 1, parts - 1)),
        grid_spec=pltpu.PrefetchScalarGridSpec(
            num_scalar_prefetch=2,
            grid=(groups, here, parts),
            in_specs=[rowspec, rowspec, keyspec, valspec],
            out_specs=[rowspec, rowspec, gradspec],
            scratch_shapes=[
                pltpu.VMEM((tiles, HD, TILE), bf16),
                pltpu.VMEM((tiles, HD, TILE), bf16),
                pltpu.VMEM((HD, rows), bf16),
                pltpu.VMEM((HD, rows), bf16),
                pltpu.VMEM((most // 2, 2 * TILE, rows), f32),
                pltpu.VMEM((most // 2, 2 * TILE, rows), bf16),
                pltpu.VMEM((HD, rows), f32),
                pltpu.VMEM((HD, rows), f32),
                pltpu.VMEM((tiles, HD, TILE), f32),
                pltpu.VMEM((tiles, HD, TILE), f32),
            ],
        ),
        out_shape=[
            jax.ShapeDtypeStruct((here, TILE, width), bf16),
            jax.ShapeDtypeStruct((here, TILE, width), bf16),
            jax.ShapeDtypeStruct((tiles, TILE, 2 * HD * groups), bf16),
        ],
        compiler_params=pltpu.CompilerParams(vmem_limit_bytes=63 << 20),
        cost_estimate=pl.CostEstimate(flops=40_000_000_000, bytes_accessed=20_000_000, transcendentals=20_000_000),
        name="attend",
    )(vis, cnt, q, do, kv, kv)


def snake(z_size, y_size):
    order = [z * y_size for z in range(z_size)]
    for z in reversed(range(z_size)):
        across = range(1, y_size)
        order += [z * y_size + y for y in (across if (z_size - 1 - z) % 2 == 0 else reversed(across))]
    return order


def ring_gather(block, forth, back, size):
    up = down = block
    got = [block]
    for step in range(size // 2 - 1):
        up = lax.ppermute(up, "ctx", forth)
        down = lax.ppermute(down, "ctx", back)
        got += [up, down]
    half = block.shape[-1] // 2
    up = lax.ppermute(up[..., :half], "ctx", forth)
    down = lax.ppermute(down[..., half:], "ctx", back)
    return got + [jnp.concatenate([up, down], axis=-1)]


def ring_sum(parts, forth, back, size):
    half = parts[0].shape[-1] // 2
    far = parts[size - 1]
    up, down = lax.ppermute(far[..., :half], "ctx", back), lax.ppermute(far[..., half:], "ctx", forth)

    def add(a, b):
        return (a.astype(f32) + b.astype(f32)).astype(bf16)

    for step in reversed(range(size // 2 - 1)):
        mine_up, mine_down = parts[1 + 2 * step], parts[2 + 2 * step]
        if step == size // 2 - 2:
            up = jnp.concatenate([add(mine_up[..., :half], up), mine_up[..., half:]], axis=-1)
            down = jnp.concatenate([mine_down[..., :half], add(mine_down[..., half:], down)], axis=-1)
        else:
            up, down = add(mine_up, up), add(mine_down, down)
        up, down = lax.ppermute(up, "ctx", back), lax.ppermute(down, "ctx", forth)
    return (parts[0].astype(f32) + up.astype(f32) + down.astype(f32)).astype(bf16)


def local(queries, keys, values, out_grad, segment_tiles, parent_list):
    rows_here, key_width = keys.shape
    ctx, heads_axis = lax.axis_size("ctx"), lax.axis_size("head")
    groups = key_width // HD // heads_axis
    heads = queries.shape[1] // key_width
    tiles = ctx * heads_axis * rows_here // TILE
    here = tiles // ctx

    y_size = heads_axis // 2
    order = snake(ctx // y_size, y_size)
    forth = [(order[i], order[(i + 1) % ctx]) for i in range(ctx)]
    back = [(b, a) for a, b in forth]
    place = [order.index(c) for c in range(ctx)]
    piece_of = [0] * ctx
    for d in range(1, ctx):
        piece_of[d] = 2 * d - 1 if d <= ctx // 2 else 2 * (ctx - d)
    me = lax.axis_index("ctx")
    places = jnp.asarray(place, jnp.int32)
    my_place = jnp.sum(jnp.where(jnp.arange(ctx) == me, places, 0))
    distance = jnp.repeat(jnp.mod(my_place - places, ctx), here)
    table = jnp.asarray(piece_of, jnp.int32)
    piece = jnp.sum(jnp.where(distance[:, None] == jnp.arange(ctx)[None, :], table[None, :], 0), axis=1)
    slot_of = piece * here + jnp.arange(tiles, dtype=jnp.int32) % here
    vis, cnt = visible_lists(segment_tiles, parent_list, me * here, here, tiles, slot_of)

    def swap(x):
        return lax.all_to_all(x, "head", split_axis=0, concat_axis=0, tiled=True)

    def to_heads(x):
        x = x.reshape(rows_here, heads_axis, -1).transpose(1, 0, 2)
        return swap(x).reshape(here, TILE, -1)

    def to_tokens(x):
        return swap(x.reshape(heads_axis, rows_here, -1)).transpose(1, 0, 2)

    kv = jnp.concatenate(
        [keys.reshape(rows_here, heads_axis, groups, HD), values.reshape(rows_here, heads_axis, groups, HD)], axis=3
    )
    kv = to_heads(kv)
    kv = jnp.concatenate(ring_gather(kv, forth, back, ctx), axis=0)
    q = to_heads(queries)
    do = to_heads(out_grad)

    o, dq, dkv = attend(vis, cnt, q, do, kv, heads)

    o = to_tokens(o).reshape(queries.shape)
    dq = to_tokens(dq).reshape(queries.shape)
    dkv = ring_sum([dkv[i * here : (i + 1) * here] for i in range(ctx)], forth, back, ctx)
    dkv = to_tokens(dkv).reshape(rows_here, heads_axis, groups, 2, HD)
    dk = dkv[:, :, :, 0].reshape(keys.shape)
    dv = dkv[:, :, :, 1].reshape(values.shape)
    return o, dq, dk, dv


def solution(mesh):
    rows = P(("ctx", "head"), None)
    return jax.shard_map(
        local,
        mesh=mesh,
        in_specs=(rows, rows, rows, rows, P(), P()),
        out_specs=(rows, rows, rows, rows),
        check_vma=False,
    )
```

profile of v0, /device:TPU:0, one launch (start us, length us, event | category | flops | bytes accessed | tf_op | source)
XLA Modules:
  0.0 257.2 jit_solution(16466600247463015049)
XLA Ops:
  4.7 4.2 %all-to-all-start.2 = ((bf16[4,128,512]{2,1,0:T(8,128)(2,1)}), bf16[4,128,512]{2,1,0:T(8,128)(2,1)S(1)}, u32[]{:S(2)}, u32[]{:S(2)}) async-start(bf16[4,128,512]{2,1,0:T(8,128)(2,1)} %bitcast.19), calls=%async_computation.2 | async-start | bytes 1048576 | tf_op jit(solution)/shard_map/all_to_all | solution.py:251
  8.9 3.2 %copy.28 = bf16[128,8192]{0,1:T(8,128)(2,1)S(1)} copy(bf16[128,8192]{1,0:T(8,128)(2,1)} %param.8) | data formatting | bytes 4194304 | tf_op args[0]
  12.1 2.6 %copy.29 = bf16[128,4,2048]{2,0,1:T(8,128)(2,1)} copy(bf16[128,4,2048]{0,2,1:T(8,128)(2,1)S(1)} %bitcast.23) | data formatting | bytes 4194304 | tf_op jit(solution)/shard_map/reshape | solution.py:254
  14.7 3.0 %all-to-all-done.2 = bf16[4,128,512]{2,1,0:T(8,128)(2,1)S(1)} async-done(((bf16[4,128,512]{2,1,0:T(8,128)(2,1)}), bf16[4,128,512]{2,1,0:T(8,128)(2,1)S(1)}, u32[]{:S(2)}, u32[]{:S(2)}) %all-to-all-start.2) | async-done | bytes 524320 | tf_op jit(solution)/shard_map/all_to_all | solution.py:251
  17.7 4.5 %all-to-all-start = ((bf16[4,128,2048]{2,1,0:T(8,128)(2,1)}), bf16[4,128,2048]{2,1,0:T(8,128)(2,1)}, u32[]{:S(2)}, u32[]{:S(2)}) async-start(bf16[4,128,2048]{2,1,0:T(8,128)(2,1)} %bitcast.3), calls=%async_computation | async-start | bytes 4194304 | tf_op jit(solution)/shard_map/all_to_all | solution.py:251
  23.7 3.2 %copy.30 = bf16[128,8192]{0,1:T(8,128)(2,1)S(1)} copy(bf16[128,8192]{1,0:T(8,128)(2,1)} %param.11) | data formatting | bytes 4194304 | tf_op args[3]
  26.9 2.6 %copy.31 = bf16[128,4,2048]{2,0,1:T(8,128)(2,1)} copy(bf16[128,4,2048]{0,2,1:T(8,128)(2,1)S(1)} %bitcast.24) | data formatting | bytes 4194304 | tf_op jit(solution)/shard_map/reshape | solution.py:254
  30.1 2.2 collective-permute-start.1
  33.6 11.3 %collective-permute-done.1 = bf16[4,128,512]{2,1,0:T(8,128)(2,1)S(1)} collective-permute-done((bf16[4,128,512]{2,1,0:T(8,128)(2,1)S(1)}, bf16[4,128,512]{2,1,0:T(8,128)(2,1)S(1)}, u32[]{:S(2)}, u32[]{:S(2)}) %collective-permute-start.1) | collective-permute-done | bytes 524320 | tf_op jit(solution)/shard_map/ppermute | solution.py:198
  48.0 4.5 %all-to-all-start.1 = ((bf16[4,128,2048]{2,1,0:T(8,128)(2,1)}), bf16[4,128,2048]{2,1,0:T(8,128)(2,1)}, u32[]{:S(2)}, u32[]{:S(2)}) async-start(bf16[4,128,2048]{2,1,0:T(8,128)(2,1)} %bitcast.5), calls=%async_computation.1 | async-start | bytes 4194304 | tf_op jit(solution)/shard_map/all_to_all | solution.py:251
  52.8 6.0 %collective-permute-done.3 = bf16[4,128,512]{2,1,0:T(8,128)(2,1)S(1)} collective-permute-done((bf16[4,128,512]{2,1,0:T(8,128)(2,1)S(1)}, bf16[4,128,512]{2,1,0:T(8,128)(2,1)S(1)}, u32[]{:S(2)}, u32[]{:S(2)}) %collective-permute-start.3) | collective-permute-done | bytes 524320 | tf_op jit(solution)/shard_map/ppermute | solution.py:198
  64.8 7.0 %collective-permute-done.5 = bf16[4,128,512]{2,1,0:T(8,128)(2,1)S(1)} collective-permute-done((bf16[4,128,512]{2,1,0:T(8,128)(2,1)S(1)}, bf16[4,128,512]{2,1,0:T(8,128)(2,1)S(1)}, u32[]{:S(2)}, u32[]{:S(2)}) %collective-permute-start.5) | collective-permute-done | bytes 524320 | tf_op jit(solution)/shard_map/ppermute | solution.py:198
  80.4 36.9 %attend.1 = (bf16[4,128,2048]{2,1,0:T(8,128)(2,1)}, bf16[4,128,2048]{2,1,0:T(8,128)(2,1)}, bf16[32,128,512]{2,1,0:T(8,128)(2,1)}) custom-call(s32[4,32]{1,0:T(4,128)} %select_reduce_fusion.vis, s32[4]{0:T(128)} %get-tuple-element.18.cnt, bf16[4,128,2048]{2,1,0:T(8,128)(2,1)} %all-to-all-done.q, bf16[4,128,2048]{2,1,0:T(8,128)(2,1)} %all-to-all-done.1.do, ...), custom_call_target="tpu_custom_call" | custom-call | flops 40000000000 | bytes 20000000 | tf_op jit(solution)/shard_map/attend/pallas_call | solution.py:154
  118.7 22.4 %collective-permute-start.8 = (bf16[4,128,256]{2,1,0:T(8,128)(2,1)S(1)}, bf16[4,128,256]{2,1,0:T(8,128)(2,1)S(1)}, u32[]{:S(2)}, u32[]{:S(2)}) collective-permute-start(bf16[4,128,256]{2,1,0:T(8,128)(2,1)S(1)} %get-tuple-element.24), channel_id=1, source_target_pairs={{8,0},{16,8},{24,16},{28,24},{20,28},{12,20},{4,12},{0,4},{9,1},{1... | collective-permute-start | bytes 786440 | tf_op jit(solution)/shard_map/ppermute | solution.py:209
  141.0 20.0 %collective-permute-start.12 = (bf16[4,128,256]{2,1,0:T(8,128)(2,1)S(1)}, bf16[4,128,256]{2,1,0:T(8,128)(2,1)S(1)}, u32[]{:S(2)}, u32[]{:S(2)}) collective-permute-start(bf16[4,128,256]{2,1,0:T(8,128)(2,1)S(1)} %get-tuple-element.25), channel_id=1, source_target_pairs={{0,8},{8,16},{16,24},{24,28},{28,20},{20,12},{12,4},{4,0},{1,9},{9... | collective-permute-start | bytes 786440 | tf_op jit(solution)/shard_map/ppermute | solution.py:209
  161.1 5.3 %collective-permute-done.8 = bf16[4,128,256]{2,1,0:T(8,128)(2,1)S(1)} collective-permute-done((bf16[4,128,256]{2,1,0:T(8,128)(2,1)S(1)}, bf16[4,128,256]{2,1,0:T(8,128)(2,1)S(1)}, u32[]{:S(2)}, u32[]{:S(2)}) %collective-permute-start.8) | collective-permute-done | bytes 262176 | tf_op jit(solution)/shard_map/ppermute | solution.py:209
  168.4 3.6 %all-to-all-start.3 = ((bf16[4,128,2048]{2,1,0:T(8,128)(2,1)}), bf16[4,128,2048]{2,1,0:T(8,128)(2,1)S(1)}, u32[]{:S(2)}, u32[]{:S(2)}) async-start(bf16[4,128,2048]{2,1,0:T(8,128)(2,1)} %get-tuple-element.7), calls=%async_computation.3 | async-start | bytes 4194304 | tf_op jit(solution)/shard_map/all_to_all | solution.py:251
  172.0 12.0 %collective-permute-start.13 = (bf16[4,128,512]{2,1,0:T(8,128)(2,1)S(1)}, bf16[4,128,512]{2,1,0:T(8,128)(2,1)S(1)}, u32[]{:S(2)}, u32[]{:S(2)}) collective-permute-start(bf16[4,128,512]{2,1,0:T(8,128)(2,1)S(1)} %pad_maximum_fusion.2), channel_id=1, source_target_pairs={{0,8},{8,16},{16,24},{24,28},{28,20},{20,12},{12,4},{4,0},{1,9},{9... | collective-permute-start | bytes 1572872 | tf_op jit(solution)/shard_map/ppermute | solution.py:221
  184.0 7.1 %collective-permute-done.9 = bf16[4,128,512]{2,1,0:T(8,128)(2,1)S(1)} collective-permute-done((bf16[4,128,512]{2,1,0:T(8,128)(2,1)}, bf16[4,128,512]{2,1,0:T(8,128)(2,1)S(1)}, u32[]{:S(2)}, u32[]{:S(2)}) %collective-permute-start.9) | collective-permute-done | bytes 524320 | tf_op jit(solution)/shard_map/ppermute | solution.py:221
  192.4 3.5 %collective-permute-done.13 = bf16[4,128,512]{2,1,0:T(8,128)(2,1)S(1)} collective-permute-done((bf16[4,128,512]{2,1,0:T(8,128)(2,1)S(1)}, bf16[4,128,512]{2,1,0:T(8,128)(2,1)S(1)}, u32[]{:S(2)}, u32[]{:S(2)}) %collective-permute-start.13) | collective-permute-done | bytes 524320 | tf_op jit(solution)/shard_map/ppermute | solution.py:221
  195.8 8.2 %collective-permute-done.10 = bf16[4,128,512]{2,1,0:T(8,128)(2,1)S(1)} collective-permute-done((bf16[4,128,512]{2,1,0:T(8,128)(2,1)S(1)}, bf16[4,128,512]{2,1,0:T(8,128)(2,1)S(1)}, u32[]{:S(2)}, u32[]{:S(2)}) %collective-permute-start.10) | collective-permute-done | bytes 524320 | tf_op jit(solution)/shard_map/ppermute | solution.py:221
  204.1 2.3 add_convert_fusion.3
  207.9 4.5 %all-to-all-start.4 = ((bf16[4,128,2048]{2,1,0:T(8,128)(2,1)}), bf16[4,128,2048]{2,1,0:T(8,128)(2,1)}, u32[]{:S(2)}, u32[]{:S(2)}) async-start(bf16[4,128,2048]{2,1,0:T(8,128)(2,1)} %get-tuple-element.8), calls=%async_computation.4 | async-start | bytes 4194304 | tf_op jit(solution)/shard_map/all_to_all | solution.py:251
  212.9 4.5 %collective-permute-done.14 = bf16[4,128,512]{2,1,0:T(8,128)(2,1)S(1)} collective-permute-done((bf16[4,128,512]{2,1,0:T(8,128)(2,1)}, bf16[4,128,512]{2,1,0:T(8,128)(2,1)S(1)}, u32[]{:S(2)}, u32[]{:S(2)}) %collective-permute-start.14) | collective-permute-done | bytes 524320 | tf_op jit(solution)/shard_map/ppermute | solution.py:221
  219.9 6.7 %collective-permute-done.11 = bf16[4,128,512]{2,1,0:T(8,128)(2,1)S(1)} collective-permute-done((bf16[4,128,512]{2,1,0:T(8,128)(2,1)S(1)}, bf16[4,128,512]{2,1,0:T(8,128)(2,1)S(1)}, u32[]{:S(2)}, u32[]{:S(2)}) %collective-permute-start.11) | collective-permute-done | bytes 524320 | tf_op jit(solution)/shard_map/ppermute | solution.py:221
  228.6 2.1 add_convert_fusion
  230.7 7.4 %all-to-all-done.4 = bf16[4,128,2048]{2,1,0:T(8,128)(2,1)} async-done(((bf16[4,128,2048]{2,1,0:T(8,128)(2,1)}), bf16[4,128,2048]{2,1,0:T(8,128)(2,1)}, u32[]{:S(2)}, u32[]{:S(2)}) %all-to-all-start.4) | async-done | bytes 2097184 | tf_op jit(solution)/shard_map/all_to_all | solution.py:251
  238.1 3.6 %all-to-all-start.5 = ((bf16[4,128,512]{2,1,0:T(8,128)(2,1)}), bf16[4,128,512]{2,1,0:T(8,128)(2,1)S(1)}, u32[]{:S(2)}, u32[]{:S(2)}) async-start(bf16[4,128,512]{2,1,0:T(8,128)(2,1)} %add_convert_fusion), calls=%async_computation.5 | async-start | bytes 1048576 | tf_op jit(solution)/shard_map/all_to_all | solution.py:251
  241.7 2.5 copy.34
  244.2 4.1 %copy.38 = bf16[128,8192]{1,0:T(8,128)(2,1)} copy(bf16[128,8192]{0,1:T(8,128)(2,1)} %bitcast.21) | data formatting | bytes 4194304
  248.3 3.0 %copy.35 = bf16[128,4,2048]{0,2,1:T(8,128)(2,1)S(1)} copy(bf16[128,4,2048]{2,0,1:T(8,128)(2,1)} %bitcast.9) | data formatting | bytes 4194304 | tf_op jit(solution)/shard_map/transpose | solution.py:258
  251.3 2.9 %copy.39 = bf16[128,8192]{1,0:T(8,128)(2,1)} copy(bf16[128,8192]{0,1:T(8,128)(2,1)S(1)} %bitcast.22) | data formatting | bytes 4194304
  (78 shorter events, 39.4 us)
Async XLA Ops:
  4.7 13.1 %all-to-all-start.2 = ((bf16[4,128,512]{2,1,0:T(8,128)(2,1)}), bf16[4,128,512]{2,1,0:T(8,128)(2,1)S(1)}, u32[]{:S(2)}, u32[]{:S(2)}) async-start(bf16[4,128,512]{2,1,0:T(8,128)(2,1)} %bitcast.19), calls=%async_computation.2 | async-start | bytes 1048576 | tf_op jit(solution)/shard_map/all_to_all | solution.py:251
  12.1 10.1 %copy-start.4 = (s32[8]{0:T(128)S(1)}, s32[8]{0:T(128)}, u32[]{:S(2)}) copy-start(s32[8]{0:T(128)} %constant.51.clone) | copy-start | bytes 100
  12.1 10.8 %copy-start.3 = (s32[8]{0:T(128)S(1)}, s32[8]{0:T(128)}, u32[]{:S(2)}) copy-start(s32[8]{0:T(128)} %constant.53) | copy-start | bytes 100
  17.7 30.3 %all-to-all-start = ((bf16[4,128,2048]{2,1,0:T(8,128)(2,1)}), bf16[4,128,2048]{2,1,0:T(8,128)(2,1)}, u32[]{:S(2)}, u32[]{:S(2)}) async-start(bf16[4,128,2048]{2,1,0:T(8,128)(2,1)} %bitcast.3), calls=%async_computation | async-start | bytes 4194304 | tf_op jit(solution)/shard_map/all_to_all | solution.py:251
  23.7 5.9 %copy-start = (s32[8]{0:T(128)S(1)}, s32[8]{0:T(128)}, u32[]{:S(2)}) copy-start(s32[8]{0:T(128)} %param.12) | copy-start | bytes 100
  23.7 6.2 %copy-start.1 = (s32[8]{0:T(128)S(1)}, s32[8]{0:T(128)}, u32[]{:S(2)}) copy-start(s32[8]{0:T(128)} %param.13) | copy-start | bytes 100
  26.9 25.5 %copy-start.2 = (s32[8]{0:T(128)S(1)}, s32[8]{0:T(128)}, u32[]{:S(2)}) copy-start(s32[8]{0:T(128)} %constant.52.clone) | copy-start | bytes 100
  30.1 14.8 %collective-permute-start.1 = (bf16[4,128,512]{2,1,0:T(8,128)(2,1)S(1)}, bf16[4,128,512]{2,1,0:T(8,128)(2,1)S(1)}, u32[]{:S(2)}, u32[]{:S(2)}) collective-permute-start(bf16[4,128,512]{2,1,0:T(8,128)(2,1)S(1)} %all-to-all-done.2), channel_id=1, source_target_pairs={{8,0},{16,8},{24,16},{28,24},{20,28},{12,20},{4,12},{0,4},{9,1},{1... | collective-permute-start | bytes 1572872 | tf_op jit(solution)/shard_map/ppermute | solution.py:198
  32.4 14.3 %collective-permute-start = (bf16[4,128,512]{2,1,0:T(8,128)(2,1)S(1)}, bf16[4,128,512]{2,1,0:T(8,128)(2,1)S(1)}, u32[]{:S(2)}, u32[]{:S(2)}) collective-permute-start(bf16[4,128,512]{2,1,0:T(8,128)(2,1)S(1)} %all-to-all-done.2), channel_id=1, source_target_pairs={{0,8},{8,16},{16,24},{24,28},{28,20},{20,12},{12,4},{4,0},{1,9},{9... | collective-permute-start | bytes 1572872 | tf_op jit(solution)/shard_map/ppermute | solution.py:197
  44.9 13.8 %collective-permute-start.3 = (bf16[4,128,512]{2,1,0:T(8,128)(2,1)S(1)}, bf16[4,128,512]{2,1,0:T(8,128)(2,1)S(1)}, u32[]{:S(2)}, u32[]{:S(2)}) collective-permute-start(bf16[4,128,512]{2,1,0:T(8,128)(2,1)S(1)} %collective-permute-done.1), channel_id=1, source_target_pairs={{8,0},{16,8},{24,16},{28,24},{20,28},{12,20},{4,12},{0,4},{9,1},{1... | collective-permute-start | bytes 1572872 | tf_op jit(solution)/shard_map/ppermute | solution.py:198
  46.6 13.6 %collective-permute-start.2 = (bf16[4,128,512]{2,1,0:T(8,128)(2,1)S(1)}, bf16[4,128,512]{2,1,0:T(8,128)(2,1)S(1)}, u32[]{:S(2)}, u32[]{:S(2)}) collective-permute-start(bf16[4,128,512]{2,1,0:T(8,128)(2,1)S(1)} %collective-permute-done), channel_id=1, source_target_pairs={{0,8},{8,16},{16,24},{24,28},{28,20},{20,12},{12,4},{4,0},{1,9},{9... | collective-permute-start | bytes 1572872 | tf_op jit(solution)/shard_map/ppermute | solution.py:197
  48.0 32.5 %all-to-all-start.1 = ((bf16[4,128,2048]{2,1,0:T(8,128)(2,1)}), bf16[4,128,2048]{2,1,0:T(8,128)(2,1)}, u32[]{:S(2)}, u32[]{:S(2)}) async-start(bf16[4,128,2048]{2,1,0:T(8,128)(2,1)} %bitcast.5), calls=%async_computation.1 | async-start | bytes 4194304 | tf_op jit(solution)/shard_map/all_to_all | solution.py:251
  58.7 13.1 %collective-permute-start.5 = (bf16[4,128,512]{2,1,0:T(8,128)(2,1)S(1)}, bf16[4,128,512]{2,1,0:T(8,128)(2,1)S(1)}, u32[]{:S(2)}, u32[]{:S(2)}) collective-permute-start(bf16[4,128,512]{2,1,0:T(8,128)(2,1)S(1)} %collective-permute-done.3), channel_id=1, source_target_pairs={{8,0},{16,8},{24,16},{28,24},{20,28},{12,20},{4,12},{0,4},{9,1},{1... | collective-permute-start | bytes 1572872 | tf_op jit(solution)/shard_map/ppermute | solution.py:198
  60.2 12.9 %collective-permute-start.4 = (bf16[4,128,512]{2,1,0:T(8,128)(2,1)S(1)}, bf16[4,128,512]{2,1,0:T(8,128)(2,1)S(1)}, u32[]{:S(2)}, u32[]{:S(2)}) collective-permute-start(bf16[4,128,512]{2,1,0:T(8,128)(2,1)S(1)} %collective-permute-done.2), channel_id=1, source_target_pairs={{0,8},{8,16},{16,24},{24,28},{28,20},{20,12},{12,4},{4,0},{1,9},{9... | collective-permute-start | bytes 1572872 | tf_op jit(solution)/shard_map/ppermute | solution.py:197
  71.8 6.7 %collective-permute-start.7 = (bf16[4,128,256]{2,1,0:T(8,128)(2,1)S(1)}, bf16[4,128,256]{2,1,0:T(8,128)(2,1)S(1)}, u32[]{:S(2)}, u32[]{:S(2)}) collective-permute-start(bf16[4,128,256]{2,1,0:T(8,128)(2,1)S(1)} %slice.70), channel_id=1, source_target_pairs={{8,0},{16,8},{24,16},{28,24},{20,28},{12,20},{4,12},{0,4},{9,1},{1... | collective-permute-start | bytes 786440 | tf_op jit(solution)/shard_map/ppermute | solution.py:202
  73.1 6.4 %collective-permute-start.6 = (bf16[4,128,256]{2,1,0:T(8,128)(2,1)S(1)}, bf16[4,128,256]{2,1,0:T(8,128)(2,1)S(1)}, u32[]{:S(2)}, u32[]{:S(2)}) collective-permute-start(bf16[4,128,256]{2,1,0:T(8,128)(2,1)S(1)} %slice.69), channel_id=1, source_target_pairs={{0,8},{8,16},{16,24},{24,28},{28,20},{20,12},{12,4},{4,0},{1,9},{9... | collective-permute-start | bytes 786440 | tf_op jit(solution)/shard_map/ppermute | solution.py:201
  118.7 47.7 %collective-permute-start.8 = (bf16[4,128,256]{2,1,0:T(8,128)(2,1)S(1)}, bf16[4,128,256]{2,1,0:T(8,128)(2,1)S(1)}, u32[]{:S(2)}, u32[]{:S(2)}) collective-permute-start(bf16[4,128,256]{2,1,0:T(8,128)(2,1)S(1)} %get-tuple-element.24), channel_id=1, source_target_pairs={{8,0},{16,8},{24,16},{28,24},{20,28},{12,20},{4,12},{0,4},{9,1},{1... | collective-permute-start | bytes 786440 | tf_op jit(solution)/shard_map/ppermute | solution.py:209
  141.0 25.3 %collective-permute-start.12 = (bf16[4,128,256]{2,1,0:T(8,128)(2,1)S(1)}, bf16[4,128,256]{2,1,0:T(8,128)(2,1)S(1)}, u32[]{:S(2)}, u32[]{:S(2)}) collective-permute-start(bf16[4,128,256]{2,1,0:T(8,128)(2,1)S(1)} %get-tuple-element.25), channel_id=1, source_target_pairs={{0,8},{8,16},{16,24},{24,28},{28,20},{20,12},{12,4},{4,0},{1,9},{9... | collective-permute-start | bytes 786440 | tf_op jit(solution)/shard_map/ppermute | solution.py:209
  168.4 22.8 %collective-permute-start.9 = (bf16[4,128,512]{2,1,0:T(8,128)(2,1)}, bf16[4,128,512]{2,1,0:T(8,128)(2,1)S(1)}, u32[]{:S(2)}, u32[]{:S(2)}) collective-permute-start(bf16[4,128,512]{2,1,0:T(8,128)(2,1)} %pad_maximum_fusion.1), channel_id=1, source_target_pairs={{8,0},{16,8},{24,16},{28,24},{20,28},{12,20},{4,12},{0,4},{9,1},{1... | collective-permute-start | bytes 1572872 | tf_op jit(solution)/shard_map/ppermute | solution.py:221
  168.4 39.5 %all-to-all-start.3 = ((bf16[4,128,2048]{2,1,0:T(8,128)(2,1)}), bf16[4,128,2048]{2,1,0:T(8,128)(2,1)S(1)}, u32[]{:S(2)}, u32[]{:S(2)}) async-start(bf16[4,128,2048]{2,1,0:T(8,128)(2,1)} %get-tuple-element.7), calls=%async_computation.3 | async-start | bytes 4194304 | tf_op jit(solution)/shard_map/all_to_all | solution.py:251
  172.0 23.8 %collective-permute-start.13 = (bf16[4,128,512]{2,1,0:T(8,128)(2,1)S(1)}, bf16[4,128,512]{2,1,0:T(8,128)(2,1)S(1)}, u32[]{:S(2)}, u32[]{:S(2)}) collective-permute-start(bf16[4,128,512]{2,1,0:T(8,128)(2,1)S(1)} %pad_maximum_fusion.2), channel_id=1, source_target_pairs={{0,8},{8,16},{16,24},{24,28},{28,20},{20,12},{12,4},{4,0},{1,9},{9... | collective-permute-start | bytes 1572872 | tf_op jit(solution)/shard_map/ppermute | solution.py:221
  192.3 11.8 %collective-permute-start.10 = (bf16[4,128,512]{2,1,0:T(8,128)(2,1)S(1)}, bf16[4,128,512]{2,1,0:T(8,128)(2,1)S(1)}, u32[]{:S(2)}, u32[]{:S(2)}) collective-permute-start(bf16[4,128,512]{2,1,0:T(8,128)(2,1)S(1)} %add_convert_fusion.4), channel_id=1, source_target_pairs={{8,0},{16,8},{24,16},{28,24},{20,28},{12,20},{4,12},{0,4},{9,1},{1... | collective-permute-start | bytes 1572872 | tf_op jit(solution)/shard_map/ppermute | solution.py:221
  206.4 11.1 %collective-permute-start.14 = (bf16[4,128,512]{2,1,0:T(8,128)(2,1)}, bf16[4,128,512]{2,1,0:T(8,128)(2,1)S(1)}, u32[]{:S(2)}, u32[]{:S(2)}) collective-permute-start(bf16[4,128,512]{2,1,0:T(8,128)(2,1)} %get-tuple-element.21), channel_id=1, source_target_pairs={{0,8},{8,16},{16,24},{24,28},{28,20},{20,12},{12,4},{4,0},{1,9},{9... | collective-permute-start | bytes 1572872 | tf_op jit(solution)/shard_map/ppermute | solution.py:221
  207.9 30.2 %all-to-all-start.4 = ((bf16[4,128,2048]{2,1,0:T(8,128)(2,1)}), bf16[4,128,2048]{2,1,0:T(8,128)(2,1)}, u32[]{:S(2)}, u32[]{:S(2)}) async-start(bf16[4,128,2048]{2,1,0:T(8,128)(2,1)} %get-tuple-element.8), calls=%async_computation.4 | async-start | bytes 4194304 | tf_op jit(solution)/shard_map/all_to_all | solution.py:251
  212.3 14.3 %collective-permute-start.11 = (bf16[4,128,512]{2,1,0:T(8,128)(2,1)S(1)}, bf16[4,128,512]{2,1,0:T(8,128)(2,1)S(1)}, u32[]{:S(2)}, u32[]{:S(2)}) collective-permute-start(bf16[4,128,512]{2,1,0:T(8,128)(2,1)S(1)} %get-tuple-element.20), channel_id=1, source_target_pairs={{8,0},{16,8},{24,16},{28,24},{20,28},{12,20},{4,12},{0,4},{9,1},{1... | collective-permute-start | bytes 1572872 | tf_op jit(solution)/shard_map/ppermute | solution.py:221
  218.6 10.0 %collective-permute-start.15 = (bf16[4,128,512]{2,1,0:T(8,128)(2,1)S(1)}, bf16[4,128,512]{2,1,0:T(8,128)(2,1)S(1)}, u32[]{:S(2)}, u32[]{:S(2)}) collective-permute-start(bf16[4,128,512]{2,1,0:T(8,128)(2,1)S(1)} %add_convert_fusion.1), channel_id=1, source_target_pairs={{0,8},{8,16},{16,24},{24,28},{28,20},{20,12},{12,4},{4,0},{1,9},{9... | collective-permute-start | bytes 1572872 | tf_op jit(solution)/shard_map/ppermute | solution.py:221
  238.1 16.1 %all-to-all-start.5 = ((bf16[4,128,512]{2,1,0:T(8,128)(2,1)}), bf16[4,128,512]{2,1,0:T(8,128)(2,1)S(1)}, u32[]{:S(2)}, u32[]{:S(2)}) async-start(bf16[4,128,512]{2,1,0:T(8,128)(2,1)} %add_convert_fusion), calls=%async_computation.5 | async-start | bytes 1048576 | tf_op jit(solution)/shard_map/all_to_all | solution.py:251
where the time goes:
time: 260 us; the launch traced here: 257 us
  starting transfers between devices  91.3 us (35%)
  waiting for transfers between devices  76 us (29%)
  local copies, waits for them, and re-layouts  37.9 us (15%)
  Pallas kernels  36.9 us (14%)
  other arithmetic  14.2 us (5%)
    pallas_call x1, Pallas kernels, attend(): pl.pallas_call(functools.partial(attend_kernel, heads=heads, last=(here -...  36.9 us
    ppermute x6, waiting for transfers between devices, ring_sum(): up, down = (lax.ppermute(up, 'ctx', back), lax.ppermute(down, 'ctx', forth))  32 us
    all_to_all x6, starting transfers between devices, swap(): return lax.all_to_all(x, 'head', split_axis=0, concat_axis=0, tiled=True)  24.9 us
    ppermute x3, waiting for transfers between devices, ring_gather(): down = lax.ppermute(down, 'ctx', back)  24.3 us
    ppermute x1, starting transfers between devices, ring_sum(): lax.ppermute(far[..., :half], 'ctx', back)  22.4 us
    ppermute x1, starting transfers between devices, ring_sum(): lax.ppermute(far[..., half:], 'ctx', forth)  20 us
    unnamed x21, local copies, waits for them, and re-layouts  19.3 us
    ppermute x6, starting transfers between devices, ring_sum(): up, down = (lax.ppermute(up, 'ctx', back), lax.ppermute(down, 'ctx', forth))  15.4 us
  transfers between devices with their start and end apart: 22, of which 15 were waited for; matrix products, arithmetic and copies ran while one was open for 16% of the time, Pallas kernels for 0%

commit v1 on v0

v1 whole, which is shorter than its diff:
```python
import functools
import math

import jax
import jax.numpy as jnp
from jax import lax
from jax.experimental import pallas as pl
from jax.experimental.pallas import tpu as pltpu
from jax.sharding import PartitionSpec as P

HD = 128
TILE = 128
LEVELS = 4
MOST = 8
WIDE = 4
NEG = -1e30
SCALE = 1.0 / math.sqrt(HD)
LOG2E = 1.4426950408889634
bf16 = jnp.bfloat16
f32 = jnp.float32


def visible_lists(segment_tiles, parent_list, first, here, tiles, slot_of):
    count = segment_tiles.shape[0]
    ends = jnp.cumsum(segment_tiles, dtype=jnp.int32)
    numbers = jnp.arange(count, dtype=jnp.int32)
    key_tiles = jnp.arange(tiles, dtype=jnp.int32)
    key_seg = jnp.sum((key_tiles[:, None] >= ends[None, :]).astype(jnp.int32), axis=1)
    mine = first + jnp.arange(here, dtype=jnp.int32)
    seg = jnp.sum((mine[:, None] >= ends[None, :]).astype(jnp.int32), axis=1)
    seen = jnp.zeros((here, tiles), jnp.bool_)
    for level in range(LEVELS):
        seen = seen | (seg[:, None] == key_seg[None, :])
        seg = jnp.sum(jnp.where(seg[:, None] == numbers[None, :], parent_list[None, :], 0), axis=1)
    seen = seen & (key_tiles[None, :] <= mine[:, None])
    rank = jnp.cumsum(seen.astype(jnp.int32), axis=1) - 1
    most = min(tiles, LEVELS * MOST)
    places = jnp.arange(most, dtype=jnp.int32)
    chosen = seen[:, :, None] & (rank[:, :, None] == places[None, None, :])
    slots = jnp.sum(jnp.where(chosen, slot_of[None, :, None], 0), axis=1)
    numbers = jnp.sum(jnp.where(chosen, key_tiles[None, :, None], 0), axis=1)
    return slots, numbers, jnp.sum(seen.astype(jnp.int32), axis=1)


def mm(a, b, ca=1, cb=0):
    return lax.dot_general(a, b, (((ca,), (cb,)), ((), ())), preferred_element_type=f32)


def attend_kernel(
    vis, into, cnt, qdo, k, v, odq, dkv, qt, dt, qn, dn, s_buf, p_buf, o_acc, q_acc, dka, dva, *, heads, last
):
    t = pl.program_id(0)
    part = pl.program_id(1)
    rows = heads * TILE

    @pl.when((t == 0) & (part == 0))
    def _():
        dka[...] = jnp.zeros_like(dka)
        dva[...] = jnp.zeros_like(dva)

    for h in range(heads):
        cols = slice(h * HD, (h + 1) * HD)
        qt[:, cols] = qdo[0, :, cols].T
        dt[:, cols] = qdo[0, :, rows + h * HD : rows + (h + 1) * HD].T
        qn[cols, :] = qdo[0, :, cols]
    n = cnt[t]
    full = (n - 1) // WIDE
    rest = n - full * WIDE

    def gathered(ref, b, wide):
        return jnp.concatenate([ref[vis[t, WIDE * b + w]] for w in range(wide)], axis=0)

    def over_blocks(step, start, first=None):
        carry = lax.fori_loop(0, full, lambda b, c: step(b, WIDE, False, c), start)
        return lax.cond(
            rest <= WIDE // 2,
            lambda c: step(full, WIDE // 2, True, c),
            lambda c: step(full, WIDE, True, c),
            carry,
        )

    def scores(b, wide, masked, m8):
        s = mm(gathered(k, b, wide), qt[...])
        if masked:
            key = lax.broadcasted_iota(jnp.int32, (wide * TILE, rows), 0)
            token = lax.broadcasted_iota(jnp.int32, (wide * TILE, rows), 1) % TILE
            s = jnp.where(key <= token + (rest - 1) * TILE, s, NEG)
        s_buf[b, : wide * TILE] = s
        return jnp.maximum(m8, jnp.max(s.reshape(wide * TILE // 8, 8, rows), axis=0))

    m8 = over_blocks(scores, jnp.full((8, rows), NEG, f32))
    m = jnp.max(m8, axis=0, keepdims=True)

    o_acc[...] = jnp.zeros_like(o_acc)

    def weigh(b, wide, masked, l8):
        p = jnp.exp2((s_buf[b, : wide * TILE] - m) * (SCALE * LOG2E))
        pb = p.astype(bf16)
        p_buf[b, : wide * TILE] = pb
        o_acc[...] += mm(gathered(v, b, wide), pb, 0, 0)
        return l8 + jnp.sum(p.reshape(wide * TILE // 8, 8, rows), axis=0)

    l8 = over_blocks(weigh, jnp.zeros((8, rows), f32))
    inv = 1.0 / jnp.sum(l8, axis=0, keepdims=True)
    ob = (o_acc[...] * inv).astype(bf16)
    db = (dt[...].astype(f32) * inv).astype(bf16)
    dt[...] = db
    rowdot = jnp.sum(db.astype(f32) * ob.astype(f32), axis=0, keepdims=True)
    for h in range(heads):
        cols = slice(h * HD, (h + 1) * HD)
        odq[0, :, cols] = ob[:, cols].T
        dn[cols, :] = db[:, cols].T

    q_acc[...] = jnp.zeros_like(q_acc)

    def back(b, wide, masked, carry):
        pb = p_buf[b, : wide * TILE]
        dp = mm(gathered(v, b, wide), dt[...])
        ds = (pb.astype(f32) * (dp - rowdot)).astype(bf16)
        dvn = mm(pb, dn[...])
        dkn = mm(ds, qn[...])
        q_acc[...] += mm(gathered(k, b, wide), ds, 0, 0)
        for w in range(wide):
            slot = into[t, WIDE * b + w]
            part_rows = slice(w * TILE, (w + 1) * TILE)
            dva[slot] += dvn[part_rows]
            dka[slot] += dkn[part_rows]
        return carry

    over_blocks(back, 0)
    qb = (q_acc[...] * SCALE).astype(bf16)
    for h in range(heads):
        odq[0, :, rows + h * HD : rows + (h + 1) * HD] = qb[:, h * HD : (h + 1) * HD].T

    @pl.when((t == last[0]) & (part == last[1]))
    def _():
        dkv[:, :, :HD] = (dka[...] * SCALE).astype(bf16)
        dkv[:, :, HD:] = dva[...].astype(bf16)


def parts_of(tiles):
    return 1 if tiles <= 64 else 2


def attend(vis, into, cnt, qdo, kv, number):
    here, _, width = qdo.shape
    tiles = kv.shape[0]
    most = vis.shape[1]
    parts = parts_of(tiles)
    rows = width // (2 * parts)
    rowspec = pl.BlockSpec((1, TILE, 2 * rows), lambda t, p, *_: (t, 0, p))
    keyspec = pl.BlockSpec((tiles, TILE, HD), lambda t, p, *_: (0, 0, 0), pipeline_mode=pl.Buffered(1))
    valspec = pl.BlockSpec((tiles, TILE, HD), lambda t, p, *_: (0, 0, 1), pipeline_mode=pl.Buffered(1))
    gradspec = pl.BlockSpec((tiles, TILE, 2 * HD), lambda t, p, *_: (0, 0, 0), pipeline_mode=pl.Buffered(1))
    return pl.pallas_call(
        functools.partial(attend_kernel, heads=rows // HD, last=(here - 1, parts - 1)),
        grid_spec=pltpu.PrefetchScalarGridSpec(
            num_scalar_prefetch=3,
            grid=(here, parts),
            in_specs=[rowspec, keyspec, valspec],
            out_specs=[rowspec, gradspec],
            scratch_shapes=[
                pltpu.VMEM((HD, rows), bf16),
                pltpu.VMEM((HD, rows), bf16),
                pltpu.VMEM((rows, HD), bf16),
                pltpu.VMEM((rows, HD), bf16),
                pltpu.VMEM((most // WIDE, WIDE * TILE, rows), f32),
                pltpu.VMEM((most // WIDE, WIDE * TILE, rows), bf16),
                pltpu.VMEM((HD, rows), f32),
                pltpu.VMEM((HD, rows), f32),
                pltpu.VMEM((tiles, TILE, HD), f32),
                pltpu.VMEM((tiles, TILE, HD), f32),
            ],
        ),
        out_shape=[
            jax.ShapeDtypeStruct((here, TILE, width), bf16),
            jax.ShapeDtypeStruct((tiles, TILE, 2 * HD), bf16),
        ],
        compiler_params=pltpu.CompilerParams(vmem_limit_bytes=63 << 20),
        cost_estimate=pl.CostEstimate(flops=40_000_000_000, bytes_accessed=20_000_000, transcendentals=20_000_000),
        name=f"attend{number}",
    )(vis, into, cnt, qdo, kv, kv)


def snake(z_size, y_size):
    order = [z * y_size for z in range(z_size)]
    for z in reversed(range(z_size)):
        across = range(1, y_size)
        order += [z * y_size + y for y in (across if (z_size - 1 - z) % 2 == 0 else reversed(across))]
    return order


def ring_gather(block, forth, back, size):
    up = down = block
    got = [block]
    for step in range(size // 2 - 1):
        up = lax.ppermute(up, "ctx", forth)
        down = lax.ppermute(down, "ctx", back)
        got += [up, down]
    half = block.shape[-1] // 2
    up = lax.ppermute(up[..., :half], "ctx", forth)
    down = lax.ppermute(down[..., half:], "ctx", back)
    return got + [jnp.concatenate([up, down], axis=-1)]


def ring_sum(parts, forth, back, size):
    half = parts[0].shape[-1] // 2
    far = parts[size - 1]
    up, down = lax.ppermute(far[..., :half], "ctx", back), lax.ppermute(far[..., half:], "ctx", forth)

    def add(a, b):
        return (a.astype(f32) + b.astype(f32)).astype(bf16)

    for step in reversed(range(size // 2 - 1)):
        mine_up, mine_down = parts[1 + 2 * step], parts[2 + 2 * step]
        if step == size // 2 - 2:
            up = jnp.concatenate([add(mine_up[..., :half], up), mine_up[..., half:]], axis=-1)
            down = jnp.concatenate([mine_down[..., :half], add(mine_down[..., half:], down)], axis=-1)
        else:
            up, down = add(mine_up, up), add(mine_down, down)
        up, down = lax.ppermute(up, "ctx", back), lax.ppermute(down, "ctx", forth)
    return (parts[0].astype(f32) + up.astype(f32) + down.astype(f32)).astype(bf16)


def local(queries, keys, values, out_grad, segment_tiles, parent_list):
    rows_here, key_width = keys.shape
    ctx, heads_axis = lax.axis_size("ctx"), lax.axis_size("head")
    groups = key_width // HD // heads_axis
    heads = queries.shape[1] // key_width
    tiles = ctx * heads_axis * rows_here // TILE
    here = tiles // ctx

    y_size = heads_axis // 2
    order = snake(ctx // y_size, y_size)
    forth = [(order[i], order[(i + 1) % ctx]) for i in range(ctx)]
    back = [(b, a) for a, b in forth]
    place = [order.index(c) for c in range(ctx)]
    piece_of = [0] * ctx
    for d in range(1, ctx):
        piece_of[d] = 2 * d - 1 if d <= ctx // 2 else 2 * (ctx - d)
    me = lax.axis_index("ctx")
    places = jnp.asarray(place, jnp.int32)
    my_place = jnp.sum(jnp.where(jnp.arange(ctx) == me, places, 0))
    distance = jnp.repeat(jnp.mod(my_place - places, ctx), here)
    table = jnp.asarray(piece_of, jnp.int32)
    piece = jnp.sum(jnp.where(distance[:, None] == jnp.arange(ctx)[None, :], table[None, :], 0), axis=1)
    slot_of = piece * here + jnp.arange(tiles, dtype=jnp.int32) % here
    slots, numbers, cnt = visible_lists(segment_tiles, parent_list, me * here, here, tiles, slot_of)

    def swap(x):
        return lax.all_to_all(x, "head", split_axis=0, concat_axis=0, tiled=True)

    def columns(x, number, width):
        return x[:, number * width : (number + 1) * width]

    parts = parts_of(tiles)
    width = heads * HD // parts

    def pair_of_rows(g):
        return jnp.stack(
            [
                jnp.concatenate(
                    [columns(x, (h * groups + g) * parts + p, width) for p in range(parts) for x in (queries, out_grad)],
                    axis=1,
                )
                for h in range(heads_axis)
            ]
        )

    def joined(pieces, which):
        w = pieces[0].shape[2] // (2 * parts)
        return jnp.concatenate(
            [
                columns(pieces[g][h], 2 * p + which, w)
                for h in range(heads_axis)
                for g in range(groups)
                for p in range(parts)
            ],
            axis=1,
        )

    kv = jnp.stack(
        [
            jnp.concatenate([columns(x, h * groups + g, HD) for g in range(groups) for x in (keys, values)], axis=1)
            for h in range(heads_axis)
        ]
    )
    qdo = [pair_of_rows(g) for g in range(groups)]
    kv = swap(kv).reshape(here, TILE, groups * 2 * HD)
    crossed = []
    for g in range(groups):
        qdo[g], before = lax.optimization_barrier((qdo[g], crossed[g - 1] if g else kv))
        if g:
            crossed[g - 1] = before
        else:
            kv = before
        crossed.append(swap(qdo[g]).reshape(here, TILE, -1))

    odq, dkv = [], []
    for g in range(groups):
        mine = kv[:, :, g * 2 * HD : (g + 1) * 2 * HD]
        if g == 0:
            ring = ring_gather(mine, forth, back, ctx)
            around, vis = jnp.concatenate(ring, axis=0), slots
        else:
            mine, ring[-1] = lax.optimization_barrier((mine, ring[-1]))
            around, vis = lax.all_gather(mine, "ctx", axis=0, tiled=True), numbers
        into = slots if g == groups - 1 else numbers
        odq_g, dkv_g = attend(vis, into, cnt, crossed[g], around, g)
        if g == groups - 1:
            if g:
                dkv_g, dkv[0] = lax.optimization_barrier((dkv_g, dkv[0]))
            dkv_g = ring_sum([dkv_g[i * here : (i + 1) * here] for i in range(ctx)], forth, back, ctx)
        else:
            dkv_g = lax.psum_scatter(dkv_g, "ctx", scatter_dimension=0, tiled=True)
        odq.append(swap(odq_g.reshape(heads_axis, rows_here, -1)))
        dkv.append(dkv_g)
    dkv = swap(jnp.concatenate(dkv, axis=-1).reshape(heads_axis, rows_here, -1))
    dk, dv = [
        jnp.concatenate(
            [columns(dkv[h], 2 * g + which, HD) for h in range(heads_axis) for g in range(groups)], axis=1
        )
        for which in range(2)
    ]
    return joined(odq, 0), joined(odq, 1), dk, dv


def solution(mesh):
    rows = P(("ctx", "head"), None)
    return jax.shard_map(
        local,
        mesh=mesh,
        in_specs=(rows, rows, rows, rows, P(), P()),
        out_specs=(rows, rows, rows, rows),
        check_vma=False,
    )
```

time: 260 us -> 246 us (0.946)
  starting transfers between devices: 91.3 us -> 42.1 us
  waiting for transfers between devices: 76 us -> 118 us
  between operations: 0.88 us -> 14.4 us
  local copies, waits for them, and re-layouts: 37.9 us -> 26.5 us
  Pallas kernels: 36.9 us -> 28.1 us
    reduce_scatter x0 -> x1, waiting for transfers between devices: none -> 58.7 us  [local(): dkv_g = lax.psum_scatter(dkv_g, 'ctx', scatter_dimension=0, tiled=True)]
    ppermute x3, waiting for transfers between devices: 24.3 us -> 0.72 us  [ring_gather(): down = lax.ppermute(down, 'ctx', back)]
    ppermute x1, starting transfers between devices: 22.4 us -> 1.29 us  [ring_sum(): lax.ppermute(far[..., :half], 'ctx', back)]
    ppermute x6, waiting for transfers between devices: 32 us -> 12.7 us  [ring_sum(): up, down = (lax.ppermute(up, 'ctx', back), lax.ppermute(down, 'ctx', forth))]
    ppermute x1, starting transfers between devices: 20 us -> 0.79 us  [ring_sum(): lax.ppermute(far[..., half:], 'ctx', forth)]
    all_to_all x6, waiting for transfers between devices: 11.4 us -> 25.8 us  [swap(): return lax.all_to_all(x, 'head', split_axis=0, concat_axis=0, tiled=True)]
    ppermute x3, waiting for transfers between devices: 0.01 us -> 12.7 us  [ring_gather(): up = lax.ppermute(up, 'ctx', forth)]
    ppermute x6, starting transfers between devices: 15.4 us -> 6.29 us  [ring_sum(): up, down = (lax.ppermute(up, 'ctx', back), lax.ppermute(down, 'ctx', forth))]
  transfers between devices with their start and end apart: 22 -> 24, of which waited for: 15 -> 15; matrix products, arithmetic and copies ran while one was open for 16% -> 14% of each run, Pallas kernels for 0% -> 11%
where the time goes in v1:
time: 246 us
  waiting for transfers between devices  118 us (48%)
  starting transfers between devices  42.1 us (17%)
  Pallas kernels  28.1 us (11%)
  local copies, waits for them, and re-layouts  26.5 us (11%)
  other arithmetic  16.5 us (7%)
  between operations  14.4 us (6%)
    reduce_scatter x1, waiting for transfers between devices, local(): dkv_g = lax.psum_scatter(dkv_g, 'ctx', scatter_dimension=0, tiled=True)  58.7 us
    pallas_call x2, Pallas kernels, attend(): pl.pallas_call(functools.partial(attend_kernel, heads=rows // HD, last=(h...  28.1 us
    all_to_all x6, waiting for transfers between devices, swap(): return lax.all_to_all(x, 'head', split_axis=0, concat_axis=0, tiled=True)  25.8 us
    all_to_all x6, starting transfers between devices, swap(): return lax.all_to_all(x, 'head', split_axis=0, concat_axis=0, tiled=True)  24 us
    unnamed x71, local copies, waits for them, and re-layouts  15 us
    ppermute x3, waiting for transfers between devices, ring_gather(): up = lax.ppermute(up, 'ctx', forth)  12.7 us
    ppermute x6, waiting for transfers between devices, ring_sum(): up, down = (lax.ppermute(up, 'ctx', back), lax.ppermute(down, 'ctx', forth))  12.7 us
    another operation x6, other arithmetic, pair_of_rows(): jnp.stack([jnp.concatenate([columns(x, (h * groups + g) * parts + p, widt...  6.62 us
  transfers between devices with their start and end apart: 24, of which 15 were waited for; matrix products, arithmetic and copies ran while one was open for 14% of the time, Pallas kernels for 11%

profile of v1, /device:TPU:0, one launch (start us, length us, event | category | flops | bytes accessed | tf_op | source)
XLA Modules:
  0.0 245.6 jit_solution(9591523813307059986)
XLA Ops:
  10.1 4.2 %all-to-all-start = ((bf16[4,128,512]{2,1,0:T(8,128)(2,1)}), bf16[4,128,512]{2,1,0:T(8,128)(2,1)S(1)}, u32[]{:S(2)}, u32[]{:S(2)}) async-start(bf16[4,128,512]{2,1,0:T(8,128)(2,1)} %pad_maximum_fusion.2), calls=%async_computation | async-start | bytes 1048576 | tf_op jit(solution)/shard_map/all_to_all | solution.py:251
  24.1 1.6 pad_maximum_fusion.1
  25.7 3.6 %all-to-all-start.1 = ((bf16[4,128,2048]{2,1,0:T(8,128)(2,1)}), bf16[4,128,2048]{2,1,0:T(8,128)(2,1)S(1)}, u32[]{:S(2)}, u32[]{:S(2)}) async-start(bf16[4,128,2048]{2,1,0:T(8,128)(2,1)} %pad_maximum_fusion.1), calls=%async_computation.1 | async-start | bytes 4194304 | tf_op jit(solution)/shard_map/all_to_all | solution.py:251
  30.2 2.3 collective-permute-start
  32.6 3.0 %pad_maximum_fusion = bf16[4,128,2048]{2,1,0:T(8,128)(2,1)} fusion(bf16[1,128,2048]{2,1,0:T(8,128)(2,1)} %get-tuple-element.120, bf16[1,128,2048]{2,1,0:T(8,128)(2,1)} %get-tuple-element.119, bf16[1,128,2048]{2,1,0:T(8,128)(2,1)} %get-tuple-element.118, bf16[1,128,2048]{2,1,0:T(8,128)(2,1)S(1)} %get-tuple-element.117), kind=kLoop, calls=%fused_computation | loop fusion | flops 3145728 | bytes 4194304 | tf_op jit(solution)/shard_map/stack | solution.py:260
  35.5 3.9 %collective-permute-done = bf16[4,128,256]{2,1,0:T(8,128)(2,1)S(1)} collective-permute-done((bf16[4,128,256]{2,1,0:T(8,128)(2,1)S(1)}, bf16[4,128,256]{2,1,0:T(8,128)(2,1)S(1)}, u32[]{:S(2)}, u32[]{:S(2)}) %collective-permute-start) | collective-permute-done | bytes 262176 | tf_op jit(solution)/shard_map/ppermute | solution.py:197
  39.4 1.8 collective-permute-start.2
  42.9 4.6 %collective-permute-done.2 = bf16[4,128,256]{2,1,0:T(8,128)(2,1)S(1)} collective-permute-done((bf16[4,128,256]{2,1,0:T(8,128)(2,1)S(1)}, bf16[4,128,256]{2,1,0:T(8,128)(2,1)S(1)}, u32[]{:S(2)}, u32[]{:S(2)}) %collective-permute-start.2) | collective-permute-done | bytes 262176 | tf_op jit(solution)/shard_map/ppermute | solution.py:197
  47.5 1.6 collective-permute-start.4
  51.7 4.2 %collective-permute-done.4 = bf16[4,128,256]{2,1,0:T(8,128)(2,1)S(1)} collective-permute-done((bf16[4,128,256]{2,1,0:T(8,128)(2,1)S(1)}, bf16[4,128,256]{2,1,0:T(8,128)(2,1)S(1)}, u32[]{:S(2)}, u32[]{:S(2)}) %collective-permute-start.4) | collective-permute-done | bytes 262176 | tf_op jit(solution)/shard_map/ppermute | solution.py:197
  55.9 2.5 %collective-permute-start.6 = (bf16[4,128,128]{2,1,0:T(8,128)(2,1)S(1)}, bf16[4,128,128]{2,1,0:T(8,128)(2,1)S(1)}, u32[]{:S(2)}, u32[]{:S(2)}) collective-permute-start(bf16[4,128,128]{2,1,0:T(8,128)(2,1)S(1)} %slice.393), channel_id=1, source_target_pairs={{0,8},{8,16},{16,24},{24,28},{28,20},{20,12},{12,4},{4,0},{1,9},{9... | collective-permute-start | bytes 393224 | tf_op jit(solution)/shard_map/ppermute | solution.py:201
  61.5 1.7 collective-permute-done.6
  63.9 3.7 %collective-permute-done.7 = bf16[4,128,128]{2,1,0:T(8,128)(2,1)S(1)} collective-permute-done((bf16[4,128,128]{2,1,0:T(8,128)(2,1)S(1)}, bf16[4,128,128]{2,1,0:T(8,128)(2,1)S(1)}, u32[]{:S(2)}, u32[]{:S(2)}) %collective-permute-start.7) | collective-permute-done | bytes 131104 | tf_op jit(solution)/shard_map/ppermute | solution.py:202
  68.3 1.3 copy-done.3
  69.6 4.5 %all-to-all-start.3 = ((bf16[4,128,2048]{2,1,0:T(8,128)(2,1)}), bf16[4,128,2048]{2,1,0:T(8,128)(2,1)}, u32[]{:S(2)}, u32[]{:S(2)}) async-start(bf16[4,128,2048]{2,1,0:T(8,128)(2,1)} %pad_maximum_fusion), calls=%async_computation.3 | async-start | bytes 4194304 | tf_op jit(solution)/shard_map/all_to_all | solution.py:251
  74.1 14.1 %attend0.1 = (bf16[4,128,2048]{2,1,0:T(8,128)(2,1)}, bf16[32,128,256]{2,1,0:T(8,128)(2,1)}) custom-call(s32[4,32]{1,0:T(4,128)} %get-tuple-element.27.vis.into, s32[4,32]{1,0:T(4,128)} %get-tuple-element.26.into.vis, s32[4]{0:T(128)} %get-tuple-element.28.cnt, bf16[4,128,2048]{2,1,0:T(8,128)(2,1)} %copy-done.3, ...), custom_call_target="tpu_custom_call" | custom-call | flops 40000000000 | bytes 20000000 | tf_op jit(solution)/shard_map/attend0/pallas_call | solution.py:155
  88.2 11.6 %all-to-all-done.3.qdo = bf16[4,128,2048]{2,1,0:T(8,128)(2,1)} async-done(((bf16[4,128,2048]{2,1,0:T(8,128)(2,1)}), bf16[4,128,2048]{2,1,0:T(8,128)(2,1)}, u32[]{:S(2)}, u32[]{:S(2)}) %all-to-all-start.3) | async-done | bytes 2097184 | tf_op jit(solution)/shard_map/all_to_all | solution.py:251
  99.8 4.6 %all-to-all-start.2 = ((bf16[4,128,2048]{2,1,0:T(8,128)(2,1)}), bf16[4,128,2048]{2,1,0:T(8,128)(2,1)}, u32[]{:S(2)}, u32[]{:S(2)}) async-start(bf16[4,128,2048]{2,1,0:T(8,128)(2,1)} %get-tuple-element.18), calls=%async_computation.2 | async-start | bytes 4194304 | tf_op jit(solution)/shard_map/all_to_all | solution.py:251
  104.5 14.0 %attend1.1 = (bf16[4,128,2048]{2,1,0:T(8,128)(2,1)}, bf16[32,128,256]{2,1,0:T(8,128)(2,1)}) custom-call(s32[4,32]{1,0:T(4,128)} %get-tuple-element.26.into.vis, s32[4,32]{1,0:T(4,128)} %get-tuple-element.27.vis.into, s32[4]{0:T(128)} %get-tuple-element.28.cnt, bf16[4,128,2048]{2,1,0:T(8,128)(2,1)} %all-to-all-done.3.qdo, ...), custom_call_target="tpu_custom_call" | custom-call | flops 40000000000 | bytes 20000000 | tf_op jit(solution)/shard_map/attend1/pallas_call | solution.py:155
  118.5 58.7 %reduce-scatter.2.cloned.1.call-done = bf16[4,128,256]{2,1,0:T(8,128)(2,1)} async-done(((bf16[32,128,256]{2,1,0:T(8,128)(2,1)}), bf16[4,128,256]{2,1,0:T(8,128)(2,1)}) %reduce-scatter.2.cloned.1.call-update) | async-done | bytes 262160 | tf_op jit(solution)/shard_map/reduce_scatter | solution.py:315
  177.2 3.6 %all-to-all-start.4 = ((bf16[4,128,2048]{2,1,0:T(8,128)(2,1)}), bf16[4,128,2048]{2,1,0:T(8,128)(2,1)S(1)}, u32[]{:S(2)}, u32[]{:S(2)}) async-start(bf16[4,128,2048]{2,1,0:T(8,128)(2,1)} %get-tuple-element.21), calls=%async_computation.4 | async-start | bytes 4194304 | tf_op jit(solution)/shard_map/all_to_all | solution.py:251
  184.0 2.5 %slice_bitcast_fusion.1 = (bf16[128,2048]{1,0:T(8,128)(2,1)S(1)}, bf16[128,2048]{1,0:T(8,128)(2,1)S(1)}, bf16[128,2048]{1,0:T(8,128)(2,1)}, bf16[128,2048]{1,0:T(8,128)(2,1)S(1)}) fusion(bf16[4,128,2048]{2,1,0:T(8,128)(2,1)} %all-to-all-done.2), kind=kLoop, calls=%fused_computation.3 | loop fusion | bytes 4194304 | tf_op jit(solution)/shard_map/squeeze | solution.py:274
  186.5 1.4 collective-permute-done.12
  189.4 1.3 collective-permute-start.9
  193.0 4.0 %collective-permute-done.9 = bf16[4,128,256]{2,1,0:T(8,128)(2,1)S(1)} collective-permute-done((bf16[4,128,256]{2,1,0:T(8,128)(2,1)S(1)}, bf16[4,128,256]{2,1,0:T(8,128)(2,1)S(1)}, u32[]{:S(2)}, u32[]{:S(2)}) %collective-permute-start.9) | collective-permute-done | bytes 262176 | tf_op jit(solution)/shard_map/ppermute | solution.py:221
  198.1 1.3 collective-permute-start.10
  199.4 7.1 %all-to-all-done.4 = bf16[4,128,2048]{2,1,0:T(8,128)(2,1)S(1)} async-done(((bf16[4,128,2048]{2,1,0:T(8,128)(2,1)}), bf16[4,128,2048]{2,1,0:T(8,128)(2,1)S(1)}, u32[]{:S(2)}, u32[]{:S(2)}) %all-to-all-start.4) | async-done | bytes 2097184 | tf_op jit(solution)/shard_map/all_to_all | solution.py:251
  211.9 1.3 collective-permute-start.11
  213.2 4.2 %collective-permute-done.14 = bf16[4,128,256]{2,1,0:T(8,128)(2,1)S(1)} collective-permute-done((bf16[4,128,256]{2,1,0:T(8,128)(2,1)S(1)}, bf16[4,128,256]{2,1,0:T(8,128)(2,1)S(1)}, u32[]{:S(2)}, u32[]{:S(2)}) %collective-permute-start.14) | collective-permute-done | bytes 262176 | tf_op jit(solution)/shard_map/ppermute | solution.py:221
  219.9 4.6 %collective-permute-done.15 = bf16[4,128,256]{2,1,0:T(8,128)(2,1)S(1)} collective-permute-done((bf16[4,128,256]{2,1,0:T(8,128)(2,1)S(1)}, bf16[4,128,256]{2,1,0:T(8,128)(2,1)S(1)}, u32[]{:S(2)}, u32[]{:S(2)}) %collective-permute-start.15) | collective-permute-done | bytes 262176 | tf_op jit(solution)/shard_map/ppermute | solution.py:221
  225.4 3.5 %all-to-all-start.5 = ((bf16[4,128,512]{2,1,0:T(8,128)(2,1)}), bf16[4,128,512]{2,1,0:T(8,128)(2,1)S(1)}, u32[]{:S(2)}, u32[]{:S(2)}) async-start(bf16[4,128,512]{2,1,0:T(8,128)(2,1)} %pad_maximum_fusion.3), calls=%async_computation.6 | async-start | bytes 1048576 | tf_op jit(solution)/shard_map/all_to_all | solution.py:251
  230.6 7.2 %all-to-all-done.5 = bf16[4,128,512]{2,1,0:T(8,128)(2,1)S(1)} async-done(((bf16[4,128,512]{2,1,0:T(8,128)(2,1)}), bf16[4,128,512]{2,1,0:T(8,128)(2,1)S(1)}, u32[]{:S(2)}, u32[]{:S(2)}) %all-to-all-start.5) | async-done | bytes 524320 | tf_op jit(solution)/shard_map/all_to_all | solution.py:251
  (140 shorter events, 41.9 us)
Async XLA Ops:
  7.2 7.1 %copy-start.1 = (bf16[128,8192]{1,0:T(8,128)(2,1)S(1)}, bf16[128,8192]{1,0:T(8,128)(2,1)}, u32[]{:S(2)}) copy-start(bf16[128,8192]{1,0:T(8,128)(2,1)} %param.8) | copy-start | bytes 6291460
  10.1 15.7 %all-to-all-start = ((bf16[4,128,512]{2,1,0:T(8,128)(2,1)}), bf16[4,128,512]{2,1,0:T(8,128)(2,1)S(1)}, u32[]{:S(2)}, u32[]{:S(2)}) async-start(bf16[4,128,512]{2,1,0:T(8,128)(2,1)} %pad_maximum_fusion.2), calls=%async_computation | async-start | bytes 1048576 | tf_op jit(solution)/shard_map/all_to_all | solution.py:251
  16.4 3.1 %copy-start.24 = (s32[8]{0:T(128)S(1)}, s32[8]{0:T(128)}, u32[]{:S(2)}) copy-start(s32[8]{0:T(128)} %constant.51.clone) | copy-start | bytes 100
  16.4 3.7 %copy-start.13 = (bf16[128,1024]{1,0:T(8,128)(2,1)S(1)}, bf16[128,1024]{1,0:T(8,128)(2,1)}, u32[]{:S(2)}) copy-start(bf16[128,1024]{1,0:T(8,128)(2,1)} %get-tuple-element.46) | copy-start | bytes 786436
  16.4 3.7 %copy-start.14 = (bf16[128,1024]{1,0:T(8,128)(2,1)S(1)}, bf16[128,1024]{1,0:T(8,128)(2,1)}, u32[]{:S(2)}) copy-start(bf16[128,1024]{1,0:T(8,128)(2,1)} %get-tuple-element.47) | copy-start | bytes 786436
  21.3 2.7 %copy-start.22 = (s32[8]{0:T(128)S(1)}, s32[8]{0:T(128)}, u32[]{:S(2)}) copy-start(s32[8]{0:T(128)} %constant.52.clone) | copy-start | bytes 100
  25.7 42.5 %all-to-all-start.1 = ((bf16[4,128,2048]{2,1,0:T(8,128)(2,1)}), bf16[4,128,2048]{2,1,0:T(8,128)(2,1)S(1)}, u32[]{:S(2)}, u32[]{:S(2)}) async-start(bf16[4,128,2048]{2,1,0:T(8,128)(2,1)} %pad_maximum_fusion.1), calls=%async_computation.1 | async-start | bytes 4194304 | tf_op jit(solution)/shard_map/all_to_all | solution.py:251
  29.3 75.1 %all-gather.2.cloned.1.call-start = ((), (), s32[]{:S(2)}) async-start(), calls=%async_computation.7 | async-start | bytes 2359296 | tf_op jit(solution)/shard_map/all_gather | solution.py:307
  30.2 9.2 %collective-permute-start = (bf16[4,128,256]{2,1,0:T(8,128)(2,1)S(1)}, bf16[4,128,256]{2,1,0:T(8,128)(2,1)S(1)}, u32[]{:S(2)}, u32[]{:S(2)}) collective-permute-start(bf16[4,128,256]{2,1,0:T(8,128)(2,1)S(1)} %get-tuple-element.84), channel_id=1, source_target_pairs={{0,8},{8,16},{16,24},{24,28},{28,20},{20,12},{12,4},{4,0},{1,9},{9... | collective-permute-start | bytes 786440 | tf_op jit(solution)/shard_map/ppermute | solution.py:197
  32.6 8.7 %collective-permute-start.1 = (bf16[4,128,256]{2,1,0:T(8,128)(2,1)S(1)}, bf16[4,128,256]{2,1,0:T(8,128)(2,1)S(1)}, u32[]{:S(2)}, u32[]{:S(2)}) collective-permute-start(bf16[4,128,256]{2,1,0:T(8,128)(2,1)S(1)} %get-tuple-element.84), channel_id=1, source_target_pairs={{8,0},{16,8},{24,16},{28,24},{20,28},{12,20},{4,12},{0,4},{9,1},{1... | collective-permute-start | bytes 786440 | tf_op jit(solution)/shard_map/ppermute | solution.py:198
  39.4 8.1 %collective-permute-start.2 = (bf16[4,128,256]{2,1,0:T(8,128)(2,1)S(1)}, bf16[4,128,256]{2,1,0:T(8,128)(2,1)S(1)}, u32[]{:S(2)}, u32[]{:S(2)}) collective-permute-start(bf16[4,128,256]{2,1,0:T(8,128)(2,1)S(1)} %collective-permute-done), channel_id=1, source_target_pairs={{0,8},{8,16},{16,24},{24,28},{28,20},{20,12},{12,4},{4,0},{1,9},{9... | collective-permute-start | bytes 786440 | tf_op jit(solution)/shard_map/ppermute | solution.py:197
  41.2 7.9 %collective-permute-start.3 = (bf16[4,128,256]{2,1,0:T(8,128)(2,1)S(1)}, bf16[4,128,256]{2,1,0:T(8,128)(2,1)S(1)}, u32[]{:S(2)}, u32[]{:S(2)}) collective-permute-start(bf16[4,128,256]{2,1,0:T(8,128)(2,1)S(1)} %collective-permute-done.1), channel_id=1, source_target_pairs={{8,0},{16,8},{24,16},{28,24},{20,28},{12,20},{4,12},{0,4},{9,1},{1... | collective-permute-start | bytes 786440 | tf_op jit(solution)/shard_map/ppermute | solution.py:198
  47.5 8.4 %collective-permute-start.4 = (bf16[4,128,256]{2,1,0:T(8,128)(2,1)S(1)}, bf16[4,128,256]{2,1,0:T(8,128)(2,1)S(1)}, u32[]{:S(2)}, u32[]{:S(2)}) collective-permute-start(bf16[4,128,256]{2,1,0:T(8,128)(2,1)S(1)} %collective-permute-done.2), channel_id=1, source_target_pairs={{0,8},{8,16},{16,24},{24,28},{28,20},{20,12},{12,4},{4,0},{1,9},{9... | collective-permute-start | bytes 786440 | tf_op jit(solution)/shard_map/ppermute | solution.py:197
  49.1 10.1 %collective-permute-start.5 = (bf16[4,128,256]{2,1,0:T(8,128)(2,1)S(1)}, bf16[4,128,256]{2,1,0:T(8,128)(2,1)S(1)}, u32[]{:S(2)}, u32[]{:S(2)}) collective-permute-start(bf16[4,128,256]{2,1,0:T(8,128)(2,1)S(1)} %collective-permute-done.3), channel_id=1, source_target_pairs={{8,0},{16,8},{24,16},{28,24},{20,28},{12,20},{4,12},{0,4},{9,1},{1... | collective-permute-start | bytes 786440 | tf_op jit(solution)/shard_map/ppermute | solution.py:198
  55.9 7.3 %collective-permute-start.6 = (bf16[4,128,128]{2,1,0:T(8,128)(2,1)S(1)}, bf16[4,128,128]{2,1,0:T(8,128)(2,1)S(1)}, u32[]{:S(2)}, u32[]{:S(2)}) collective-permute-start(bf16[4,128,128]{2,1,0:T(8,128)(2,1)S(1)} %slice.393), channel_id=1, source_target_pairs={{0,8},{8,16},{16,24},{24,28},{28,20},{20,12},{12,4},{4,0},{1,9},{9... | collective-permute-start | bytes 393224 | tf_op jit(solution)/shard_map/ppermute | solution.py:201
  59.2 8.4 %collective-permute-start.7 = (bf16[4,128,128]{2,1,0:T(8,128)(2,1)S(1)}, bf16[4,128,128]{2,1,0:T(8,128)(2,1)S(1)}, u32[]{:S(2)}, u32[]{:S(2)}) collective-permute-start(bf16[4,128,128]{2,1,0:T(8,128)(2,1)S(1)} %slice.394), channel_id=1, source_target_pairs={{8,0},{16,8},{24,16},{28,24},{20,28},{12,20},{4,12},{0,4},{9,1},{1... | collective-permute-start | bytes 393224 | tf_op jit(solution)/shard_map/ppermute | solution.py:202
  69.6 30.2 %all-to-all-start.3 = ((bf16[4,128,2048]{2,1,0:T(8,128)(2,1)}), bf16[4,128,2048]{2,1,0:T(8,128)(2,1)}, u32[]{:S(2)}, u32[]{:S(2)}) async-start(bf16[4,128,2048]{2,1,0:T(8,128)(2,1)} %pad_maximum_fusion), calls=%async_computation.3 | async-start | bytes 4194304 | tf_op jit(solution)/shard_map/all_to_all | solution.py:251
  74.0 103.2 %reduce-scatter.2.cloned.1.call-start = ((), (), s32[]{:S(2)}) async-start(), calls=%async_computation.8 | async-start | bytes 2359296 | tf_op jit(solution)/shard_map/reduce_scatter | solution.py:315
  99.8 77.4 %all-to-all-start.2 = ((bf16[4,128,2048]{2,1,0:T(8,128)(2,1)}), bf16[4,128,2048]{2,1,0:T(8,128)(2,1)}, u32[]{:S(2)}, u32[]{:S(2)}) async-start(bf16[4,128,2048]{2,1,0:T(8,128)(2,1)} %get-tuple-element.18), calls=%async_computation.2 | async-start | bytes 4194304 | tf_op jit(solution)/shard_map/all_to_all | solution.py:251
  177.2 29.3 %all-to-all-start.4 = ((bf16[4,128,2048]{2,1,0:T(8,128)(2,1)}), bf16[4,128,2048]{2,1,0:T(8,128)(2,1)S(1)}, u32[]{:S(2)}, u32[]{:S(2)}) async-start(bf16[4,128,2048]{2,1,0:T(8,128)(2,1)} %get-tuple-element.21), calls=%async_computation.4 | async-start | bytes 4194304 | tf_op jit(solution)/shard_map/all_to_all | solution.py:251
  181.9 5.9 %collective-permute-start.12 = (bf16[4,128,128]{2,1,0:T(8,128)(2,1)S(1)}, bf16[4,128,128]{2,1,0:T(8,128)(2,1)S(1)}, u32[]{:S(2)}, u32[]{:S(2)}) collective-permute-start(bf16[4,128,128]{2,1,0:T(8,128)(2,1)S(1)} %get-tuple-element.35), channel_id=1, source_target_pairs={{0,8},{8,16},{16,24},{24,28},{28,20},{20,12},{12,4},{4,0},{1,9},{9... | collective-permute-start | bytes 393224 | tf_op jit(solution)/shard_map/ppermute | solution.py:209
  182.7 5.6 %collective-permute-start.8 = (bf16[4,128,128]{2,1,0:T(8,128)(2,1)S(1)}, bf16[4,128,128]{2,1,0:T(8,128)(2,1)S(1)}, u32[]{:S(2)}, u32[]{:S(2)}) collective-permute-start(bf16[4,128,128]{2,1,0:T(8,128)(2,1)S(1)} %get-tuple-element.34), channel_id=1, source_target_pairs={{8,0},{16,8},{24,16},{28,24},{20,28},{12,20},{4,12},{0,4},{9,1},{1... | collective-permute-start | bytes 393224 | tf_op jit(solution)/shard_map/ppermute | solution.py:209
  189.4 7.6 %collective-permute-start.9 = (bf16[4,128,256]{2,1,0:T(8,128)(2,1)S(1)}, bf16[4,128,256]{2,1,0:T(8,128)(2,1)S(1)}, u32[]{:S(2)}, u32[]{:S(2)}) collective-permute-start(bf16[4,128,256]{2,1,0:T(8,128)(2,1)S(1)} %pad_maximum_fusion.4), channel_id=1, source_target_pairs={{8,0},{16,8},{24,16},{28,24},{20,28},{12,20},{4,12},{0,4},{9,1},{1... | collective-permute-start | bytes 786440 | tf_op jit(solution)/shard_map/ppermute | solution.py:221
  192.3 16.0 %collective-permute-start.13 = (bf16[4,128,256]{2,1,0:T(8,128)(2,1)}, bf16[4,128,256]{2,1,0:T(8,128)(2,1)}, u32[]{:S(2)}, u32[]{:S(2)}) collective-permute-start(bf16[4,128,256]{2,1,0:T(8,128)(2,1)} %pad_maximum_fusion.5), channel_id=1, source_target_pairs={{0,8},{8,16},{16,24},{24,28},{28,20},{20,12},{12,4},{4,0},{1,9},{9... | collective-permute-start | bytes 786440 | tf_op jit(solution)/shard_map/ppermute | solution.py:221
  198.1 10.3 %collective-permute-start.10 = (bf16[4,128,256]{2,1,0:T(8,128)(2,1)S(1)}, bf16[4,128,256]{2,1,0:T(8,128)(2,1)}, u32[]{:S(2)}, u32[]{:S(2)}) collective-permute-start(bf16[4,128,256]{2,1,0:T(8,128)(2,1)S(1)} %add_convert_fusion.4), channel_id=1, source_target_pairs={{8,0},{16,8},{24,16},{28,24},{20,28},{12,20},{4,12},{0,4},{9,1},{1... | collective-permute-start | bytes 786440 | tf_op jit(solution)/shard_map/ppermute | solution.py:221
  207.5 2.8 %copy-start.5 = (bf16[128,2048]{1,0:T(8,128)(2,1)S(1)}, bf16[128,2048]{1,0:T(8,128)(2,1)}, u32[]{:S(2)}) copy-start(bf16[128,2048]{1,0:T(8,128)(2,1)} %get-tuple-element.44) | copy-start | bytes 1572868
  209.5 7.9 %collective-permute-start.14 = (bf16[4,128,256]{2,1,0:T(8,128)(2,1)S(1)}, bf16[4,128,256]{2,1,0:T(8,128)(2,1)S(1)}, u32[]{:S(2)}, u32[]{:S(2)}) collective-permute-start(bf16[4,128,256]{2,1,0:T(8,128)(2,1)S(1)} %get-tuple-element.31), channel_id=1, source_target_pairs={{0,8},{8,16},{16,24},{24,28},{28,20},{20,12},{12,4},{4,0},{1,9},{9... | collective-permute-start | bytes 786440 | tf_op jit(solution)/shard_map/ppermute | solution.py:221
  211.9 12.6 %copy-start.17 = (bf16[4,128,256]{2,1,0:T(8,128)(2,1)S(1)}, bf16[4,128,256]{2,1,0:T(8,128)(2,1)}, u32[]{:S(2)}) copy-start(bf16[4,128,256]{2,1,0:T(8,128)(2,1)} %reduce-scatter.2.cloned.1.call-done) | copy-start | bytes 786436
  211.9 8.0 %collective-permute-start.11 = (bf16[4,128,256]{2,1,0:T(8,128)(2,1)S(1)}, bf16[4,128,256]{2,1,0:T(8,128)(2,1)S(1)}, u32[]{:S(2)}, u32[]{:S(2)}) collective-permute-start(bf16[4,128,256]{2,1,0:T(8,128)(2,1)S(1)} %get-tuple-element.30), channel_id=1, source_target_pairs={{8,0},{16,8},{24,16},{28,24},{20,28},{12,20},{4,12},{0,4},{9,1},{1... | collective-permute-start | bytes 786440 | tf_op jit(solution)/shard_map/ppermute | solution.py:221
  217.5 7.0 %collective-permute-start.15 = (bf16[4,128,256]{2,1,0:T(8,128)(2,1)S(1)}, bf16[4,128,256]{2,1,0:T(8,128)(2,1)S(1)}, u32[]{:S(2)}, u32[]{:S(2)}) collective-permute-start(bf16[4,128,256]{2,1,0:T(8,128)(2,1)S(1)} %add_convert_fusion.1), channel_id=1, source_target_pairs={{0,8},{8,16},{16,24},{24,28},{28,20},{20,12},{12,4},{4,0},{1,9},{9... | collective-permute-start | bytes 786440 | tf_op jit(solution)/shard_map/ppermute | solution.py:221
  219.9 9.8 %copy-start.4 = (bf16[128,2048]{1,0:T(8,128)(2,1)S(1)}, bf16[128,2048]{1,0:T(8,128)(2,1)}, u32[]{:S(2)}) copy-start(bf16[128,2048]{1,0:T(8,128)(2,1)} %get-tuple-element.38) | copy-start | bytes 1572868
  225.4 12.3 %all-to-all-start.5 = ((bf16[4,128,512]{2,1,0:T(8,128)(2,1)}), bf16[4,128,512]{2,1,0:T(8,128)(2,1)S(1)}, u32[]{:S(2)}, u32[]{:S(2)}) async-start(bf16[4,128,512]{2,1,0:T(8,128)(2,1)} %pad_maximum_fusion.3), calls=%async_computation.6 | async-start | bytes 1048576 | tf_op jit(solution)/shard_map/all_to_all | solution.py:251
  (17 other events, 23.1 us)
Sparse Core Ops, SparseCore 0:
  42.3 52.9 all-gather.1
  98.9 78.2 reduce-scatter.1

commit v2 on v1

--- a/solution.py
+++ b/solution.py
@@ -12,7 +12,8 @@
 TILE = 128
 LEVELS = 4
 MOST = 8
-WIDE = 4
+WIDE = 8
+HALF = WIDE // 2
 NEG = -1e30
 SCALE = 1.0 / math.sqrt(HD)
 LOG2E = 1.4426950408889634
@@ -20,7 +21,7 @@
 f32 = jnp.float32
 
 
-def visible_lists(segment_tiles, parent_list, first, here, tiles, slot_of):
+def visible_lists(segment_tiles, parent_list, first, here, tiles):
     count = segment_tiles.shape[0]
     ends = jnp.cumsum(segment_tiles, dtype=jnp.int32)
     numbers = jnp.arange(count, dtype=jnp.int32)
@@ -37,9 +38,13 @@
     most = min(tiles, LEVELS * MOST)
     places = jnp.arange(most, dtype=jnp.int32)
     chosen = seen[:, :, None] & (rank[:, :, None] == places[None, None, :])
-    slots = jnp.sum(jnp.where(chosen, slot_of[None, :, None], 0), axis=1)
     numbers = jnp.sum(jnp.where(chosen, key_tiles[None, :, None], 0), axis=1)
-    return slots, numbers, jnp.sum(seen.astype(jnp.int32), axis=1)
+    return numbers, jnp.sum(seen.astype(jnp.int32), axis=1)
+
+
+def renamed(numbers, table):
+    places = jnp.arange(table.shape[0], dtype=jnp.int32)
+    return jnp.sum(jnp.where(numbers[:, :, None] == places, table, 0), axis=2)
 
 
 def mm(a, b, ca=1, cb=0):
@@ -64,28 +69,35 @@
         dt[:, cols] = qdo[0, :, rows + h * HD : rows + (h + 1) * HD].T
         qn[cols, :] = qdo[0, :, cols]
     n = cnt[t]
-    full = (n - 1) // WIDE
-    rest = n - full * WIDE
-
-    def gathered(ref, b, wide):
-        return jnp.concatenate([ref[vis[t, WIDE * b + w]] for w in range(wide)], axis=0)
-
-    def over_blocks(step, start, first=None):
-        carry = lax.fori_loop(0, full, lambda b, c: step(b, WIDE, False, c), start)
+    wides = (n - 1) // WIDE
+    halves = (n - 1) // HALF
+    rest = n - halves * HALF
+
+    def gathered(ref, at, wide):
+        return jnp.concatenate([ref[vis[t, at + w]] for w in range(wide)], axis=0)
+
+    def rows_of(at, wide):
+        return pl.ds(pl.multiple_of(at * TILE, TILE), wide * TILE)
+
+    def over_blocks(step, carry):
+        carry = lax.fori_loop(0, wides, lambda b, c: step(b * WIDE, WIDE, False, c), carry)
+        carry = lax.cond(
+            halves > 2 * wides, lambda c: step(wides * WIDE, HALF, False, c), lambda c: c, carry
+        )
         return lax.cond(
-            rest <= WIDE // 2,
-            lambda c: step(full, WIDE // 2, True, c),
-            lambda c: step(full, WIDE, True, c),
+            rest <= HALF // 2,
+            lambda c: step(halves * HALF, HALF // 2, True, c),
+            lambda c: step(halves * HALF, HALF, True, c),
             carry,
         )
 
-    def scores(b, wide, masked, m8):
-        s = mm(gathered(k, b, wide), qt[...])
+    def scores(at, wide, masked, m8):
+        s = mm(gathered(k, at, wide), qt[...])
         if masked:
             key = lax.broadcasted_iota(jnp.int32, (wide * TILE, rows), 0)
             token = lax.broadcasted_iota(jnp.int32, (wide * TILE, rows), 1) % TILE
             s = jnp.where(key <= token + (rest - 1) * TILE, s, NEG)
-        s_buf[b, : wide * TILE] = s
+        s_buf[rows_of(at, wide)] = s
         return jnp.maximum(m8, jnp.max(s.reshape(wide * TILE // 8, 8, rows), axis=0))
 
     m8 = over_blocks(scores, jnp.full((8, rows), NEG, f32))
@@ -93,19 +105,22 @@
 
     o_acc[...] = jnp.zeros_like(o_acc)
 
-    def weigh(b, wide, masked, l8):
-        p = jnp.exp2((s_buf[b, : wide * TILE] - m) * (SCALE * LOG2E))
+    def weigh(at, wide, masked, l8):
+        vb = gathered(v, at, wide)
+        p = jnp.exp2((s_buf[rows_of(at, wide)] - m) * (SCALE * LOG2E))
+        dp = mm(vb, dt[...])
         pb = p.astype(bf16)
-        p_buf[b, : wide * TILE] = pb
-        o_acc[...] += mm(gathered(v, b, wide), pb, 0, 0)
+        p_buf[rows_of(at, wide)] = pb
+        s_buf[rows_of(at, wide)] = dp
+        o_acc[...] += mm(vb, pb, 0, 0)
         return l8 + jnp.sum(p.reshape(wide * TILE // 8, 8, rows), axis=0)
 
     l8 = over_blocks(weigh, jnp.zeros((8, rows), f32))
     inv = 1.0 / jnp.sum(l8, axis=0, keepdims=True)
     ob = (o_acc[...] * inv).astype(bf16)
-    db = (dt[...].astype(f32) * inv).astype(bf16)
-    dt[...] = db
-    rowdot = jnp.sum(db.astype(f32) * ob.astype(f32), axis=0, keepdims=True)
+    grads = dt[...].astype(f32)
+    db = (grads * inv).astype(bf16)
+    rowdot = jnp.sum(grads * ob.astype(f32), axis=0, keepdims=True) * inv
     for h in range(heads):
         cols = slice(h * HD, (h + 1) * HD)
         odq[0, :, cols] = ob[:, cols].T
@@ -113,15 +128,15 @@
 
     q_acc[...] = jnp.zeros_like(q_acc)
 
-    def back(b, wide, masked, carry):
-        pb = p_buf[b, : wide * TILE]
-        dp = mm(gathered(v, b, wide), dt[...])
-        ds = (pb.astype(f32) * (dp - rowdot)).astype(bf16)
+    def back(at, wide, masked, carry):
+        pb = p_buf[rows_of(at, wide)]
+        dp = s_buf[rows_of(at, wide)]
+        ds = (pb.astype(f32) * (dp * inv - rowdot)).astype(bf16)
         dvn = mm(pb, dn[...])
         dkn = mm(ds, qn[...])
-        q_acc[...] += mm(gathered(k, b, wide), ds, 0, 0)
+        q_acc[...] += mm(gathered(k, at, wide), ds, 0, 0)
         for w in range(wide):
-            slot = into[t, WIDE * b + w]
+            slot = into[t, at + w]
             part_rows = slice(w * TILE, (w + 1) * TILE)
             dva[slot] += dvn[part_rows]
             dka[slot] += dkn[part_rows]
@@ -164,8 +179,8 @@
                 pltpu.VMEM((HD, rows), bf16),
                 pltpu.VMEM((rows, HD), bf16),
                 pltpu.VMEM((rows, HD), bf16),
-                pltpu.VMEM((most // WIDE, WIDE * TILE, rows), f32),
-                pltpu.VMEM((most // WIDE, WIDE * TILE, rows), bf16),
+                pltpu.VMEM((most * TILE, rows), f32),
+                pltpu.VMEM((most * TILE, rows), bf16),
                 pltpu.VMEM((HD, rows), f32),
                 pltpu.VMEM((HD, rows), f32),
                 pltpu.VMEM((tiles, TILE, HD), f32),
@@ -190,36 +205,57 @@
     return order
 
 
-def ring_gather(block, forth, back, size):
-    up = down = block
-    got = [block]
-    for step in range(size // 2 - 1):
-        up = lax.ppermute(up, "ctx", forth)
-        down = lax.ppermute(down, "ctx", back)
-        got += [up, down]
-    half = block.shape[-1] // 2
-    up = lax.ppermute(up[..., :half], "ctx", forth)
-    down = lax.ppermute(down[..., half:], "ctx", back)
-    return got + [jnp.concatenate([up, down], axis=-1)]
-
-
-def ring_sum(parts, forth, back, size):
-    half = parts[0].shape[-1] // 2
-    far = parts[size - 1]
-    up, down = lax.ppermute(far[..., :half], "ctx", back), lax.ppermute(far[..., half:], "ctx", forth)
-
-    def add(a, b):
-        return (a.astype(f32) + b.astype(f32)).astype(bf16)
-
-    for step in reversed(range(size // 2 - 1)):
-        mine_up, mine_down = parts[1 + 2 * step], parts[2 + 2 * step]
-        if step == size // 2 - 2:
-            up = jnp.concatenate([add(mine_up[..., :half], up), mine_up[..., half:]], axis=-1)
-            down = jnp.concatenate([mine_down[..., :half], add(mine_down[..., half:], down)], axis=-1)
-        else:
-            up, down = add(mine_up, up), add(mine_down, down)
-        up, down = lax.ppermute(up, "ctx", back), lax.ppermute(down, "ctx", forth)
-    return (parts[0].astype(f32) + up.astype(f32) + down.astype(f32)).astype(bf16)
+class Ring:
+    def __init__(self, ctx, size, y_size):
+        order = snake(size // y_size, y_size)
+        self.size = size
+        self.place = [order.index(c) for c in range(size)]
+        self.forth = [
+            (at + order[i], at + order[(i + 1) % size]) for at in range(0, ctx, size) for i in range(size)
+        ]
+        self.back = [(b, a) for a, b in self.forth]
+
+    def piece(self, me, owner):
+        places = jnp.asarray(self.place, jnp.int32)
+        numbers = jnp.arange(self.size, dtype=jnp.int32)
+
+        def place(c):
+            return jnp.sum(jnp.where((c % self.size)[..., None] == numbers, places, 0), axis=-1)
+
+        d = (place(jnp.asarray(me)) - place(owner)) % self.size
+        return jnp.where(d == 0, 0, jnp.where(d <= self.size // 2, 2 * d - 1, 2 * (self.size - d)))
+
+    def gather(self, block):
+        up = down = block
+        got = [block]
+        for step in range(self.size // 2 - 1):
+            up = lax.ppermute(up, "ctx", self.forth)
+            down = lax.ppermute(down, "ctx", self.back)
+            got += [up, down]
+        middle = block.shape[-1] // 2
+        up = lax.ppermute(up[..., :middle], "ctx", self.forth)
+        down = lax.ppermute(down[..., middle:], "ctx", self.back)
+        return got + [jnp.concatenate([up, down], axis=-1)]
+
+    def sum(self, parts):
+        middle = parts[0].shape[-1] // 2
+        far = parts[self.size - 1]
+        up = lax.ppermute(far[..., :middle], "ctx", self.back)
+        down = lax.ppermute(far[..., middle:], "ctx", self.forth)
+        for step in reversed(range(self.size // 2 - 1)):
+            mine_up, mine_down = parts[1 + 2 * step], parts[2 + 2 * step]
+            if step == self.size // 2 - 2:
+                up = jnp.concatenate([add(mine_up[..., :middle], up), mine_up[..., middle:]], axis=-1)
+                down = jnp.concatenate([mine_down[..., :middle], add(mine_down[..., middle:], down)], axis=-1)
+            else:
+                up, down = add(mine_up, up), add(mine_down, down)
+            up = lax.ppermute(up, "ctx", self.back)
+            down = lax.ppermute(down, "ctx", self.forth)
+        return add(parts[0], up, down)
+
+
+def add(*terms):
+    return sum(x.astype(f32) for x in terms).astype(bf16)
 
 
 def local(queries, keys, values, out_grad, segment_tiles, parent_list):
@@ -230,22 +266,19 @@
     tiles = ctx * heads_axis * rows_here // TILE
     here = tiles // ctx
 
+    me = lax.axis_index("ctx")
     y_size = heads_axis // 2
-    order = snake(ctx // y_size, y_size)
-    forth = [(order[i], order[(i + 1) % ctx]) for i in range(ctx)]
-    back = [(b, a) for a, b in forth]
-    place = [order.index(c) for c in range(ctx)]
-    piece_of = [0] * ctx
-    for d in range(1, ctx):
-        piece_of[d] = 2 * d - 1 if d <= ctx // 2 else 2 * (ctx - d)
-    me = lax.axis_index("ctx")
-    places = jnp.asarray(place, jnp.int32)
-    my_place = jnp.sum(jnp.where(jnp.arange(ctx) == me, places, 0))
-    distance = jnp.repeat(jnp.mod(my_place - places, ctx), here)
-    table = jnp.asarray(piece_of, jnp.int32)
-    piece = jnp.sum(jnp.where(distance[:, None] == jnp.arange(ctx)[None, :], table[None, :], 0), axis=1)
-    slot_of = piece * here + jnp.arange(tiles, dtype=jnp.int32) % here
-    slots, numbers, cnt = visible_lists(segment_tiles, parent_list, me * here, here, tiles, slot_of)
+    whole = Ring(ctx, ctx, y_size)
+    half = Ring(ctx, ctx // 2, y_size)
+    partner = [(c, (c + ctx // 2) % ctx) for c in range(ctx)]
+    block = jnp.arange(tiles, dtype=jnp.int32) // here
+    within = jnp.arange(tiles, dtype=jnp.int32) % here
+    slot_of = whole.piece(me, block) * here + within
+    other = block // (ctx // 2) != me // (ctx // 2)
+    seen_from = jnp.where(other, (me + ctx // 2) % ctx, me)
+    half_slot_of = (half.piece(seen_from, block) + jnp.where(other, ctx // 2, 0)) * here + within
+    numbers, cnt = visible_lists(segment_tiles, parent_list, me * here, here, tiles)
+    slots, half_slots = [renamed(numbers, table) for table in (slot_of, half_slot_of)]
 
     def swap(x):
         return lax.all_to_all(x, "head", split_axis=0, concat_axis=0, tiled=True)
@@ -289,32 +322,33 @@
     kv = swap(kv).reshape(here, TILE, groups * 2 * HD)
     crossed = []
     for g in range(groups):
-        qdo[g], before = lax.optimization_barrier((qdo[g], crossed[g - 1] if g else kv))
         if g:
-            crossed[g - 1] = before
-        else:
-            kv = before
+            qdo[g], crossed[g - 1] = lax.optimization_barrier((qdo[g], crossed[g - 1]))
         crossed.append(swap(qdo[g]).reshape(here, TILE, -1))
 
     odq, dkv = [], []
     for g in range(groups):
         mine = kv[:, :, g * 2 * HD : (g + 1) * 2 * HD]
         if g == 0:
-            ring = ring_gather(mine, forth, back, ctx)
+            ring = whole.gather(mine)
             around, vis = jnp.concatenate(ring, axis=0), slots
         else:
             mine, ring[-1] = lax.optimization_barrier((mine, ring[-1]))
             around, vis = lax.all_gather(mine, "ctx", axis=0, tiled=True), numbers
-        into = slots if g == groups - 1 else numbers
-        odq_g, dkv_g = attend(vis, into, cnt, crossed[g], around, g)
-        if g == groups - 1:
-            if g:
-                dkv_g, dkv[0] = lax.optimization_barrier((dkv_g, dkv[0]))
-            dkv_g = ring_sum([dkv_g[i * here : (i + 1) * here] for i in range(ctx)], forth, back, ctx)
+        last = g == groups - 1
+        odq_g, dkv_g = attend(vis, slots if last else half_slots, cnt, crossed[g], around, g)
+        if g:
+            far, odq[g - 1], odq_g, dkv_g = lax.optimization_barrier((far, odq[g - 1], odq_g, dkv_g))
+            dkv[g - 1] = half.sum(
+                [add(near[i * here : (i + 1) * here], far[i * here : (i + 1) * here]) for i in range(ctx // 2)]
+            )
+        if last:
+            dkv_g = whole.sum([dkv_g[i * here : (i + 1) * here] for i in range(ctx)])
         else:
-            dkv_g = lax.psum_scatter(dkv_g, "ctx", scatter_dimension=0, tiled=True)
+            near, far = dkv_g[: tiles // 2], lax.ppermute(dkv_g[tiles // 2 :], "ctx", partner)
         odq.append(swap(odq_g.reshape(heads_axis, rows_here, -1)))
         dkv.append(dkv_g)
+    dkv[-1], odq[-1] = lax.optimization_barrier((dkv[-1], odq[-1]))
     dkv = swap(jnp.concatenate(dkv, axis=-1).reshape(heads_axis, rows_here, -1))
     dk, dv = [
         jnp.concatenate(

time: 246 us -> 232 us (0.943); the launches traced: 246 us -> 236 us
  waiting for transfers between devices: 118 us -> 64.5 us
  starting transfers between devices: 42.1 us -> 83.1 us
    reduce_scatter x1 -> x0, waiting for transfers between devices: 58.7 us -> none  [local(): dkv_g = lax.psum_scatter(dkv_g, 'ctx', scatter_dimension=0, tiled=True)]
    ppermute x16 -> x21, starting transfers between devices: 18.1 us -> 58.9 us  [the longest x1 26.7 us: local(): lax.ppermute(dkv_g[tiles // 2:], 'ctx', partner)]
    ppermute x16 -> x21, waiting for transfers between devices: 33.4 us -> 61.4 us  [the longest x1 25.3 us: local(): lax.ppermute(dkv_g[tiles // 2:], 'ctx', partner)]
    all_to_all x6, waiting for transfers between devices: 25.8 us -> 3 us  [swap(): return lax.all_to_all(x, 'head', split_axis=0, concat_axis=0, tiled=True)]
    slice x3 -> x7, local copies, waits for them, and re-layouts: 1.18 us -> 3.71 us  [the longest x1 2.29 us: local(): dkv_g[tiles // 2:]]
    unnamed x71 -> x79, local copies, waits for them, and re-layouts: 15 us -> 14 us
  transfers between devices with their start and end apart: 24 -> 28, of which waited for: 15 -> 13; matrix products, arithmetic and copies ran while one was open for 14% -> 15% of each run, Pallas kernels for 11% -> 12%
where the time goes in v2:
time: 232 us; the launch traced here: 236 us
  starting transfers between devices  83.1 us (36%)
  waiting for transfers between devices  64.5 us (28%)
  local copies, waits for them, and re-layouts  28.6 us (12%)
  Pallas kernels  27.2 us (12%)
  other arithmetic  18 us (8%)
  between operations  14.6 us (6%)
    pallas_call x2, Pallas kernels, attend(): pl.pallas_call(functools.partial(attend_kernel, heads=rows // HD, last=(h...  27.2 us
    ppermute x1, starting transfers between devices, local(): lax.ppermute(dkv_g[tiles // 2:], 'ctx', partner)  26.7 us
    ppermute x1, waiting for transfers between devices, local(): lax.ppermute(dkv_g[tiles // 2:], 'ctx', partner)  25.3 us
    all_to_all x6, starting transfers between devices, swap(): return lax.all_to_all(x, 'head', split_axis=0, concat_axis=0, tiled=True)  24.2 us
    unnamed x79, local copies, waits for them, and re-layouts  14 us
    ppermute x4, waiting for transfers between devices, sum(): down = lax.ppermute(down, 'ctx', self.forth)  12.2 us
    ppermute x3, waiting for transfers between devices, gather(): down = lax.ppermute(down, 'ctx', self.back)  11.8 us
    ppermute x4, starting transfers between devices, sum(): up = lax.ppermute(up, 'ctx', self.back)  10.6 us
  transfers between devices with their start and end apart: 28, of which 13 were waited for; matrix products, arithmetic and copies ran while one was open for 15% of the time, Pallas kernels for 12%

profile of v2, /device:TPU:0, one launch (start us, length us, event | category | flops | bytes accessed | tf_op | source)
XLA Modules:
  0.0 235.9 jit_solution(8260760307998314963)
XLA Ops:
  10.1 4.2 %all-to-all-start.1 = ((bf16[4,128,512]{2,1,0:T(8,128)(2,1)}), bf16[4,128,512]{2,1,0:T(8,128)(2,1)S(1)}, u32[]{:S(2)}, u32[]{:S(2)}) async-start(bf16[4,128,512]{2,1,0:T(8,128)(2,1)} %pad_maximum_fusion.2), calls=%async_computation.1 | async-start | bytes 1048576 | tf_op jit(solution)/shard_map/all_to_all | solution.py:284
  26.2 3.6 %all-to-all-start = ((bf16[4,128,2048]{2,1,0:T(8,128)(2,1)}), bf16[4,128,2048]{2,1,0:T(8,128)(2,1)S(1)}, u32[]{:S(2)}, u32[]{:S(2)}) async-start(bf16[4,128,2048]{2,1,0:T(8,128)(2,1)} %pad_maximum_fusion.1), calls=%async_computation | async-start | bytes 4194304 | tf_op jit(solution)/shard_map/all_to_all | solution.py:284
  30.7 2.3 collective-permute-start.1
  33.0 2.9 %pad_maximum_fusion = bf16[4,128,2048]{2,1,0:T(8,128)(2,1)} fusion(bf16[1,128,2048]{2,1,0:T(8,128)(2,1)} %get-tuple-element.133, bf16[1,128,2048]{2,1,0:T(8,128)(2,1)S(1)} %get-tuple-element.132, bf16[1,128,2048]{2,1,0:T(8,128)(2,1)} %get-tuple-element.131, bf16[1,128,2048]{2,1,0:T(8,128)(2,1)} %get-tuple-element.130), kind=kLoop, calls=%fused_computation | loop fusion | flops 3145728 | bytes 4194304 | tf_op jit(solution)/shard_map/stack | solution.py:293
  36.0 4.0 %collective-permute-done.1 = bf16[4,128,256]{2,1,0:T(8,128)(2,1)S(1)} collective-permute-done((bf16[4,128,256]{2,1,0:T(8,128)(2,1)S(1)}, bf16[4,128,256]{2,1,0:T(8,128)(2,1)S(1)}, u32[]{:S(2)}, u32[]{:S(2)}) %collective-permute-start.1) | collective-permute-done | bytes 262176 | tf_op jit(solution)/shard_map/ppermute | solution.py:233
  43.7 4.3 %collective-permute-done.3 = bf16[4,128,256]{2,1,0:T(8,128)(2,1)S(1)} collective-permute-done((bf16[4,128,256]{2,1,0:T(8,128)(2,1)S(1)}, bf16[4,128,256]{2,1,0:T(8,128)(2,1)S(1)}, u32[]{:S(2)}, u32[]{:S(2)}) %collective-permute-start.3) | collective-permute-done | bytes 262176 | tf_op jit(solution)/shard_map/ppermute | solution.py:233
  52.2 3.5 %collective-permute-done.5 = bf16[4,128,256]{2,1,0:T(8,128)(2,1)S(1)} collective-permute-done((bf16[4,128,256]{2,1,0:T(8,128)(2,1)S(1)}, bf16[4,128,256]{2,1,0:T(8,128)(2,1)S(1)}, u32[]{:S(2)}, u32[]{:S(2)}) %collective-permute-start.5) | collective-permute-done | bytes 262176 | tf_op jit(solution)/shard_map/ppermute | solution.py:233
  55.8 2.5 %collective-permute-start.7 = (bf16[4,128,128]{2,1,0:T(8,128)(2,1)S(1)}, bf16[4,128,128]{2,1,0:T(8,128)(2,1)S(1)}, u32[]{:S(2)}, u32[]{:S(2)}) collective-permute-start(bf16[4,128,128]{2,1,0:T(8,128)(2,1)S(1)} %slice.460), channel_id=1, source_target_pairs={{8,0},{16,8},{24,16},{28,24},{20,28},{12,20},{4,12},{0,4},{9,1},{1... | collective-permute-start | bytes 393224 | tf_op jit(solution)/shard_map/ppermute | solution.py:237
  60.9 3.5 %collective-permute-done.6 = bf16[4,128,128]{2,1,0:T(8,128)(2,1)S(1)} collective-permute-done((bf16[4,128,128]{2,1,0:T(8,128)(2,1)S(1)}, bf16[4,128,128]{2,1,0:T(8,128)(2,1)S(1)}, u32[]{:S(2)}, u32[]{:S(2)}) %collective-permute-start.6) | collective-permute-done | bytes 131104 | tf_op jit(solution)/shard_map/ppermute | solution.py:236
  67.1 4.6 %all-to-all-start.3 = ((bf16[4,128,2048]{2,1,0:T(8,128)(2,1)}), bf16[4,128,2048]{2,1,0:T(8,128)(2,1)}, u32[]{:S(2)}, u32[]{:S(2)}) async-start(bf16[4,128,2048]{2,1,0:T(8,128)(2,1)} %pad_maximum_fusion), calls=%async_computation.3 | async-start | bytes 4194304 | tf_op jit(solution)/shard_map/all_to_all | solution.py:284
  71.7 13.7 %attend0.1 = (bf16[4,128,2048]{2,1,0:T(8,128)(2,1)}, bf16[32,128,256]{2,1,0:T(8,128)(2,1)}) custom-call(s32[4,32]{1,0:T(4,128)} %get-tuple-element.31.vis.into, s32[4,32]{1,0:T(4,128)} %get-tuple-element.30.into, s32[4]{0:T(128)} %get-tuple-element.34.cnt, bf16[4,128,2048]{2,1,0:T(8,128)(2,1)} %copy-done.3, ...), custom_call_target="tpu_custom_call" | custom-call | flops 40000000000 | bytes 20000000 | tf_op jit(solution)/shard_map/attend0/pallas_call | solution.py:170
  85.4 2.3 slice.387
  87.7 26.7 %collective-permute-start.8 = (bf16[16,128,256]{2,1,0:T(8,128)(2,1)}, bf16[16,128,256]{2,1,0:T(8,128)(2,1)}, u32[]{:S(2)}, u32[]{:S(2)}) collective-permute-start(bf16[16,128,256]{2,1,0:T(8,128)(2,1)} %slice.387), channel_id=1, source_target_pairs={{0,16},{4,20},{8,24},{12,28},{16,0},{20,4},{24,8},{28,12},{1,17},{... | collective-permute-start | bytes 3145736 | tf_op jit(solution)/shard_map/ppermute | solution.py:348
  114.5 4.7 %all-to-all-start.2 = ((bf16[4,128,2048]{2,1,0:T(8,128)(2,1)}), bf16[4,128,2048]{2,1,0:T(8,128)(2,1)}, u32[]{:S(2)}, u32[]{:S(2)}) async-start(bf16[4,128,2048]{2,1,0:T(8,128)(2,1)} %get-tuple-element.19), calls=%async_computation.2 | async-start | bytes 4194304 | tf_op jit(solution)/shard_map/all_to_all | solution.py:284
  119.2 13.5 %attend1.1 = (bf16[4,128,2048]{2,1,0:T(8,128)(2,1)}, bf16[32,128,256]{2,1,0:T(8,128)(2,1)}) custom-call(s32[4,32]{1,0:T(4,128)} %copy-done.22, s32[4,32]{1,0:T(4,128)} %get-tuple-element.31.vis.into, s32[4]{0:T(128)} %get-tuple-element.34.cnt, bf16[4,128,2048]{2,1,0:T(8,128)(2,1)} %all-to-all-done.3.qdo, ...), custom_call_target="tpu_custom_call" | custom-call | flops 40000000000 | bytes 20000000 | tf_op jit(solution)/shard_map/attend1/pallas_call | solution.py:170
  132.6 25.3 %collective-permute-done.8 = bf16[16,128,256]{2,1,0:T(8,128)(2,1)} collective-permute-done((bf16[16,128,256]{2,1,0:T(8,128)(2,1)}, bf16[16,128,256]{2,1,0:T(8,128)(2,1)}, u32[]{:S(2)}, u32[]{:S(2)}) %collective-permute-start.8) | collective-permute-done | bytes 1048608 | tf_op jit(solution)/shard_map/ppermute | solution.py:348
  158.0 2.7 %slice_bitcast_fusion.1 = (bf16[128,2048]{1,0:T(8,128)(2,1)S(1)}, bf16[128,2048]{1,0:T(8,128)(2,1)S(1)}, bf16[128,2048]{1,0:T(8,128)(2,1)}, bf16[128,2048]{1,0:T(8,128)(2,1)}) fusion(bf16[4,128,2048]{2,1,0:T(8,128)(2,1)} %all-to-all-done.2), kind=kLoop, calls=%fused_computation.18 | loop fusion | bytes 4194304 | tf_op jit(solution)/shard_map/squeeze | solution.py:307
  160.7 3.6 %all-to-all-start.4 = ((bf16[4,128,2048]{2,1,0:T(8,128)(2,1)}), bf16[4,128,2048]{2,1,0:T(8,128)(2,1)S(1)}, u32[]{:S(2)}, u32[]{:S(2)}) async-start(bf16[4,128,2048]{2,1,0:T(8,128)(2,1)} %get-tuple-element.26), calls=%async_computation.4 | async-start | bytes 4194304 | tf_op jit(solution)/shard_map/all_to_all | solution.py:284
  165.6 8.1 %collective-permute-start.9 = (bf16[4,128,128]{2,1,0:T(8,128)(2,1)S(1)}, bf16[4,128,128]{2,1,0:T(8,128)(2,1)S(1)}, u32[]{:S(2)}, u32[]{:S(2)}) collective-permute-start(bf16[4,128,128]{2,1,0:T(8,128)(2,1)S(1)} %get-tuple-element.51), channel_id=1, source_target_pairs={{8,0},{16,8},{24,16},{28,24},{20,28},{12,20},{4,12},{0,4},{9,1},{1... | collective-permute-start | bytes 393224 | tf_op jit(solution)/shard_map/ppermute | solution.py:243
  175.3 1.8 collective-permute-done.9
  177.1 2.2 collective-permute-done.13
  179.4 3.8 %collective-permute-start.10 = (bf16[4,128,256]{2,1,0:T(8,128)(2,1)S(1)}, bf16[4,128,256]{2,1,0:T(8,128)(2,1)S(1)}, u32[]{:S(2)}, u32[]{:S(2)}) collective-permute-start(bf16[4,128,256]{2,1,0:T(8,128)(2,1)S(1)} %pad_maximum_fusion.4), channel_id=1, source_target_pairs={{8,0},{16,8},{24,16},{28,24},{20,28},{12,20},{4,12},{0,4},{9,1},{1... | collective-permute-start | bytes 786440 | tf_op jit(solution)/shard_map/ppermute | solution.py:252
  183.3 1.8 collective-permute-start.17
  185.6 4.4 %collective-permute-done.10 = bf16[4,128,256]{2,1,0:T(8,128)(2,1)S(1)} collective-permute-done((bf16[4,128,256]{2,1,0:T(8,128)(2,1)S(1)}, bf16[4,128,256]{2,1,0:T(8,128)(2,1)S(1)}, u32[]{:S(2)}, u32[]{:S(2)}) %collective-permute-start.10) | collective-permute-done | bytes 262176 | tf_op jit(solution)/shard_map/ppermute | solution.py:252
  190.1 2.5 %collective-permute-start.11 = (bf16[4,128,256]{2,1,0:T(8,128)(2,1)S(1)}, bf16[4,128,256]{2,1,0:T(8,128)(2,1)S(1)}, u32[]{:S(2)}, u32[]{:S(2)}) collective-permute-start(bf16[4,128,256]{2,1,0:T(8,128)(2,1)S(1)} %add_convert_fusion.9), channel_id=1, source_target_pairs={{8,0},{16,8},{24,16},{28,24},{20,28},{12,20},{4,12},{0,4},{9,1},{1... | collective-permute-start | bytes 786440 | tf_op jit(solution)/shard_map/ppermute | solution.py:252
  192.8 4.4 %collective-permute-done.14 = bf16[4,128,256]{2,1,0:T(8,128)(2,1)S(1)} collective-permute-done((bf16[4,128,256]{2,1,0:T(8,128)(2,1)S(1)}, bf16[4,128,256]{2,1,0:T(8,128)(2,1)S(1)}, u32[]{:S(2)}, u32[]{:S(2)}) %collective-permute-start.14) | collective-permute-done | bytes 262176 | tf_op jit(solution)/shard_map/ppermute | solution.py:253
  197.7 2.2 collective-permute-start.18
  199.9 2.0 collective-permute-start.12
  201.9 4.2 %collective-permute-done.15 = bf16[4,128,256]{2,1,0:T(8,128)(2,1)S(1)} collective-permute-done((bf16[4,128,256]{2,1,0:T(8,128)(2,1)S(1)}, bf16[4,128,256]{2,1,0:T(8,128)(2,1)S(1)}, u32[]{:S(2)}, u32[]{:S(2)}) %collective-permute-start.15) | collective-permute-done | bytes 262176 | tf_op jit(solution)/shard_map/ppermute | solution.py:253
  209.1 3.6 %collective-permute-done.16 = bf16[4,128,256]{2,1,0:T(8,128)(2,1)S(1)} collective-permute-done((bf16[4,128,256]{2,1,0:T(8,128)(2,1)S(1)}, bf16[4,128,256]{2,1,0:T(8,128)(2,1)S(1)}, u32[]{:S(2)}, u32[]{:S(2)}) %collective-permute-start.16) | collective-permute-done | bytes 262176 | tf_op jit(solution)/shard_map/ppermute | solution.py:253
  215.7 3.5 %all-to-all-start.5 = ((bf16[4,128,512]{2,1,0:T(8,128)(2,1)}), bf16[4,128,512]{2,1,0:T(8,128)(2,1)S(1)}, u32[]{:S(2)}, u32[]{:S(2)}) async-start(bf16[4,128,512]{2,1,0:T(8,128)(2,1)} %pad_maximum_fusion.3), calls=%async_computation.5 | async-start | bytes 1048576 | tf_op jit(solution)/shard_map/all_to_all | solution.py:284
  225.0 3.0 %all-to-all-done.5 = bf16[4,128,512]{2,1,0:T(8,128)(2,1)S(1)} async-done(((bf16[4,128,512]{2,1,0:T(8,128)(2,1)}), bf16[4,128,512]{2,1,0:T(8,128)(2,1)S(1)}, u32[]{:S(2)}, u32[]{:S(2)}) %all-to-all-start.5) | async-done | bytes 524320 | tf_op jit(solution)/shard_map/all_to_all | solution.py:284
  (167 shorter events, 45.8 us)
Async XLA Ops:
  7.2 9.9 %copy-start.1 = (bf16[128,8192]{1,0:T(8,128)(2,1)S(1)}, bf16[128,8192]{1,0:T(8,128)(2,1)}, u32[]{:S(2)}) copy-start(bf16[128,8192]{1,0:T(8,128)(2,1)} %param.8) | copy-start | bytes 6291460
  10.1 16.1 %all-to-all-start.1 = ((bf16[4,128,512]{2,1,0:T(8,128)(2,1)}), bf16[4,128,512]{2,1,0:T(8,128)(2,1)S(1)}, u32[]{:S(2)}, u32[]{:S(2)}) async-start(bf16[4,128,512]{2,1,0:T(8,128)(2,1)} %pad_maximum_fusion.2), calls=%async_computation.1 | async-start | bytes 1048576 | tf_op jit(solution)/shard_map/all_to_all | solution.py:284
  26.2 39.6 %all-to-all-start = ((bf16[4,128,2048]{2,1,0:T(8,128)(2,1)}), bf16[4,128,2048]{2,1,0:T(8,128)(2,1)S(1)}, u32[]{:S(2)}, u32[]{:S(2)}) async-start(bf16[4,128,2048]{2,1,0:T(8,128)(2,1)} %pad_maximum_fusion.1), calls=%async_computation | async-start | bytes 4194304 | tf_op jit(solution)/shard_map/all_to_all | solution.py:284
  29.8 89.4 %all-gather.2.cloned.1.call-start = ((), (), s32[]{:S(2)}) async-start(), calls=%async_computation.6 | async-start | bytes 2359296 | tf_op jit(solution)/shard_map/all_gather | solution.py:337
  30.7 9.2 %collective-permute-start.1 = (bf16[4,128,256]{2,1,0:T(8,128)(2,1)S(1)}, bf16[4,128,256]{2,1,0:T(8,128)(2,1)S(1)}, u32[]{:S(2)}, u32[]{:S(2)}) collective-permute-start(bf16[4,128,256]{2,1,0:T(8,128)(2,1)S(1)} %get-tuple-element.93), channel_id=1, source_target_pairs={{8,0},{16,8},{24,16},{28,24},{20,28},{12,20},{4,12},{0,4},{9,1},{1... | collective-permute-start | bytes 786440 | tf_op jit(solution)/shard_map/ppermute | solution.py:233
  33.0 8.7 %collective-permute-start = (bf16[4,128,256]{2,1,0:T(8,128)(2,1)S(1)}, bf16[4,128,256]{2,1,0:T(8,128)(2,1)S(1)}, u32[]{:S(2)}, u32[]{:S(2)}) collective-permute-start(bf16[4,128,256]{2,1,0:T(8,128)(2,1)S(1)} %get-tuple-element.93), channel_id=1, source_target_pairs={{0,8},{8,16},{16,24},{24,28},{28,20},{20,12},{12,4},{4,0},{1,9},{9... | collective-permute-start | bytes 786440 | tf_op jit(solution)/shard_map/ppermute | solution.py:232
  39.9 8.1 %collective-permute-start.3 = (bf16[4,128,256]{2,1,0:T(8,128)(2,1)S(1)}, bf16[4,128,256]{2,1,0:T(8,128)(2,1)S(1)}, u32[]{:S(2)}, u32[]{:S(2)}) collective-permute-start(bf16[4,128,256]{2,1,0:T(8,128)(2,1)S(1)} %collective-permute-done.1), channel_id=1, source_target_pairs={{8,0},{16,8},{24,16},{28,24},{20,28},{12,20},{4,12},{0,4},{9,1},{1... | collective-permute-start | bytes 786440 | tf_op jit(solution)/shard_map/ppermute | solution.py:233
  41.6 7.9 %collective-permute-start.2 = (bf16[4,128,256]{2,1,0:T(8,128)(2,1)S(1)}, bf16[4,128,256]{2,1,0:T(8,128)(2,1)S(1)}, u32[]{:S(2)}, u32[]{:S(2)}) collective-permute-start(bf16[4,128,256]{2,1,0:T(8,128)(2,1)S(1)} %collective-permute-done), channel_id=1, source_target_pairs={{0,8},{8,16},{16,24},{24,28},{28,20},{20,12},{12,4},{4,0},{1,9},{9... | collective-permute-start | bytes 786440 | tf_op jit(solution)/shard_map/ppermute | solution.py:232
  42.1 23.0 %copy-start.22 = (s32[4,32]{1,0:T(4,128)}, s32[4,32]{1,0:T(4,128)S(1)}, u32[]{:S(2)}) copy-start(s32[4,32]{1,0:T(4,128)S(1)} %select_reduce_fusion.2.vis) | copy-start | bytes 1540
  48.0 7.7 %collective-permute-start.5 = (bf16[4,128,256]{2,1,0:T(8,128)(2,1)S(1)}, bf16[4,128,256]{2,1,0:T(8,128)(2,1)S(1)}, u32[]{:S(2)}, u32[]{:S(2)}) collective-permute-start(bf16[4,128,256]{2,1,0:T(8,128)(2,1)S(1)} %collective-permute-done.3), channel_id=1, source_target_pairs={{8,0},{16,8},{24,16},{28,24},{20,28},{12,20},{4,12},{0,4},{9,1},{1... | collective-permute-start | bytes 786440 | tf_op jit(solution)/shard_map/ppermute | solution.py:233
  49.5 8.8 %collective-permute-start.4 = (bf16[4,128,256]{2,1,0:T(8,128)(2,1)S(1)}, bf16[4,128,256]{2,1,0:T(8,128)(2,1)S(1)}, u32[]{:S(2)}, u32[]{:S(2)}) collective-permute-start(bf16[4,128,256]{2,1,0:T(8,128)(2,1)S(1)} %collective-permute-done.2), channel_id=1, source_target_pairs={{0,8},{8,16},{16,24},{24,28},{28,20},{20,12},{12,4},{4,0},{1,9},{9... | collective-permute-start | bytes 786440 | tf_op jit(solution)/shard_map/ppermute | solution.py:232
  55.8 9.3 %collective-permute-start.7 = (bf16[4,128,128]{2,1,0:T(8,128)(2,1)S(1)}, bf16[4,128,128]{2,1,0:T(8,128)(2,1)S(1)}, u32[]{:S(2)}, u32[]{:S(2)}) collective-permute-start(bf16[4,128,128]{2,1,0:T(8,128)(2,1)S(1)} %slice.460), channel_id=1, source_target_pairs={{8,0},{16,8},{24,16},{28,24},{20,28},{12,20},{4,12},{0,4},{9,1},{1... | collective-permute-start | bytes 393224 | tf_op jit(solution)/shard_map/ppermute | solution.py:237
  58.3 6.1 %collective-permute-start.6 = (bf16[4,128,128]{2,1,0:T(8,128)(2,1)S(1)}, bf16[4,128,128]{2,1,0:T(8,128)(2,1)S(1)}, u32[]{:S(2)}, u32[]{:S(2)}) collective-permute-start(bf16[4,128,128]{2,1,0:T(8,128)(2,1)S(1)} %slice.459), channel_id=1, source_target_pairs={{0,8},{8,16},{16,24},{24,28},{28,20},{20,12},{12,4},{4,0},{1,9},{9... | collective-permute-start | bytes 393224 | tf_op jit(solution)/shard_map/ppermute | solution.py:236
  67.1 47.4 %all-to-all-start.3 = ((bf16[4,128,2048]{2,1,0:T(8,128)(2,1)}), bf16[4,128,2048]{2,1,0:T(8,128)(2,1)}, u32[]{:S(2)}, u32[]{:S(2)}) async-start(bf16[4,128,2048]{2,1,0:T(8,128)(2,1)} %pad_maximum_fusion), calls=%async_computation.3 | async-start | bytes 4194304 | tf_op jit(solution)/shard_map/all_to_all | solution.py:284
  87.7 70.3 %collective-permute-start.8 = (bf16[16,128,256]{2,1,0:T(8,128)(2,1)}, bf16[16,128,256]{2,1,0:T(8,128)(2,1)}, u32[]{:S(2)}, u32[]{:S(2)}) collective-permute-start(bf16[16,128,256]{2,1,0:T(8,128)(2,1)} %slice.387), channel_id=1, source_target_pairs={{0,16},{4,20},{8,24},{12,28},{16,0},{20,4},{24,8},{28,12},{1,17},{... | collective-permute-start | bytes 3145736 | tf_op jit(solution)/shard_map/ppermute | solution.py:348
  114.5 43.5 %all-to-all-start.2 = ((bf16[4,128,2048]{2,1,0:T(8,128)(2,1)}), bf16[4,128,2048]{2,1,0:T(8,128)(2,1)}, u32[]{:S(2)}, u32[]{:S(2)}) async-start(bf16[4,128,2048]{2,1,0:T(8,128)(2,1)} %get-tuple-element.19), calls=%async_computation.2 | async-start | bytes 4194304 | tf_op jit(solution)/shard_map/all_to_all | solution.py:284
  160.7 52.8 %all-to-all-start.4 = ((bf16[4,128,2048]{2,1,0:T(8,128)(2,1)}), bf16[4,128,2048]{2,1,0:T(8,128)(2,1)S(1)}, u32[]{:S(2)}, u32[]{:S(2)}) async-start(bf16[4,128,2048]{2,1,0:T(8,128)(2,1)} %get-tuple-element.26), calls=%async_computation.4 | async-start | bytes 4194304 | tf_op jit(solution)/shard_map/all_to_all | solution.py:284
  164.3 15.0 %copy-start = (bf16[32,128,256]{2,1,0:T(8,128)(2,1)S(1)}, bf16[32,128,256]{2,1,0:T(8,128)(2,1)}, u32[]{:S(2)}) copy-start(bf16[32,128,256]{2,1,0:T(8,128)(2,1)} %get-tuple-element.25) | copy-start | bytes 6291460
  165.6 11.5 %collective-permute-start.9 = (bf16[4,128,128]{2,1,0:T(8,128)(2,1)S(1)}, bf16[4,128,128]{2,1,0:T(8,128)(2,1)S(1)}, u32[]{:S(2)}, u32[]{:S(2)}) collective-permute-start(bf16[4,128,128]{2,1,0:T(8,128)(2,1)S(1)} %get-tuple-element.51), channel_id=1, source_target_pairs={{8,0},{16,8},{24,16},{28,24},{20,28},{12,20},{4,12},{0,4},{9,1},{1... | collective-permute-start | bytes 393224 | tf_op jit(solution)/shard_map/ppermute | solution.py:243
  173.7 5.6 %collective-permute-start.13 = (bf16[4,128,128]{2,1,0:T(8,128)(2,1)S(1)}, bf16[4,128,128]{2,1,0:T(8,128)(2,1)S(1)}, u32[]{:S(2)}, u32[]{:S(2)}) collective-permute-start(bf16[4,128,128]{2,1,0:T(8,128)(2,1)S(1)} %get-tuple-element.52), channel_id=1, source_target_pairs={{0,8},{8,16},{16,24},{24,28},{28,20},{20,12},{12,4},{4,0},{1,9},{9... | collective-permute-start | bytes 393224 | tf_op jit(solution)/shard_map/ppermute | solution.py:244
  179.4 10.6 %collective-permute-start.10 = (bf16[4,128,256]{2,1,0:T(8,128)(2,1)S(1)}, bf16[4,128,256]{2,1,0:T(8,128)(2,1)S(1)}, u32[]{:S(2)}, u32[]{:S(2)}) collective-permute-start(bf16[4,128,256]{2,1,0:T(8,128)(2,1)S(1)} %pad_maximum_fusion.4), channel_id=1, source_target_pairs={{8,0},{16,8},{24,16},{28,24},{20,28},{12,20},{4,12},{0,4},{9,1},{1... | collective-permute-start | bytes 786440 | tf_op jit(solution)/shard_map/ppermute | solution.py:252
  183.3 14.3 %collective-permute-start.17 = (bf16[4,128,128]{2,1,0:T(8,128)(2,1)S(1)}, bf16[4,128,128]{2,1,0:T(8,128)(2,1)S(1)}, u32[]{:S(2)}, u32[]{:S(2)}) collective-permute-start(bf16[4,128,128]{2,1,0:T(8,128)(2,1)S(1)} %get-tuple-element.94), channel_id=1, source_target_pairs={{8,0},{12,8},{4,12},{0,4},{24,16},{28,24},{20,28},{16,20},{9,1},{1... | collective-permute-start | bytes 393224 | tf_op jit(solution)/shard_map/ppermute | solution.py:243
  185.1 7.5 %collective-permute-start.19 = (bf16[4,128,128]{2,1,0:T(8,128)(2,1)S(1)}, bf16[4,128,128]{2,1,0:T(8,128)(2,1)S(1)}, u32[]{:S(2)}, u32[]{:S(2)}) collective-permute-start(bf16[4,128,128]{2,1,0:T(8,128)(2,1)S(1)} %get-tuple-element.95), channel_id=1, source_target_pairs={{0,8},{8,12},{12,4},{4,0},{16,24},{24,28},{28,20},{20,16},{1,9},{9... | collective-permute-start | bytes 393224 | tf_op jit(solution)/shard_map/ppermute | solution.py:244
  185.4 11.7 %collective-permute-start.14 = (bf16[4,128,256]{2,1,0:T(8,128)(2,1)S(1)}, bf16[4,128,256]{2,1,0:T(8,128)(2,1)S(1)}, u32[]{:S(2)}, u32[]{:S(2)}) collective-permute-start(bf16[4,128,256]{2,1,0:T(8,128)(2,1)S(1)} %pad_maximum_fusion.5), channel_id=1, source_target_pairs={{0,8},{8,16},{16,24},{24,28},{28,20},{20,12},{12,4},{4,0},{1,9},{9... | collective-permute-start | bytes 786440 | tf_op jit(solution)/shard_map/ppermute | solution.py:253
  190.1 16.8 %copy-start.5 = (bf16[128,2048]{1,0:T(8,128)(2,1)S(1)}, bf16[128,2048]{1,0:T(8,128)(2,1)}, u32[]{:S(2)}) copy-start(bf16[128,2048]{1,0:T(8,128)(2,1)} %get-tuple-element.46) | copy-start | bytes 1572868
  190.1 7.1 %collective-permute-start.11 = (bf16[4,128,256]{2,1,0:T(8,128)(2,1)S(1)}, bf16[4,128,256]{2,1,0:T(8,128)(2,1)S(1)}, u32[]{:S(2)}, u32[]{:S(2)}) collective-permute-start(bf16[4,128,256]{2,1,0:T(8,128)(2,1)S(1)} %add_convert_fusion.9), channel_id=1, source_target_pairs={{8,0},{16,8},{24,16},{28,24},{20,28},{12,20},{4,12},{0,4},{9,1},{1... | collective-permute-start | bytes 786440 | tf_op jit(solution)/shard_map/ppermute | solution.py:252
  192.7 15.0 %collective-permute-start.20 = (bf16[4,128,256]{2,1,0:T(8,128)(2,1)S(1)}, bf16[4,128,256]{2,1,0:T(8,128)(2,1)S(1)}, u32[]{:S(2)}, u32[]{:S(2)}) collective-permute-start(bf16[4,128,256]{2,1,0:T(8,128)(2,1)S(1)} %pad_maximum_fusion.7), channel_id=1, source_target_pairs={{0,8},{8,12},{12,4},{4,0},{16,24},{24,28},{28,20},{20,16},{1,9},{9... | collective-permute-start | bytes 786440 | tf_op jit(solution)/shard_map/ppermute | solution.py:253
  197.3 8.9 %collective-permute-start.15 = (bf16[4,128,256]{2,1,0:T(8,128)(2,1)S(1)}, bf16[4,128,256]{2,1,0:T(8,128)(2,1)S(1)}, u32[]{:S(2)}, u32[]{:S(2)}) collective-permute-start(bf16[4,128,256]{2,1,0:T(8,128)(2,1)S(1)} %get-tuple-element.48), channel_id=1, source_target_pairs={{0,8},{8,16},{16,24},{24,28},{28,20},{20,12},{12,4},{4,0},{1,9},{9... | collective-permute-start | bytes 786440 | tf_op jit(solution)/shard_map/ppermute | solution.py:253
  197.7 10.0 %collective-permute-start.18 = (bf16[4,128,256]{2,1,0:T(8,128)(2,1)S(1)}, bf16[4,128,256]{2,1,0:T(8,128)(2,1)S(1)}, u32[]{:S(2)}, u32[]{:S(2)}) collective-permute-start(bf16[4,128,256]{2,1,0:T(8,128)(2,1)S(1)} %pad_maximum_fusion.6), channel_id=1, source_target_pairs={{8,0},{12,8},{4,12},{0,4},{24,16},{28,24},{20,28},{16,20},{9,1},{1... | collective-permute-start | bytes 786440 | tf_op jit(solution)/shard_map/ppermute | solution.py:252
  199.9 9.2 %collective-permute-start.12 = (bf16[4,128,256]{2,1,0:T(8,128)(2,1)S(1)}, bf16[4,128,256]{2,1,0:T(8,128)(2,1)S(1)}, u32[]{:S(2)}, u32[]{:S(2)}) collective-permute-start(bf16[4,128,256]{2,1,0:T(8,128)(2,1)S(1)} %get-tuple-element.47), channel_id=1, source_target_pairs={{8,0},{16,8},{24,16},{28,24},{20,28},{12,20},{4,12},{0,4},{9,1},{1... | collective-permute-start | bytes 786440 | tf_op jit(solution)/shard_map/ppermute | solution.py:252
  206.2 6.4 %collective-permute-start.16 = (bf16[4,128,256]{2,1,0:T(8,128)(2,1)S(1)}, bf16[4,128,256]{2,1,0:T(8,128)(2,1)S(1)}, u32[]{:S(2)}, u32[]{:S(2)}) collective-permute-start(bf16[4,128,256]{2,1,0:T(8,128)(2,1)S(1)} %add_convert_fusion.6), channel_id=1, source_target_pairs={{0,8},{8,16},{16,24},{24,28},{28,20},{20,12},{12,4},{4,0},{1,9},{9... | collective-permute-start | bytes 786440 | tf_op jit(solution)/shard_map/ppermute | solution.py:253
  215.7 12.3 %all-to-all-start.5 = ((bf16[4,128,512]{2,1,0:T(8,128)(2,1)}), bf16[4,128,512]{2,1,0:T(8,128)(2,1)S(1)}, u32[]{:S(2)}, u32[]{:S(2)}) async-start(bf16[4,128,512]{2,1,0:T(8,128)(2,1)} %pad_maximum_fusion.3), calls=%async_computation.5 | async-start | bytes 1048576 | tf_op jit(solution)/shard_map/all_to_all | solution.py:284
  (25 other events, 73.3 us)
Sparse Core Ops, SparseCore 0:
  43.1 53.2 all-gather.1

commit v3 on v2

--- a/solution.py
+++ b/solution.py
@@ -52,7 +52,7 @@
 
 
 def attend_kernel(
-    vis, into, cnt, qdo, k, v, odq, dkv, qt, dt, qn, dn, s_buf, p_buf, o_acc, q_acc, dka, dva, *, heads, last
+    vis, into, cnt, qdo, k, v, odq, near, far, qt, dt, qn, dn, s_buf, p_buf, o_acc, q_acc, dka, dva, *, heads, last
 ):
     t = pl.program_id(0)
     part = pl.program_id(1)
@@ -149,8 +149,10 @@
 
     @pl.when((t == last[0]) & (part == last[1]))
     def _():
-        dkv[:, :, :HD] = (dka[...] * SCALE).astype(bf16)
-        dkv[:, :, HD:] = dva[...].astype(bf16)
+        for at, ref in ((0, near), (near.shape[0], far)):
+            own = pl.ds(at, near.shape[0])
+            ref[:, :, :HD] = (dka[own] * SCALE).astype(bf16)
+            ref[:, :, HD:] = dva[own].astype(bf16)
 
 
 def parts_of(tiles):
@@ -166,14 +168,14 @@
     rowspec = pl.BlockSpec((1, TILE, 2 * rows), lambda t, p, *_: (t, 0, p))
     keyspec = pl.BlockSpec((tiles, TILE, HD), lambda t, p, *_: (0, 0, 0), pipeline_mode=pl.Buffered(1))
     valspec = pl.BlockSpec((tiles, TILE, HD), lambda t, p, *_: (0, 0, 1), pipeline_mode=pl.Buffered(1))
-    gradspec = pl.BlockSpec((tiles, TILE, 2 * HD), lambda t, p, *_: (0, 0, 0), pipeline_mode=pl.Buffered(1))
+    gradspec = pl.BlockSpec((tiles // 2, TILE, 2 * HD), lambda t, p, *_: (0, 0, 0), pipeline_mode=pl.Buffered(1))
     return pl.pallas_call(
         functools.partial(attend_kernel, heads=rows // HD, last=(here - 1, parts - 1)),
         grid_spec=pltpu.PrefetchScalarGridSpec(
             num_scalar_prefetch=3,
             grid=(here, parts),
             in_specs=[rowspec, keyspec, valspec],
-            out_specs=[rowspec, gradspec],
+            out_specs=[rowspec, gradspec, gradspec],
             scratch_shapes=[
                 pltpu.VMEM((HD, rows), bf16),
                 pltpu.VMEM((HD, rows), bf16),
@@ -189,7 +191,8 @@
         ),
         out_shape=[
             jax.ShapeDtypeStruct((here, TILE, width), bf16),
-            jax.ShapeDtypeStruct((tiles, TILE, 2 * HD), bf16),
+            jax.ShapeDtypeStruct((tiles // 2, TILE, 2 * HD), bf16),
+            jax.ShapeDtypeStruct((tiles // 2, TILE, 2 * HD), bf16),
         ],
         compiler_params=pltpu.CompilerParams(vmem_limit_bytes=63 << 20),
         cost_estimate=pl.CostEstimate(flops=40_000_000_000, bytes_accessed=20_000_000, transcendentals=20_000_000),
@@ -203,6 +206,33 @@
         across = range(1, y_size)
         order += [z * y_size + y for y in (across if (z_size - 1 - z) % 2 == 0 else reversed(across))]
     return order
+
+
+def pack_kernel(*refs):
+    out = refs[-1]
+    width = refs[0].shape[1]
+    for i, ref in enumerate(refs[:-1]):
+        out[0, :, i * width : (i + 1) * width] = ref[...]
+
+
+def packed(one, two, width, heads_axis, pieces, at, name):
+    rows = one.shape[0]
+    stride = one.shape[1] // (width * heads_axis)
+
+    def spec(piece):
+        return pl.BlockSpec((rows, width), lambda h: (0, h * stride + at + piece))
+
+    return pl.pallas_call(
+        pack_kernel,
+        grid=(heads_axis,),
+        in_specs=[spec(p) for p in range(pieces) for _ in range(2)],
+        out_specs=pl.BlockSpec((1, rows, 2 * pieces * width), lambda h: (h, 0, 0)),
+        out_shape=jax.ShapeDtypeStruct((heads_axis, rows, 2 * pieces * width), one.dtype),
+        cost_estimate=pl.CostEstimate(
+            flops=0, bytes_accessed=8 * heads_axis * rows * pieces * width, transcendentals=0
+        ),
+        name=name,
+    )(*[x for _ in range(pieces) for x in (one, two)])
 
 
 class Ring:
@@ -266,6 +296,19 @@
     tiles = ctx * heads_axis * rows_here // TILE
     here = tiles // ctx
 
+    def swap(x):
+        return lax.all_to_all(x, "head", split_axis=0, concat_axis=0, tiled=True)
+
+    def columns(x, number, width):
+        return x[:, number * width : (number + 1) * width]
+
+    kv = packed(keys, values, HD, heads_axis, groups, 0, "pack_keys")
+    kv = swap(kv).reshape(here, TILE, groups * 2 * HD)
+    first = queries, out_grad
+    kv, queries, out_grad, segment_tiles, parent_list = lax.optimization_barrier(
+        (kv, queries, out_grad, segment_tiles, parent_list)
+    )
+
     me = lax.axis_index("ctx")
     y_size = heads_axis // 2
     whole = Ring(ctx, ctx, y_size)
@@ -280,25 +323,11 @@
     numbers, cnt = visible_lists(segment_tiles, parent_list, me * here, here, tiles)
     slots, half_slots = [renamed(numbers, table) for table in (slot_of, half_slot_of)]
 
-    def swap(x):
-        return lax.all_to_all(x, "head", split_axis=0, concat_axis=0, tiled=True)
-
-    def columns(x, number, width):
-        return x[:, number * width : (number + 1) * width]
-
     parts = parts_of(tiles)
     width = heads * HD // parts
 
-    def pair_of_rows(g):
-        return jnp.stack(
-            [
-                jnp.concatenate(
-                    [columns(x, (h * groups + g) * parts + p, width) for p in range(parts) for x in (queries, out_grad)],
-                    axis=1,
-                )
-                for h in range(heads_axis)
-            ]
-        )
+    def pair_of_rows(g, queries, out_grad):
+        return packed(queries, out_grad, width, heads_axis, parts, g * parts, f"pack_rows{g}")
 
     def joined(pieces, which):
         w = pieces[0].shape[2] // (2 * parts)
@@ -312,19 +341,15 @@
             axis=1,
         )
 
-    kv = jnp.stack(
-        [
-            jnp.concatenate([columns(x, h * groups + g, HD) for g in range(groups) for x in (keys, values)], axis=1)
-            for h in range(heads_axis)
-        ]
-    )
-    qdo = [pair_of_rows(g) for g in range(groups)]
-    kv = swap(kv).reshape(here, TILE, groups * 2 * HD)
+    qdo = [pair_of_rows(g, *((queries, out_grad) if g else first)) for g in range(groups)]
     crossed = []
     for g in range(groups):
         if g:
             qdo[g], crossed[g - 1] = lax.optimization_barrier((qdo[g], crossed[g - 1]))
         crossed.append(swap(qdo[g]).reshape(here, TILE, -1))
+
+    def blocks(x):
+        return [x[i * here : (i + 1) * here] for i in range(x.shape[0] // here)]
 
     odq, dkv = [], []
     for g in range(groups):
@@ -336,19 +361,17 @@
             mine, ring[-1] = lax.optimization_barrier((mine, ring[-1]))
             around, vis = lax.all_gather(mine, "ctx", axis=0, tiled=True), numbers
         last = g == groups - 1
-        odq_g, dkv_g = attend(vis, slots if last else half_slots, cnt, crossed[g], around, g)
+        odq_g, near_g, far_g = attend(vis, slots if last else half_slots, cnt, crossed[g], around, g)
         if g:
-            far, odq[g - 1], odq_g, dkv_g = lax.optimization_barrier((far, odq[g - 1], odq_g, dkv_g))
-            dkv[g - 1] = half.sum(
-                [add(near[i * here : (i + 1) * here], far[i * here : (i + 1) * here]) for i in range(ctx // 2)]
-            )
+            far, odq[g - 1], odq_g, near_g, far_g = lax.optimization_barrier((far, odq[g - 1], odq_g, near_g, far_g))
+            dkv[g - 1] = half.sum([add(a, b) for a, b in zip(blocks(near), blocks(far))])
         if last:
-            dkv_g = whole.sum([dkv_g[i * here : (i + 1) * here] for i in range(ctx)])
+            dkv_g = whole.sum(blocks(near_g) + blocks(far_g))
         else:
-            near, far = dkv_g[: tiles // 2], lax.ppermute(dkv_g[tiles // 2 :], "ctx", partner)
+            dkv_g, near, far = None, near_g, lax.ppermute(far_g, "ctx", partner)
         odq.append(swap(odq_g.reshape(heads_axis, rows_here, -1)))
         dkv.append(dkv_g)
-    dkv[-1], odq[-1] = lax.optimization_barrier((dkv[-1], odq[-1]))
+    dkv[-1], odq = lax.optimization_barrier((dkv[-1], odq))
     dkv = swap(jnp.concatenate(dkv, axis=-1).reshape(heads_axis, rows_here, -1))
     dk, dv = [
         jnp.concatenate(

time: 232 us -> 215 us (0.927); the launches traced: 236 us -> 214 us
  starting transfers between devices: 83.1 us -> 63.4 us
  Pallas kernels: 27.2 us -> 37.6 us
  local copies, waits for them, and re-layouts: 28.6 us -> 20 us
  other arithmetic: 18 us -> 10.8 us
  waiting for transfers between devices: 64.5 us -> 67.9 us
    ppermute x3, waiting for transfers between devices: 0.01 us -> 11.3 us  [gather(): up = lax.ppermute(up, 'ctx', self.forth)]
    ppermute x3, waiting for transfers between devices: 11.8 us -> 1.02 us  [gather(): down = lax.ppermute(down, 'ctx', self.back)]
    pallas_call x0 -> x3, Pallas kernels: none -> 10.6 us  [packed(): pl.pallas_call(pack_kernel, grid=(heads_axis,), in_specs=[spec(p) for p i...]
    ppermute x1, starting transfers between devices: 26.7 us -> 17.3 us  [local(): dkv_g, near, far = (None, near_g, lax.ppermute(far_g, 'ctx', partner))]
    another operation x10 -> x1, other arithmetic: 8.84 us -> 0.18 us  [the longest x6 7.73 us: pair_of_rows(): jnp.stack([jnp.concatenate([columns(x, (h * groups + g) * parts + p, widt...]
    slice x5 -> x0, local copies, waits for them, and re-layouts: 6.7 us -> none  [the longest x4 4.42 us: columns(): return x[:, number * width:(number + 1) * width]]
    ppermute x2, starting transfers between devices: 9.93 us -> 3.54 us  [sum(): up = lax.ppermute(far[..., :middle], 'ctx', self.back)]
    ppermute x3, starting transfers between devices: 5.48 us -> 0.63 us  [gather(): down = lax.ppermute(down, 'ctx', self.back)]
  transfers between devices with their start and end apart: 28 -> 28, of which waited for: 13 -> 15; matrix products, arithmetic and copies ran while one was open for 15% -> 12% of each run, Pallas kernels for 12% -> 16%
where the time goes in v3:
time: 215 us; the launch traced here: 214 us
  waiting for transfers between devices  67.9 us (32%)
  starting transfers between devices  63.4 us (29%)
  Pallas kernels  37.6 us (17%)
  local copies, waits for them, and re-layouts  20 us (9%)
  between operations  14.4 us (7%)
  other arithmetic  10.8 us (5%)
    ppermute x1, waiting for transfers between devices, local(): dkv_g, near, far = (None, near_g, lax.ppermute(far_g, 'ctx', partner))  28.4 us
    pallas_call x2, Pallas kernels, attend(): pl.pallas_call(functools.partial(attend_kernel, heads=rows // HD, last=(h...  27 us
    all_to_all x6, starting transfers between devices, swap(): return lax.all_to_all(x, 'head', split_axis=0, concat_axis=0, tiled=True)  24 us
    ppermute x1, starting transfers between devices, local(): dkv_g, near, far = (None, near_g, lax.ppermute(far_g, 'ctx', partner))  17.3 us
    ppermute x4, waiting for transfers between devices, sum(): down = lax.ppermute(down, 'ctx', self.forth)  13.2 us
    unnamed x39, local copies, waits for them, and re-layouts  13 us
    ppermute x3, waiting for transfers between devices, gather(): up = lax.ppermute(up, 'ctx', self.forth)  11.3 us
    pallas_call x3, Pallas kernels, packed(): pl.pallas_call(pack_kernel, grid=(heads_axis,), in_specs=[spec(p) for p i...  10.6 us
  transfers between devices with their start and end apart: 28, of which 15 were waited for; matrix products, arithmetic and copies ran while one was open for 12% of the time, Pallas kernels for 16%

profile of v3, /device:TPU:0, one launch (start us, length us, event | category | flops | bytes accessed | tf_op | source)
XLA Modules:
  0.0 214.1 jit_solution(4738949041432092943)
XLA Ops:
  7.2 3.0 %pack_keys.1 = bf16[4,128,512]{2,1,0:T(8,128)(2,1)} custom-call(bf16[128,1024]{1,0:T(8,128)(2,1)} %refs_2_.1, bf16[128,1024]{1,0:T(8,128)(2,1)} %refs_3_.1, bf16[128,1024]{1,0:T(8,128)(2,1)} %refs_2_.1, bf16[128,1024]{1,0:T(8,128)(2,1)} %refs_3_.1), custom_call_target="tpu_custom_call" | custom-call | bytes 1048576 | tf_op jit(solution)/shard_map/pack_keys/pallas_call | solution.py:225
  10.2 4.2 %all-to-all-start = ((bf16[4,128,512]{2,1,0:T(8,128)(2,1)}), bf16[4,128,512]{2,1,0:T(8,128)(2,1)S(1)}, u32[]{:S(2)}, u32[]{:S(2)}) async-start(bf16[4,128,512]{2,1,0:T(8,128)(2,1)} %pack_keys.1), calls=%async_computation | async-start | bytes 1048576 | tf_op jit(solution)/shard_map/all_to_all | solution.py:300
  15.2 3.8 %pack_rows0.1 = bf16[4,128,2048]{2,1,0:T(8,128)(2,1)} custom-call(bf16[128,8192]{1,0:T(8,128)(2,1)} %refs_0_.4, bf16[128,8192]{1,0:T(8,128)(2,1)} %refs_1_.4), custom_call_target="tpu_custom_call" | custom-call | bytes 4194304 | tf_op jit(solution)/shard_map/pack_rows0/pallas_call | solution.py:225
  19.7 3.5 %all-to-all-done = bf16[4,128,512]{2,1,0:T(8,128)(2,1)S(1)} async-done(((bf16[4,128,512]{2,1,0:T(8,128)(2,1)}), bf16[4,128,512]{2,1,0:T(8,128)(2,1)S(1)}, u32[]{:S(2)}, u32[]{:S(2)}) %all-to-all-start) | async-done | bytes 524320 | tf_op jit(solution)/shard_map/all_to_all | solution.py:300
  23.2 3.6 %all-to-all-start.1 = ((bf16[4,128,2048]{2,1,0:T(8,128)(2,1)}), bf16[4,128,2048]{2,1,0:T(8,128)(2,1)S(1)}, u32[]{:S(2)}, u32[]{:S(2)}) async-start(bf16[4,128,2048]{2,1,0:T(8,128)(2,1)} %pack_rows0.1), calls=%async_computation.1 | async-start | bytes 4194304 | tf_op jit(solution)/shard_map/all_to_all | solution.py:300
  27.8 2.3 %collective-permute-start = (bf16[4,128,256]{2,1,0:T(8,128)(2,1)S(1)}, bf16[4,128,256]{2,1,0:T(8,128)(2,1)S(1)}, u32[]{:S(2)}, u32[]{:S(2)}) collective-permute-start(bf16[4,128,256]{2,1,0:T(8,128)(2,1)S(1)} %get-tuple-element.95), channel_id=1, source_target_pairs={{0,8},{8,16},{16,24},{24,28},{28,20},{20,12},{12,4},{4,0},{1,9},{9... | collective-permute-start | bytes 786440 | tf_op jit(solution)/shard_map/ppermute | solution.py:262
  32.0 4.9 %collective-permute-done = bf16[4,128,256]{2,1,0:T(8,128)(2,1)S(1)} collective-permute-done((bf16[4,128,256]{2,1,0:T(8,128)(2,1)S(1)}, bf16[4,128,256]{2,1,0:T(8,128)(2,1)S(1)}, u32[]{:S(2)}, u32[]{:S(2)}) %collective-permute-start) | collective-permute-done | bytes 262176 | tf_op jit(solution)/shard_map/ppermute | solution.py:262
  36.9 1.8 collective-permute-start.2
  39.0 3.8 %pack_rows1.1 = bf16[4,128,2048]{2,1,0:T(8,128)(2,1)} custom-call(bf16[128,8192]{1,0:T(8,128)(2,1)} %refs_0_.4, bf16[128,8192]{1,0:T(8,128)(2,1)} %refs_1_.4), custom_call_target="tpu_custom_call" | custom-call | bytes 4194304 | tf_op jit(solution)/shard_map/pack_rows1/pallas_call | solution.py:225
  44.9 1.6 collective-permute-start.4
  49.1 5.9 %collective-permute-done.4 = bf16[4,128,256]{2,1,0:T(8,128)(2,1)S(1)} collective-permute-done((bf16[4,128,256]{2,1,0:T(8,128)(2,1)S(1)}, bf16[4,128,256]{2,1,0:T(8,128)(2,1)S(1)}, u32[]{:S(2)}, u32[]{:S(2)}) %collective-permute-start.4) | collective-permute-done | bytes 262176 | tf_op jit(solution)/shard_map/ppermute | solution.py:262
  55.0 2.5 %collective-permute-start.6 = (bf16[4,128,128]{2,1,0:T(8,128)(2,1)S(1)}, bf16[4,128,128]{2,1,0:T(8,128)(2,1)S(1)}, u32[]{:S(2)}, u32[]{:S(2)}) collective-permute-start(bf16[4,128,128]{2,1,0:T(8,128)(2,1)S(1)} %slice.321), channel_id=1, source_target_pairs={{0,8},{8,16},{16,24},{24,28},{28,20},{20,12},{12,4},{4,0},{1,9},{9... | collective-permute-start | bytes 393224 | tf_op jit(solution)/shard_map/ppermute | solution.py:266
  60.1 2.1 collective-permute-done.6
  62.9 2.9 %collective-permute-done.7 = bf16[4,128,128]{2,1,0:T(8,128)(2,1)S(1)} collective-permute-done((bf16[4,128,128]{2,1,0:T(8,128)(2,1)S(1)}, bf16[4,128,128]{2,1,0:T(8,128)(2,1)S(1)}, u32[]{:S(2)}, u32[]{:S(2)}) %collective-permute-start.7) | collective-permute-done | bytes 131104 | tf_op jit(solution)/shard_map/ppermute | solution.py:267
  67.9 4.5 %all-to-all-start.3 = ((bf16[4,128,2048]{2,1,0:T(8,128)(2,1)}), bf16[4,128,2048]{2,1,0:T(8,128)(2,1)}, u32[]{:S(2)}, u32[]{:S(2)}) async-start(bf16[4,128,2048]{2,1,0:T(8,128)(2,1)} %pack_rows1.1), calls=%async_computation.3 | async-start | bytes 4194304 | tf_op jit(solution)/shard_map/all_to_all | solution.py:300
  72.3 13.5 %attend0.1 = (bf16[4,128,2048]{2,1,0:T(8,128)(2,1)}, bf16[16,128,256]{2,1,0:T(8,128)(2,1)}, bf16[16,128,256]{2,1,0:T(8,128)(2,1)}) custom-call(s32[4,32]{1,0:T(4,128)} %get-tuple-element.49.vis.into, s32[4,32]{1,0:T(4,128)} %get-tuple-element.48.into, s32[4]{0:T(128)} %get-tuple-element.52.cnt, bf16[4,128,2048]{2,1,0:T(8,128)(2,1)} %copy-done, ...), custom_call_target="tpu_custom_call" | custom-call | flops 40000000000 | bytes 20000000 | tf_op jit(solution)/shard_map/attend0/pallas_call | solution.py:172
  85.9 17.3 %collective-permute-start.8 = (bf16[16,128,256]{2,1,0:T(8,128)(2,1)}, bf16[16,128,256]{2,1,0:T(8,128)(2,1)}, u32[]{:S(2)}, u32[]{:S(2)}) collective-permute-start(bf16[16,128,256]{2,1,0:T(8,128)(2,1)} %get-tuple-element.32), channel_id=1, source_target_pairs={{0,16},{4,20},{8,24},{12,28},{16,0},{20,4},{24,8},{28,12},{1,17},{... | collective-permute-start | bytes 3145736 | tf_op jit(solution)/shard_map/ppermute | solution.py:371
  103.1 4.6 %all-to-all-start.2 = ((bf16[4,128,2048]{2,1,0:T(8,128)(2,1)}), bf16[4,128,2048]{2,1,0:T(8,128)(2,1)}, u32[]{:S(2)}, u32[]{:S(2)}) async-start(bf16[4,128,2048]{2,1,0:T(8,128)(2,1)} %get-tuple-element.33), calls=%async_computation.2 | async-start | bytes 4194304 | tf_op jit(solution)/shard_map/all_to_all | solution.py:300
  107.8 13.5 %attend1.1 = (bf16[4,128,2048]{2,1,0:T(8,128)(2,1)}, bf16[16,128,256]{2,1,0:T(8,128)(2,1)}, bf16[16,128,256]{2,1,0:T(8,128)(2,1)}) custom-call(s32[4,32]{1,0:T(4,128)} %copy-done.2, s32[4,32]{1,0:T(4,128)} %get-tuple-element.49.vis.into, s32[4]{0:T(128)} %get-tuple-element.52.cnt, bf16[4,128,2048]{2,1,0:T(8,128)(2,1)} %all-to-all-done.3.qdo, ...), custom_call_target="tpu_custom_call" | custom-call | flops 40000000000 | bytes 20000000 | tf_op jit(solution)/shard_map/attend1/pallas_call | solution.py:172
  121.3 28.4 %collective-permute-done.8 = bf16[16,128,256]{2,1,0:T(8,128)(2,1)} collective-permute-done((bf16[16,128,256]{2,1,0:T(8,128)(2,1)}, bf16[16,128,256]{2,1,0:T(8,128)(2,1)}, u32[]{:S(2)}, u32[]{:S(2)}) %collective-permute-start.8) | collective-permute-done | bytes 1048608 | tf_op jit(solution)/shard_map/ppermute | solution.py:371
  149.7 1.8 fusion.10
  152.2 1.5 collective-permute-start.9
  153.8 1.5 add_convert_fusion.3
  156.0 2.0 collective-permute-start.17
  158.2 3.6 %all-to-all-start.4 = ((bf16[4,128,2048]{2,1,0:T(8,128)(2,1)}), bf16[4,128,2048]{2,1,0:T(8,128)(2,1)S(1)}, u32[]{:S(2)}, u32[]{:S(2)}) async-start(bf16[4,128,2048]{2,1,0:T(8,128)(2,1)} %get-tuple-element.42), calls=%async_computation.4 | async-start | bytes 4194304 | tf_op jit(solution)/shard_map/all_to_all | solution.py:300
  165.4 2.1 collective-permute-start.18
  167.4 4.7 %collective-permute-done.14 = bf16[4,128,256]{2,1,0:T(8,128)(2,1)S(1)} collective-permute-done((bf16[4,128,256]{2,1,0:T(8,128)(2,1)S(1)}, bf16[4,128,256]{2,1,0:T(8,128)(2,1)S(1)}, u32[]{:S(2)}, u32[]{:S(2)}) %collective-permute-start.14) | collective-permute-done | bytes 262176 | tf_op jit(solution)/shard_map/ppermute | solution.py:283
  173.7 1.6 collective-permute-start.11
  175.9 6.5 %collective-permute-done.15 = bf16[4,128,256]{2,1,0:T(8,128)(2,1)S(1)} collective-permute-done((bf16[4,128,256]{2,1,0:T(8,128)(2,1)S(1)}, bf16[4,128,256]{2,1,0:T(8,128)(2,1)S(1)}, u32[]{:S(2)}, u32[]{:S(2)}) %collective-permute-start.15) | collective-permute-done | bytes 262176 | tf_op jit(solution)/shard_map/ppermute | solution.py:283
  188.0 3.7 %collective-permute-done.12 = bf16[4,128,256]{2,1,0:T(8,128)(2,1)S(1)} collective-permute-done((bf16[4,128,256]{2,1,0:T(8,128)(2,1)S(1)}, bf16[4,128,256]{2,1,0:T(8,128)(2,1)S(1)}, u32[]{:S(2)}, u32[]{:S(2)}) %collective-permute-start.12) | collective-permute-done | bytes 262176 | tf_op jit(solution)/shard_map/ppermute | solution.py:282
  193.9 3.5 %all-to-all-start.5 = ((bf16[4,128,512]{2,1,0:T(8,128)(2,1)}), bf16[4,128,512]{2,1,0:T(8,128)(2,1)S(1)}, u32[]{:S(2)}, u32[]{:S(2)}) async-start(bf16[4,128,512]{2,1,0:T(8,128)(2,1)} %pad_maximum_fusion), calls=%async_computation.5 | async-start | bytes 1048576 | tf_op jit(solution)/shard_map/all_to_all | solution.py:300
  197.4 1.7 slice_bitcast_fusion.1
  (116 shorter events, 37.8 us)
Async XLA Ops:
  7.2 7.2 %copy-start.8 = (s32[8]{0:T(128)S(1)}, s32[8]{0:T(128)}, u32[]{:S(2)}) copy-start(s32[8]{0:T(128)} %constant.120.clone) | copy-start | bytes 100
  10.2 13.1 %all-to-all-start = ((bf16[4,128,512]{2,1,0:T(8,128)(2,1)}), bf16[4,128,512]{2,1,0:T(8,128)(2,1)S(1)}, u32[]{:S(2)}, u32[]{:S(2)}) async-start(bf16[4,128,512]{2,1,0:T(8,128)(2,1)} %pack_keys.1), calls=%async_computation | async-start | bytes 1048576 | tf_op jit(solution)/shard_map/all_to_all | solution.py:300
  19.7 10.3 %copy-start.6 = (s32[8]{0:T(128)S(1)}, s32[8]{0:T(128)}, u32[]{:S(2)}) copy-start(s32[8]{0:T(128)} %param.12) | copy-start | bytes 100
  19.7 10.8 %copy-start.7 = (s32[8]{0:T(128)S(1)}, s32[8]{0:T(128)}, u32[]{:S(2)}) copy-start(s32[8]{0:T(128)} %param.13) | copy-start | bytes 100
  23.2 43.3 %all-to-all-start.1 = ((bf16[4,128,2048]{2,1,0:T(8,128)(2,1)}), bf16[4,128,2048]{2,1,0:T(8,128)(2,1)S(1)}, u32[]{:S(2)}, u32[]{:S(2)}) async-start(bf16[4,128,2048]{2,1,0:T(8,128)(2,1)} %pack_rows0.1), calls=%async_computation.1 | async-start | bytes 4194304 | tf_op jit(solution)/shard_map/all_to_all | solution.py:300
  26.9 80.9 %all-gather.2.cloned.1.call-start = ((), (), s32[]{:S(2)}) async-start(), calls=%async_computation.6 | async-start | bytes 2359296 | tf_op jit(solution)/shard_map/all_gather | solution.py:362
  27.8 9.1 %collective-permute-start = (bf16[4,128,256]{2,1,0:T(8,128)(2,1)S(1)}, bf16[4,128,256]{2,1,0:T(8,128)(2,1)S(1)}, u32[]{:S(2)}, u32[]{:S(2)}) collective-permute-start(bf16[4,128,256]{2,1,0:T(8,128)(2,1)S(1)} %get-tuple-element.95), channel_id=1, source_target_pairs={{0,8},{8,16},{16,24},{24,28},{28,20},{20,12},{12,4},{4,0},{1,9},{9... | collective-permute-start | bytes 786440 | tf_op jit(solution)/shard_map/ppermute | solution.py:262
  30.0 8.7 %collective-permute-start.1 = (bf16[4,128,256]{2,1,0:T(8,128)(2,1)S(1)}, bf16[4,128,256]{2,1,0:T(8,128)(2,1)S(1)}, u32[]{:S(2)}, u32[]{:S(2)}) collective-permute-start(bf16[4,128,256]{2,1,0:T(8,128)(2,1)S(1)} %get-tuple-element.95), channel_id=1, source_target_pairs={{8,0},{16,8},{24,16},{28,24},{20,28},{12,20},{4,12},{0,4},{9,1},{1... | collective-permute-start | bytes 786440 | tf_op jit(solution)/shard_map/ppermute | solution.py:263
  36.9 8.1 %collective-permute-start.2 = (bf16[4,128,256]{2,1,0:T(8,128)(2,1)S(1)}, bf16[4,128,256]{2,1,0:T(8,128)(2,1)S(1)}, u32[]{:S(2)}, u32[]{:S(2)}) collective-permute-start(bf16[4,128,256]{2,1,0:T(8,128)(2,1)S(1)} %collective-permute-done), channel_id=1, source_target_pairs={{0,8},{8,16},{16,24},{24,28},{28,20},{20,12},{12,4},{4,0},{1,9},{9... | collective-permute-start | bytes 786440 | tf_op jit(solution)/shard_map/ppermute | solution.py:262
  38.7 7.9 %collective-permute-start.3 = (bf16[4,128,256]{2,1,0:T(8,128)(2,1)S(1)}, bf16[4,128,256]{2,1,0:T(8,128)(2,1)S(1)}, u32[]{:S(2)}, u32[]{:S(2)}) collective-permute-start(bf16[4,128,256]{2,1,0:T(8,128)(2,1)S(1)} %collective-permute-done.1), channel_id=1, source_target_pairs={{8,0},{16,8},{24,16},{28,24},{20,28},{12,20},{4,12},{0,4},{9,1},{1... | collective-permute-start | bytes 786440 | tf_op jit(solution)/shard_map/ppermute | solution.py:263
  44.9 10.1 %collective-permute-start.4 = (bf16[4,128,256]{2,1,0:T(8,128)(2,1)S(1)}, bf16[4,128,256]{2,1,0:T(8,128)(2,1)S(1)}, u32[]{:S(2)}, u32[]{:S(2)}) collective-permute-start(bf16[4,128,256]{2,1,0:T(8,128)(2,1)S(1)} %collective-permute-done.2), channel_id=1, source_target_pairs={{0,8},{8,16},{16,24},{24,28},{28,20},{20,12},{12,4},{4,0},{1,9},{9... | collective-permute-start | bytes 786440 | tf_op jit(solution)/shard_map/ppermute | solution.py:262
  46.5 12.1 %collective-permute-start.5 = (bf16[4,128,256]{2,1,0:T(8,128)(2,1)S(1)}, bf16[4,128,256]{2,1,0:T(8,128)(2,1)S(1)}, u32[]{:S(2)}, u32[]{:S(2)}) collective-permute-start(bf16[4,128,256]{2,1,0:T(8,128)(2,1)S(1)} %collective-permute-done.3), channel_id=1, source_target_pairs={{8,0},{16,8},{24,16},{28,24},{20,28},{12,20},{4,12},{0,4},{9,1},{1... | collective-permute-start | bytes 786440 | tf_op jit(solution)/shard_map/ppermute | solution.py:263
  55.0 7.2 %collective-permute-start.6 = (bf16[4,128,128]{2,1,0:T(8,128)(2,1)S(1)}, bf16[4,128,128]{2,1,0:T(8,128)(2,1)S(1)}, u32[]{:S(2)}, u32[]{:S(2)}) collective-permute-start(bf16[4,128,128]{2,1,0:T(8,128)(2,1)S(1)} %slice.321), channel_id=1, source_target_pairs={{0,8},{8,16},{16,24},{24,28},{28,20},{20,12},{12,4},{4,0},{1,9},{9... | collective-permute-start | bytes 393224 | tf_op jit(solution)/shard_map/ppermute | solution.py:266
  58.6 7.3 %collective-permute-start.7 = (bf16[4,128,128]{2,1,0:T(8,128)(2,1)S(1)}, bf16[4,128,128]{2,1,0:T(8,128)(2,1)S(1)}, u32[]{:S(2)}, u32[]{:S(2)}) collective-permute-start(bf16[4,128,128]{2,1,0:T(8,128)(2,1)S(1)} %slice.322), channel_id=1, source_target_pairs={{8,0},{16,8},{24,16},{28,24},{20,28},{12,20},{4,12},{0,4},{9,1},{1... | collective-permute-start | bytes 393224 | tf_op jit(solution)/shard_map/ppermute | solution.py:267
  67.9 35.3 %all-to-all-start.3 = ((bf16[4,128,2048]{2,1,0:T(8,128)(2,1)}), bf16[4,128,2048]{2,1,0:T(8,128)(2,1)}, u32[]{:S(2)}, u32[]{:S(2)}) async-start(bf16[4,128,2048]{2,1,0:T(8,128)(2,1)} %pack_rows1.1), calls=%async_computation.3 | async-start | bytes 4194304 | tf_op jit(solution)/shard_map/all_to_all | solution.py:300
  85.9 63.8 %collective-permute-start.8 = (bf16[16,128,256]{2,1,0:T(8,128)(2,1)}, bf16[16,128,256]{2,1,0:T(8,128)(2,1)}, u32[]{:S(2)}, u32[]{:S(2)}) collective-permute-start(bf16[16,128,256]{2,1,0:T(8,128)(2,1)} %get-tuple-element.32), channel_id=1, source_target_pairs={{0,16},{4,20},{8,24},{12,28},{16,0},{20,4},{24,8},{28,12},{1,17},{... | collective-permute-start | bytes 3145736 | tf_op jit(solution)/shard_map/ppermute | solution.py:371
  103.1 46.6 %all-to-all-start.2 = ((bf16[4,128,2048]{2,1,0:T(8,128)(2,1)}), bf16[4,128,2048]{2,1,0:T(8,128)(2,1)}, u32[]{:S(2)}, u32[]{:S(2)}) async-start(bf16[4,128,2048]{2,1,0:T(8,128)(2,1)} %get-tuple-element.33), calls=%async_computation.2 | async-start | bytes 4194304 | tf_op jit(solution)/shard_map/all_to_all | solution.py:300
  151.5 10.3 %collective-permute-start.13 = (bf16[4,128,128]{2,1,0:T(8,128)(2,1)}, bf16[4,128,128]{2,1,0:T(8,128)(2,1)}, u32[]{:S(2)}, u32[]{:S(2)}) collective-permute-start(bf16[4,128,128]{2,1,0:T(8,128)(2,1)} %get-tuple-element.70), channel_id=1, source_target_pairs={{0,8},{8,16},{16,24},{24,28},{28,20},{20,12},{12,4},{4,0},{1,9},{9... | collective-permute-start | bytes 393224 | tf_op jit(solution)/shard_map/ppermute | solution.py:274
  152.2 9.6 %collective-permute-start.9 = (bf16[4,128,128]{2,1,0:T(8,128)(2,1)}, bf16[4,128,128]{2,1,0:T(8,128)(2,1)}, u32[]{:S(2)}, u32[]{:S(2)}) collective-permute-start(bf16[4,128,128]{2,1,0:T(8,128)(2,1)} %get-tuple-element.69), channel_id=1, source_target_pairs={{8,0},{16,8},{24,16},{28,24},{20,28},{12,20},{4,12},{0,4},{9,1},{1... | collective-permute-start | bytes 393224 | tf_op jit(solution)/shard_map/ppermute | solution.py:273
  156.0 9.3 %collective-permute-start.17 = (bf16[4,128,128]{2,1,0:T(8,128)(2,1)}, bf16[4,128,128]{2,1,0:T(8,128)(2,1)S(1)}, u32[]{:S(2)}, u32[]{:S(2)}) collective-permute-start(bf16[4,128,128]{2,1,0:T(8,128)(2,1)} %get-tuple-element.96), channel_id=1, source_target_pairs={{8,0},{12,8},{4,12},{0,4},{24,16},{28,24},{20,28},{16,20},{9,1},{1... | collective-permute-start | bytes 393224 | tf_op jit(solution)/shard_map/ppermute | solution.py:273
  158.1 17.3 %collective-permute-start.19 = (bf16[4,128,128]{2,1,0:T(8,128)(2,1)S(1)}, bf16[4,128,128]{2,1,0:T(8,128)(2,1)S(1)}, u32[]{:S(2)}, u32[]{:S(2)}) collective-permute-start(bf16[4,128,128]{2,1,0:T(8,128)(2,1)S(1)} %get-tuple-element.97), channel_id=1, source_target_pairs={{0,8},{8,12},{12,4},{4,0},{16,24},{24,28},{28,20},{20,16},{1,9},{9... | collective-permute-start | bytes 393224 | tf_op jit(solution)/shard_map/ppermute | solution.py:274
  158.2 34.9 %all-to-all-start.4 = ((bf16[4,128,2048]{2,1,0:T(8,128)(2,1)}), bf16[4,128,2048]{2,1,0:T(8,128)(2,1)S(1)}, u32[]{:S(2)}, u32[]{:S(2)}) async-start(bf16[4,128,2048]{2,1,0:T(8,128)(2,1)} %get-tuple-element.42), calls=%async_computation.4 | async-start | bytes 4194304 | tf_op jit(solution)/shard_map/all_to_all | solution.py:300
  161.8 11.8 %copy-start.1 = (bf16[16,128,256]{2,1,0:T(8,128)(2,1)S(1)}, bf16[16,128,256]{2,1,0:T(8,128)(2,1)}, u32[]{:S(2)}) copy-start(bf16[16,128,256]{2,1,0:T(8,128)(2,1)} %get-tuple-element.39) | copy-start | bytes 3145732
  163.1 9.0 %collective-permute-start.14 = (bf16[4,128,256]{2,1,0:T(8,128)(2,1)S(1)}, bf16[4,128,256]{2,1,0:T(8,128)(2,1)S(1)}, u32[]{:S(2)}, u32[]{:S(2)}) collective-permute-start(bf16[4,128,256]{2,1,0:T(8,128)(2,1)S(1)} %pad_maximum_fusion.2), channel_id=1, source_target_pairs={{0,8},{8,16},{16,24},{24,28},{28,20},{20,12},{12,4},{4,0},{1,9},{9... | collective-permute-start | bytes 786440 | tf_op jit(solution)/shard_map/ppermute | solution.py:283
  163.9 9.7 %collective-permute-start.10 = (bf16[4,128,256]{2,1,0:T(8,128)(2,1)S(1)}, bf16[4,128,256]{2,1,0:T(8,128)(2,1)S(1)}, u32[]{:S(2)}, u32[]{:S(2)}) collective-permute-start(bf16[4,128,256]{2,1,0:T(8,128)(2,1)S(1)} %pad_maximum_fusion.1), channel_id=1, source_target_pairs={{8,0},{16,8},{24,16},{28,24},{20,28},{12,20},{4,12},{0,4},{9,1},{1... | collective-permute-start | bytes 786440 | tf_op jit(solution)/shard_map/ppermute | solution.py:282
  165.4 20.6 %collective-permute-start.18 = (bf16[4,128,256]{2,1,0:T(8,128)(2,1)S(1)}, bf16[4,128,256]{2,1,0:T(8,128)(2,1)S(1)}, u32[]{:S(2)}, u32[]{:S(2)}) collective-permute-start(bf16[4,128,256]{2,1,0:T(8,128)(2,1)S(1)} %pad_maximum_fusion.3), channel_id=1, source_target_pairs={{8,0},{12,8},{4,12},{0,4},{24,16},{28,24},{20,28},{16,20},{9,1},{1... | collective-permute-start | bytes 786440 | tf_op jit(solution)/shard_map/ppermute | solution.py:282
  173.1 9.2 %collective-permute-start.15 = (bf16[4,128,256]{2,1,0:T(8,128)(2,1)S(1)}, bf16[4,128,256]{2,1,0:T(8,128)(2,1)S(1)}, u32[]{:S(2)}, u32[]{:S(2)}) collective-permute-start(bf16[4,128,256]{2,1,0:T(8,128)(2,1)S(1)} %add_convert_fusion.7), channel_id=1, source_target_pairs={{0,8},{8,16},{16,24},{24,28},{28,20},{20,12},{12,4},{4,0},{1,9},{9... | collective-permute-start | bytes 786440 | tf_op jit(solution)/shard_map/ppermute | solution.py:283
  173.7 10.1 %collective-permute-start.11 = (bf16[4,128,256]{2,1,0:T(8,128)(2,1)S(1)}, bf16[4,128,256]{2,1,0:T(8,128)(2,1)S(1)}, u32[]{:S(2)}, u32[]{:S(2)}) collective-permute-start(bf16[4,128,256]{2,1,0:T(8,128)(2,1)S(1)} %add_convert_fusion.9), channel_id=1, source_target_pairs={{8,0},{16,8},{24,16},{28,24},{20,28},{12,20},{4,12},{0,4},{9,1},{1... | collective-permute-start | bytes 786440 | tf_op jit(solution)/shard_map/ppermute | solution.py:282
  175.4 11.4 %collective-permute-start.20 = (bf16[4,128,256]{2,1,0:T(8,128)(2,1)S(1)}, bf16[4,128,256]{2,1,0:T(8,128)(2,1)S(1)}, u32[]{:S(2)}, u32[]{:S(2)}) collective-permute-start(bf16[4,128,256]{2,1,0:T(8,128)(2,1)S(1)} %pad_maximum_fusion.4), channel_id=1, source_target_pairs={{0,8},{8,12},{12,4},{4,0},{16,24},{24,28},{28,20},{20,16},{1,9},{9... | collective-permute-start | bytes 786440 | tf_op jit(solution)/shard_map/ppermute | solution.py:283
  183.9 7.8 %collective-permute-start.12 = (bf16[4,128,256]{2,1,0:T(8,128)(2,1)S(1)}, bf16[4,128,256]{2,1,0:T(8,128)(2,1)S(1)}, u32[]{:S(2)}, u32[]{:S(2)}) collective-permute-start(bf16[4,128,256]{2,1,0:T(8,128)(2,1)S(1)} %get-tuple-element.65), channel_id=1, source_target_pairs={{8,0},{16,8},{24,16},{28,24},{20,28},{12,20},{4,12},{0,4},{9,1},{1... | collective-permute-start | bytes 786440 | tf_op jit(solution)/shard_map/ppermute | solution.py:282
  185.4 7.6 %collective-permute-start.16 = (bf16[4,128,256]{2,1,0:T(8,128)(2,1)S(1)}, bf16[4,128,256]{2,1,0:T(8,128)(2,1)S(1)}, u32[]{:S(2)}, u32[]{:S(2)}) collective-permute-start(bf16[4,128,256]{2,1,0:T(8,128)(2,1)S(1)} %get-tuple-element.66), channel_id=1, source_target_pairs={{0,8},{8,16},{16,24},{24,28},{28,20},{20,12},{12,4},{4,0},{1,9},{9... | collective-permute-start | bytes 786440 | tf_op jit(solution)/shard_map/ppermute | solution.py:283
  193.9 12.3 %all-to-all-start.5 = ((bf16[4,128,512]{2,1,0:T(8,128)(2,1)}), bf16[4,128,512]{2,1,0:T(8,128)(2,1)S(1)}, u32[]{:S(2)}, u32[]{:S(2)}) async-start(bf16[4,128,512]{2,1,0:T(8,128)(2,1)} %pad_maximum_fusion), calls=%async_computation.5 | async-start | bytes 1048576 | tf_op jit(solution)/shard_map/all_to_all | solution.py:300
  (5 other events, 10.4 us)
Sparse Core Ops, SparseCore 0:
  39.2 53.3 all-gather.1

commit v4 on v3

--- a/solution.py
+++ b/solution.py
@@ -299,11 +299,23 @@
     def swap(x):
         return lax.all_to_all(x, "head", split_axis=0, concat_axis=0, tiled=True)
 
+    def swap_small(x):
+        own = lax.axis_index("head")
+
+        def pick(y, number):
+            return lax.dynamic_index_in_dim(y, own ^ number, 0, keepdims=False)
+
+        came = [pick(x, 0)]
+        for k in range(1, heads_axis):
+            came.append(lax.ppermute(pick(x, k), "head", [(h, h ^ k) for h in range(heads_axis)]))
+        came = jnp.stack(came)
+        return jnp.stack([pick(came, h) for h in range(heads_axis)])
+
     def columns(x, number, width):
         return x[:, number * width : (number + 1) * width]
 
     kv = packed(keys, values, HD, heads_axis, groups, 0, "pack_keys")
-    kv = swap(kv).reshape(here, TILE, groups * 2 * HD)
+    kv = swap_small(kv).reshape(here, TILE, groups * 2 * HD)
     first = queries, out_grad
     kv, queries, out_grad, segment_tiles, parent_list = lax.optimization_barrier(
         (kv, queries, out_grad, segment_tiles, parent_list)
@@ -356,9 +368,9 @@
         mine = kv[:, :, g * 2 * HD : (g + 1) * 2 * HD]
         if g == 0:
             ring = whole.gather(mine)
+            kv, ring[4] = lax.optimization_barrier((kv, ring[4]))
             around, vis = jnp.concatenate(ring, axis=0), slots
         else:
-            mine, ring[-1] = lax.optimization_barrier((mine, ring[-1]))
             around, vis = lax.all_gather(mine, "ctx", axis=0, tiled=True), numbers
         last = g == groups - 1
         odq_g, near_g, far_g = attend(vis, slots if last else half_slots, cnt, crossed[g], around, g)
@@ -372,7 +384,7 @@
         odq.append(swap(odq_g.reshape(heads_axis, rows_here, -1)))
         dkv.append(dkv_g)
     dkv[-1], odq = lax.optimization_barrier((dkv[-1], odq))
-    dkv = swap(jnp.concatenate(dkv, axis=-1).reshape(heads_axis, rows_here, -1))
+    dkv = swap_small(jnp.concatenate(dkv, axis=-1).reshape(heads_axis, rows_here, -1))
     dk, dv = [
         jnp.concatenate(
             [columns(dkv[h], 2 * g + which, HD) for h in range(heads_axis) for g in range(groups)], axis=1

time: 215 us -> 202 us (0.940)
  starting transfers between devices: 63.4 us -> 57.5 us
  local copies, waits for them, and re-layouts: 20 us -> 16 us
  waiting for transfers between devices: 67.9 us -> 65 us
    all_gather x1, waiting for transfers between devices: 0.02 us -> 28.2 us  [local(): around, vis = (lax.all_gather(mine, 'ctx', axis=0, tiled=True), numbers)]
    ppermute x1, waiting for transfers between devices: 28.4 us -> 5.59 us  [local(): dkv_g, near, far = (None, near_g, lax.ppermute(far_g, 'ctx', partner))]
    all_to_all x6 -> x4, starting transfers between devices: 24 us -> 16.4 us  [swap(): return lax.all_to_all(x, 'head', split_axis=0, concat_axis=0, tiled=True)]
    ppermute x4, starting transfers between devices: 2.37 us -> 9.87 us  [sum(): down = lax.ppermute(down, 'ctx', self.forth)]
    ppermute x3, waiting for transfers between devices: 11.3 us -> 4.46 us  [gather(): up = lax.ppermute(up, 'ctx', self.forth)]
    ppermute x4, starting transfers between devices: 6.52 us -> 0.36 us  [sum(): up = lax.ppermute(up, 'ctx', self.back)]
    ppermute x0 -> x6, starting transfers between devices: none -> 5.08 us  [swap_small(): lax.ppermute(pick(x, k), 'head', [(h, h ^ k) for h in range(heads_axis)])]
    unnamed x39 -> x42, local copies, waits for them, and re-layouts: 13 us -> 8.74 us
  transfers between devices with their start and end apart: 28 -> 32, of which waited for: 15 -> 14; matrix products, arithmetic and copies ran while one was open for 12% -> 11% of each run, Pallas kernels for 16% -> 17%
where the time goes in v4:
time: 202 us
  waiting for transfers between devices  65 us (32%)
  starting transfers between devices  57.5 us (28%)
  Pallas kernels  37.5 us (19%)
  local copies, waits for them, and re-layouts  16 us (8%)
  between operations  14.6 us (7%)
  other arithmetic  10.8 us (5%)
    all_gather x1, waiting for transfers between devices, local(): around, vis = (lax.all_gather(mine, 'ctx', axis=0, tiled=True), numbers)  28.2 us
    pallas_call x2, Pallas kernels, attend(): pl.pallas_call(functools.partial(attend_kernel, heads=rows // HD, last=(h...  27 us
    all_to_all x4, starting transfers between devices, swap(): return lax.all_to_all(x, 'head', split_axis=0, concat_axis=0, tiled=True)  16.4 us
    ppermute x1, starting transfers between devices, local(): dkv_g, near, far = (None, near_g, lax.ppermute(far_g, 'ctx', partner))  13 us
    pallas_call x3, Pallas kernels, packed(): pl.pallas_call(pack_kernel, grid=(heads_axis,), in_specs=[spec(p) for p i...  10.5 us
    ppermute x4, waiting for transfers between devices, sum(): down = lax.ppermute(down, 'ctx', self.forth)  10.3 us
    ppermute x4, starting transfers between devices, sum(): down = lax.ppermute(down, 'ctx', self.forth)  9.87 us
    unnamed x42, local copies, waits for them, and re-layouts  8.74 us
  transfers between devices with their start and end apart: 32, of which 14 were waited for; matrix products, arithmetic and copies ran while one was open for 11% of the time, Pallas kernels for 17%

profile of v4, /device:TPU:0, one launch (start us, length us, event | category | flops | bytes accessed | tf_op | source)
XLA Modules:
  0.0 201.5 jit_solution(5925296570619578761)
XLA Ops:
  7.2 3.0 %pack_keys.1 = bf16[4,128,512]{2,1,0:T(8,128)(2,1)} custom-call(bf16[128,1024]{1,0:T(8,128)(2,1)} %refs_2_.1, bf16[128,1024]{1,0:T(8,128)(2,1)} %refs_3_.1, bf16[128,1024]{1,0:T(8,128)(2,1)} %refs_2_.1, bf16[128,1024]{1,0:T(8,128)(2,1)} %refs_3_.1), custom_call_target="tpu_custom_call" | custom-call | bytes 1048576 | tf_op jit(solution)/shard_map/pack_keys/pallas_call | solution.py:225
  11.8 2.6 %collective-permute-start.1 = (bf16[128,512]{1,0:T(8,128)(2,1)S(1)}, bf16[128,512]{1,0:T(8,128)(2,1)S(1)}, u32[]{:S(2)}, u32[]{:S(2)}) collective-permute-start(bf16[128,512]{1,0:T(8,128)(2,1)S(1)} %get-tuple-element.107), channel_id=1, source_target_pairs={{0,2},{1,3},{2,0},{3,1},{4,6},{5,7},{6,4},{7,5},{8,10},{9,11},{10,... | collective-permute-start | bytes 393224 | tf_op jit(solution)/shard_map/ppermute | solution.py:310
  14.5 3.8 %pack_rows0.1 = bf16[4,128,2048]{2,1,0:T(8,128)(2,1)} custom-call(bf16[128,8192]{1,0:T(8,128)(2,1)} %refs_0_.4, bf16[128,8192]{1,0:T(8,128)(2,1)} %refs_1_.4), custom_call_target="tpu_custom_call" | custom-call | bytes 4194304 | tf_op jit(solution)/shard_map/pack_rows0/pallas_call | solution.py:225
  18.2 3.7 %all-to-all-start = ((bf16[4,128,2048]{2,1,0:T(8,128)(2,1)}), bf16[4,128,2048]{2,1,0:T(8,128)(2,1)S(1)}, u32[]{:S(2)}, u32[]{:S(2)}) async-start(bf16[4,128,2048]{2,1,0:T(8,128)(2,1)} %pack_rows0.1), calls=%async_computation | async-start | bytes 4194304 | tf_op jit(solution)/shard_map/all_to_all | solution.py:300
  23.9 1.8 collective-permute-start.3
  28.5 4.0 %collective-permute-done.3 = bf16[4,128,256]{2,1,0:T(8,128)(2,1)S(1)} collective-permute-done((bf16[4,128,256]{2,1,0:T(8,128)(2,1)S(1)}, bf16[4,128,256]{2,1,0:T(8,128)(2,1)S(1)}, u32[]{:S(2)}, u32[]{:S(2)}) %collective-permute-start.3) | collective-permute-done | bytes 262176 | tf_op jit(solution)/shard_map/ppermute | solution.py:262
  32.5 1.8 collective-permute-start.5
  34.7 3.8 %pack_rows1.1 = bf16[4,128,2048]{2,1,0:T(8,128)(2,1)} custom-call(bf16[128,8192]{1,0:T(8,128)(2,1)} %refs_0_.4, bf16[128,8192]{1,0:T(8,128)(2,1)} %refs_1_.4), custom_call_target="tpu_custom_call" | custom-call | bytes 4194304 | tf_op jit(solution)/shard_map/pack_rows1/pallas_call | solution.py:225
  40.5 1.8 collective-permute-start.7
  44.0 1.7 constant_dynamic-update-slice_fusion.3
  47.3 1.8 collective-permute-done.8
  49.5 1.8 collective-permute-start.9
  56.6 4.4 %all-to-all-start.2 = ((bf16[4,128,2048]{2,1,0:T(8,128)(2,1)}), bf16[4,128,2048]{2,1,0:T(8,128)(2,1)}, u32[]{:S(2)}, u32[]{:S(2)}) async-start(bf16[4,128,2048]{2,1,0:T(8,128)(2,1)} %pack_rows1.1), calls=%async_computation.2 | async-start | bytes 4194304 | tf_op jit(solution)/shard_map/all_to_all | solution.py:300
  61.1 13.5 %attend0.1 = (bf16[4,128,2048]{2,1,0:T(8,128)(2,1)}, bf16[16,128,256]{2,1,0:T(8,128)(2,1)}, bf16[16,128,256]{2,1,0:T(8,128)(2,1)}) custom-call(s32[4,32]{1,0:T(4,128)} %get-tuple-element.51.vis.into, s32[4,32]{1,0:T(4,128)} %get-tuple-element.50.into, s32[4]{0:T(128)} %get-tuple-element.54.cnt, bf16[4,128,2048]{2,1,0:T(8,128)(2,1)} %copy-done, ...), custom_call_target="tpu_custom_call" | custom-call | flops 40000000000 | bytes 20000000 | tf_op jit(solution)/shard_map/attend0/pallas_call | solution.py:172
  74.6 13.0 %collective-permute-start.11 = (bf16[16,128,256]{2,1,0:T(8,128)(2,1)}, bf16[16,128,256]{2,1,0:T(8,128)(2,1)}, u32[]{:S(2)}, u32[]{:S(2)}) collective-permute-start(bf16[16,128,256]{2,1,0:T(8,128)(2,1)} %get-tuple-element.34), channel_id=1, source_target_pairs={{0,16},{4,20},{8,24},{12,28},{16,0},{20,4},{24,8},{28,12},{1,17},{... | collective-permute-start | bytes 3145736 | tf_op jit(solution)/shard_map/ppermute | solution.py:383
  87.7 4.6 %all-to-all-start.1 = ((bf16[4,128,2048]{2,1,0:T(8,128)(2,1)}), bf16[4,128,2048]{2,1,0:T(8,128)(2,1)}, u32[]{:S(2)}, u32[]{:S(2)}) async-start(bf16[4,128,2048]{2,1,0:T(8,128)(2,1)} %get-tuple-element.35), calls=%async_computation.1 | async-start | bytes 4194304 | tf_op jit(solution)/shard_map/all_to_all | solution.py:300
  92.3 28.2 %all-gather.2.cloned.1.call-done.k.v = bf16[32,128,256]{2,1,0:T(8,128)(2,1)} async-done(((bf16[4,128,256]{2,1,0:T(8,128)(2,1)}), bf16[32,128,256]{2,1,0:T(8,128)(2,1)}) %all-gather.2.cloned.1.call-update) | async-done | bytes 2097168 | tf_op jit(solution)/shard_map/all_gather | solution.py:374
  120.5 13.5 %attend1.1 = (bf16[4,128,2048]{2,1,0:T(8,128)(2,1)}, bf16[16,128,256]{2,1,0:T(8,128)(2,1)}, bf16[16,128,256]{2,1,0:T(8,128)(2,1)}) custom-call(s32[4,32]{1,0:T(4,128)} %copy-done.4, s32[4,32]{1,0:T(4,128)} %get-tuple-element.51.vis.into, s32[4]{0:T(128)} %get-tuple-element.54.cnt, bf16[4,128,2048]{2,1,0:T(8,128)(2,1)} %all-to-all-done.2.qdo, ...), custom_call_target="tpu_custom_call" | custom-call | flops 40000000000 | bytes 20000000 | tf_op jit(solution)/shard_map/attend1/pallas_call | solution.py:172
  134.0 5.6 %collective-permute-done.11 = bf16[16,128,256]{2,1,0:T(8,128)(2,1)} collective-permute-done((bf16[16,128,256]{2,1,0:T(8,128)(2,1)}, bf16[16,128,256]{2,1,0:T(8,128)(2,1)}, u32[]{:S(2)}, u32[]{:S(2)}) %collective-permute-start.11) | collective-permute-done | bytes 1048608 | tf_op jit(solution)/shard_map/ppermute | solution.py:383
  139.6 1.8 fusion.17
  146.3 1.9 collective-permute-start.22
  148.2 3.6 %all-to-all-start.3 = ((bf16[4,128,2048]{2,1,0:T(8,128)(2,1)}), bf16[4,128,2048]{2,1,0:T(8,128)(2,1)S(1)}, u32[]{:S(2)}, u32[]{:S(2)}) async-start(bf16[4,128,2048]{2,1,0:T(8,128)(2,1)} %get-tuple-element.44), calls=%async_computation.3 | async-start | bytes 4194304 | tf_op jit(solution)/shard_map/all_to_all | solution.py:300
  153.2 2.1 %collective-permute-start.17 = (bf16[4,128,256]{2,1,0:T(8,128)(2,1)S(1)}, bf16[4,128,256]{2,1,0:T(8,128)(2,1)S(1)}, u32[]{:S(2)}, u32[]{:S(2)}) collective-permute-start(bf16[4,128,256]{2,1,0:T(8,128)(2,1)S(1)} %pad_maximum_fusion.4), channel_id=1, source_target_pairs={{0,8},{8,16},{16,24},{24,28},{28,20},{20,12},{12,4},{4,0},{1,9},{9... | collective-permute-start | bytes 786440 | tf_op jit(solution)/shard_map/ppermute | solution.py:283
  155.7 6.3 %collective-permute-done.17 = bf16[4,128,256]{2,1,0:T(8,128)(2,1)S(1)} collective-permute-done((bf16[4,128,256]{2,1,0:T(8,128)(2,1)S(1)}, bf16[4,128,256]{2,1,0:T(8,128)(2,1)S(1)}, u32[]{:S(2)}, u32[]{:S(2)}) %collective-permute-start.17) | collective-permute-done | bytes 262176 | tf_op jit(solution)/shard_map/ppermute | solution.py:283
  162.9 3.3 %collective-permute-start.18 = (bf16[4,128,256]{2,1,0:T(8,128)(2,1)S(1)}, bf16[4,128,256]{2,1,0:T(8,128)(2,1)S(1)}, u32[]{:S(2)}, u32[]{:S(2)}) collective-permute-start(bf16[4,128,256]{2,1,0:T(8,128)(2,1)S(1)} %add_convert_fusion.7), channel_id=1, source_target_pairs={{0,8},{8,16},{16,24},{24,28},{28,20},{20,12},{12,4},{4,0},{1,9},{9... | collective-permute-start | bytes 786440 | tf_op jit(solution)/shard_map/ppermute | solution.py:283
  166.4 2.5 %collective-permute-start.23 = (bf16[4,128,256]{2,1,0:T(8,128)(2,1)S(1)}, bf16[4,128,256]{2,1,0:T(8,128)(2,1)S(1)}, u32[]{:S(2)}, u32[]{:S(2)}) collective-permute-start(bf16[4,128,256]{2,1,0:T(8,128)(2,1)S(1)} %pad_maximum_fusion.6), channel_id=1, source_target_pairs={{0,8},{8,12},{12,4},{4,0},{16,24},{24,28},{28,20},{20,16},{1,9},{9... | collective-permute-start | bytes 786440 | tf_op jit(solution)/shard_map/ppermute | solution.py:283
  169.0 4.0 %collective-permute-done.18 = bf16[4,128,256]{2,1,0:T(8,128)(2,1)S(1)} collective-permute-done((bf16[4,128,256]{2,1,0:T(8,128)(2,1)S(1)}, bf16[4,128,256]{2,1,0:T(8,128)(2,1)S(1)}, u32[]{:S(2)}, u32[]{:S(2)}) %collective-permute-start.18) | collective-permute-done | bytes 262176 | tf_op jit(solution)/shard_map/ppermute | solution.py:283
  172.9 4.0 %collective-permute-done.14 = bf16[4,128,256]{2,1,0:T(8,128)(2,1)S(1)} collective-permute-done((bf16[4,128,256]{2,1,0:T(8,128)(2,1)S(1)}, bf16[4,128,256]{2,1,0:T(8,128)(2,1)S(1)}, u32[]{:S(2)}, u32[]{:S(2)}) %collective-permute-start.14) | collective-permute-done | bytes 262176 | tf_op jit(solution)/shard_map/ppermute | solution.py:282
  177.1 2.0 collective-permute-start.19
  180.3 4.7 %collective-permute-done.15 = bf16[4,128,256]{2,1,0:T(8,128)(2,1)S(1)} collective-permute-done((bf16[4,128,256]{2,1,0:T(8,128)(2,1)S(1)}, bf16[4,128,256]{2,1,0:T(8,128)(2,1)S(1)}, u32[]{:S(2)}, u32[]{:S(2)}) %collective-permute-start.15) | collective-permute-done | bytes 262176 | tf_op jit(solution)/shard_map/ppermute | solution.py:282
  189.4 2.2 %collective-permute-done.25 = bf16[128,512]{1,0:T(8,128)(2,1)S(1)} collective-permute-done((bf16[128,512]{1,0:T(8,128)(2,1)S(1)}, bf16[128,512]{1,0:T(8,128)(2,1)S(1)}, u32[]{:S(2)}, u32[]{:S(2)}) %collective-permute-start.25) | collective-permute-done | bytes 131104 | tf_op jit(solution)/shard_map/ppermute | solution.py:310
  191.6 1.9 collective-permute-done.26
  (132 shorter events, 32.2 us)
Async XLA Ops:
  11.3 11.6 %collective-permute-start = (bf16[128,512]{1,0:T(8,128)(2,1)S(1)}, bf16[128,512]{1,0:T(8,128)(2,1)S(1)}, u32[]{:S(2)}, u32[]{:S(2)}) collective-permute-start(bf16[128,512]{1,0:T(8,128)(2,1)S(1)} %get-tuple-element.108), channel_id=1, source_target_pairs={{0,1},{1,0},{2,3},{3,2},{4,5},{5,4},{6,7},{7,6},{8,9},{9,8},{10,11... | collective-permute-start | bytes 393224 | tf_op jit(solution)/shard_map/ppermute | solution.py:310
  11.8 11.1 %collective-permute-start.1 = (bf16[128,512]{1,0:T(8,128)(2,1)S(1)}, bf16[128,512]{1,0:T(8,128)(2,1)S(1)}, u32[]{:S(2)}, u32[]{:S(2)}) collective-permute-start(bf16[128,512]{1,0:T(8,128)(2,1)S(1)} %get-tuple-element.107), channel_id=1, source_target_pairs={{0,2},{1,3},{2,0},{3,1},{4,6},{5,7},{6,4},{7,5},{8,10},{9,11},{10,... | collective-permute-start | bytes 393224 | tf_op jit(solution)/shard_map/ppermute | solution.py:310
  14.4 8.5 %collective-permute-start.2 = (bf16[128,512]{1,0:T(8,128)(2,1)S(1)}, bf16[128,512]{1,0:T(8,128)(2,1)S(1)}, u32[]{:S(2)}, u32[]{:S(2)}) collective-permute-start(bf16[128,512]{1,0:T(8,128)(2,1)S(1)} %get-tuple-element.106), channel_id=1, source_target_pairs={{0,3},{1,2},{2,1},{3,0},{4,7},{5,6},{6,5},{7,4},{8,11},{9,10},{10,... | collective-permute-start | bytes 393224 | tf_op jit(solution)/shard_map/ppermute | solution.py:310
  18.2 37.1 %all-to-all-start = ((bf16[4,128,2048]{2,1,0:T(8,128)(2,1)}), bf16[4,128,2048]{2,1,0:T(8,128)(2,1)S(1)}, u32[]{:S(2)}, u32[]{:S(2)}) async-start(bf16[4,128,2048]{2,1,0:T(8,128)(2,1)} %pack_rows0.1), calls=%async_computation | async-start | bytes 4194304 | tf_op jit(solution)/shard_map/all_to_all | solution.py:300
  22.0 98.5 %all-gather.2.cloned.1.call-start = ((), (), s32[]{:S(2)}) async-start(), calls=%async_computation.4 | async-start | bytes 2359296 | tf_op jit(solution)/shard_map/all_gather | solution.py:374
  23.9 8.6 %collective-permute-start.3 = (bf16[4,128,256]{2,1,0:T(8,128)(2,1)S(1)}, bf16[4,128,256]{2,1,0:T(8,128)(2,1)S(1)}, u32[]{:S(2)}, u32[]{:S(2)}) collective-permute-start(bf16[4,128,256]{2,1,0:T(8,128)(2,1)S(1)} %get-tuple-element.99), channel_id=1, source_target_pairs={{0,8},{8,16},{16,24},{24,28},{28,20},{20,12},{12,4},{4,0},{1,9},{9... | collective-permute-start | bytes 786440 | tf_op jit(solution)/shard_map/ppermute | solution.py:262
  25.7 8.6 %collective-permute-start.4 = (bf16[4,128,256]{2,1,0:T(8,128)(2,1)S(1)}, bf16[4,128,256]{2,1,0:T(8,128)(2,1)S(1)}, u32[]{:S(2)}, u32[]{:S(2)}) collective-permute-start(bf16[4,128,256]{2,1,0:T(8,128)(2,1)S(1)} %get-tuple-element.99), channel_id=1, source_target_pairs={{8,0},{16,8},{24,16},{28,24},{20,28},{12,20},{4,12},{0,4},{9,1},{1... | collective-permute-start | bytes 786440 | tf_op jit(solution)/shard_map/ppermute | solution.py:263
  32.5 8.0 %collective-permute-start.5 = (bf16[4,128,256]{2,1,0:T(8,128)(2,1)S(1)}, bf16[4,128,256]{2,1,0:T(8,128)(2,1)}, u32[]{:S(2)}, u32[]{:S(2)}) collective-permute-start(bf16[4,128,256]{2,1,0:T(8,128)(2,1)S(1)} %collective-permute-done.3), channel_id=1, source_target_pairs={{0,8},{8,16},{16,24},{24,28},{28,20},{20,12},{12,4},{4,0},{1,9},{9... | collective-permute-start | bytes 786440 | tf_op jit(solution)/shard_map/ppermute | solution.py:262
  34.3 8.0 %collective-permute-start.6 = (bf16[4,128,256]{2,1,0:T(8,128)(2,1)S(1)}, bf16[4,128,256]{2,1,0:T(8,128)(2,1)}, u32[]{:S(2)}, u32[]{:S(2)}) collective-permute-start(bf16[4,128,256]{2,1,0:T(8,128)(2,1)S(1)} %collective-permute-done.4), channel_id=1, source_target_pairs={{8,0},{16,8},{24,16},{28,24},{20,28},{12,20},{4,12},{0,4},{9,1},{1... | collective-permute-start | bytes 786440 | tf_op jit(solution)/shard_map/ppermute | solution.py:263
  40.5 9.1 %collective-permute-start.7 = (bf16[4,128,256]{2,1,0:T(8,128)(2,1)}, bf16[4,128,256]{2,1,0:T(8,128)(2,1)S(1)}, u32[]{:S(2)}, u32[]{:S(2)}) collective-permute-start(bf16[4,128,256]{2,1,0:T(8,128)(2,1)} %collective-permute-done.5), channel_id=1, source_target_pairs={{0,8},{8,16},{16,24},{24,28},{28,20},{20,12},{12,4},{4,0},{1,9},{9... | collective-permute-start | bytes 786440 | tf_op jit(solution)/shard_map/ppermute | solution.py:262
  42.3 6.9 %collective-permute-start.8 = (bf16[4,128,256]{2,1,0:T(8,128)(2,1)}, bf16[4,128,256]{2,1,0:T(8,128)(2,1)S(1)}, u32[]{:S(2)}, u32[]{:S(2)}) collective-permute-start(bf16[4,128,256]{2,1,0:T(8,128)(2,1)} %collective-permute-done.6), channel_id=1, source_target_pairs={{8,0},{16,8},{24,16},{28,24},{20,28},{12,20},{4,12},{0,4},{9,1},{1... | collective-permute-start | bytes 786440 | tf_op jit(solution)/shard_map/ppermute | solution.py:263
  49.2 5.0 %collective-permute-start.10 = (bf16[4,128,128]{2,1,0:T(8,128)(2,1)S(1)}, bf16[4,128,128]{2,1,0:T(8,128)(2,1)S(1)}, u32[]{:S(2)}, u32[]{:S(2)}) collective-permute-start(bf16[4,128,128]{2,1,0:T(8,128)(2,1)S(1)} %slice.294), channel_id=1, source_target_pairs={{8,0},{16,8},{24,16},{28,24},{20,28},{12,20},{4,12},{0,4},{9,1},{1... | collective-permute-start | bytes 393224 | tf_op jit(solution)/shard_map/ppermute | solution.py:267
  49.5 5.0 %collective-permute-start.9 = (bf16[4,128,128]{2,1,0:T(8,128)(2,1)S(1)}, bf16[4,128,128]{2,1,0:T(8,128)(2,1)S(1)}, u32[]{:S(2)}, u32[]{:S(2)}) collective-permute-start(bf16[4,128,128]{2,1,0:T(8,128)(2,1)S(1)} %slice.293), channel_id=1, source_target_pairs={{0,8},{8,16},{16,24},{24,28},{28,20},{20,12},{12,4},{4,0},{1,9},{9... | collective-permute-start | bytes 393224 | tf_op jit(solution)/shard_map/ppermute | solution.py:266
  56.6 31.0 %all-to-all-start.2 = ((bf16[4,128,2048]{2,1,0:T(8,128)(2,1)}), bf16[4,128,2048]{2,1,0:T(8,128)(2,1)}, u32[]{:S(2)}, u32[]{:S(2)}) async-start(bf16[4,128,2048]{2,1,0:T(8,128)(2,1)} %pack_rows1.1), calls=%async_computation.2 | async-start | bytes 4194304 | tf_op jit(solution)/shard_map/all_to_all | solution.py:300
  74.6 65.0 %collective-permute-start.11 = (bf16[16,128,256]{2,1,0:T(8,128)(2,1)}, bf16[16,128,256]{2,1,0:T(8,128)(2,1)}, u32[]{:S(2)}, u32[]{:S(2)}) collective-permute-start(bf16[16,128,256]{2,1,0:T(8,128)(2,1)} %get-tuple-element.34), channel_id=1, source_target_pairs={{0,16},{4,20},{8,24},{12,28},{16,0},{20,4},{24,8},{28,12},{1,17},{... | collective-permute-start | bytes 3145736 | tf_op jit(solution)/shard_map/ppermute | solution.py:383
  87.7 51.9 %all-to-all-start.1 = ((bf16[4,128,2048]{2,1,0:T(8,128)(2,1)}), bf16[4,128,2048]{2,1,0:T(8,128)(2,1)}, u32[]{:S(2)}, u32[]{:S(2)}) async-start(bf16[4,128,2048]{2,1,0:T(8,128)(2,1)} %get-tuple-element.35), calls=%async_computation.1 | async-start | bytes 4194304 | tf_op jit(solution)/shard_map/all_to_all | solution.py:300
  141.4 10.5 %collective-permute-start.12 = (bf16[4,128,128]{2,1,0:T(8,128)(2,1)}, bf16[4,128,128]{2,1,0:T(8,128)(2,1)}, u32[]{:S(2)}, u32[]{:S(2)}) collective-permute-start(bf16[4,128,128]{2,1,0:T(8,128)(2,1)} %get-tuple-element.71), channel_id=1, source_target_pairs={{8,0},{16,8},{24,16},{28,24},{20,28},{12,20},{4,12},{0,4},{9,1},{1... | collective-permute-start | bytes 393224 | tf_op jit(solution)/shard_map/ppermute | solution.py:273
  142.0 9.9 %collective-permute-start.16 = (bf16[4,128,128]{2,1,0:T(8,128)(2,1)}, bf16[4,128,128]{2,1,0:T(8,128)(2,1)}, u32[]{:S(2)}, u32[]{:S(2)}) collective-permute-start(bf16[4,128,128]{2,1,0:T(8,128)(2,1)} %get-tuple-element.72), channel_id=1, source_target_pairs={{0,8},{8,16},{16,24},{24,28},{28,20},{20,12},{12,4},{4,0},{1,9},{9... | collective-permute-start | bytes 393224 | tf_op jit(solution)/shard_map/ppermute | solution.py:274
  145.7 9.7 %collective-permute-start.20 = (bf16[4,128,128]{2,1,0:T(8,128)(2,1)}, bf16[4,128,128]{2,1,0:T(8,128)(2,1)S(1)}, u32[]{:S(2)}, u32[]{:S(2)}) collective-permute-start(bf16[4,128,128]{2,1,0:T(8,128)(2,1)} %get-tuple-element.109), channel_id=1, source_target_pairs={{8,0},{12,8},{4,12},{0,4},{24,16},{28,24},{20,28},{16,20},{9,1},{1... | collective-permute-start | bytes 393224 | tf_op jit(solution)/shard_map/ppermute | solution.py:273
  146.3 20.0 %collective-permute-start.22 = (bf16[4,128,128]{2,1,0:T(8,128)(2,1)S(1)}, bf16[4,128,128]{2,1,0:T(8,128)(2,1)S(1)}, u32[]{:S(2)}, u32[]{:S(2)}) collective-permute-start(bf16[4,128,128]{2,1,0:T(8,128)(2,1)S(1)} %get-tuple-element.110), channel_id=1, source_target_pairs={{0,8},{8,12},{12,4},{4,0},{16,24},{24,28},{28,20},{20,16},{1,9},{9... | collective-permute-start | bytes 393224 | tf_op jit(solution)/shard_map/ppermute | solution.py:274
  148.2 36.9 %all-to-all-start.3 = ((bf16[4,128,2048]{2,1,0:T(8,128)(2,1)}), bf16[4,128,2048]{2,1,0:T(8,128)(2,1)S(1)}, u32[]{:S(2)}, u32[]{:S(2)}) async-start(bf16[4,128,2048]{2,1,0:T(8,128)(2,1)} %get-tuple-element.44), calls=%async_computation.3 | async-start | bytes 4194304 | tf_op jit(solution)/shard_map/all_to_all | solution.py:300
  153.2 8.7 %collective-permute-start.17 = (bf16[4,128,256]{2,1,0:T(8,128)(2,1)S(1)}, bf16[4,128,256]{2,1,0:T(8,128)(2,1)S(1)}, u32[]{:S(2)}, u32[]{:S(2)}) collective-permute-start(bf16[4,128,256]{2,1,0:T(8,128)(2,1)S(1)} %pad_maximum_fusion.4), channel_id=1, source_target_pairs={{0,8},{8,16},{16,24},{24,28},{28,20},{20,12},{12,4},{4,0},{1,9},{9... | collective-permute-start | bytes 786440 | tf_op jit(solution)/shard_map/ppermute | solution.py:283
  155.3 10.9 %collective-permute-start.13 = (bf16[4,128,256]{2,1,0:T(8,128)(2,1)S(1)}, bf16[4,128,256]{2,1,0:T(8,128)(2,1)S(1)}, u32[]{:S(2)}, u32[]{:S(2)}) collective-permute-start(bf16[4,128,256]{2,1,0:T(8,128)(2,1)S(1)} %pad_maximum_fusion.3), channel_id=1, source_target_pairs={{8,0},{16,8},{24,16},{28,24},{20,28},{12,20},{4,12},{0,4},{9,1},{1... | collective-permute-start | bytes 786440 | tf_op jit(solution)/shard_map/ppermute | solution.py:282
  155.5 23.6 %collective-permute-start.21 = (bf16[4,128,256]{2,1,0:T(8,128)(2,1)S(1)}, bf16[4,128,256]{2,1,0:T(8,128)(2,1)S(1)}, u32[]{:S(2)}, u32[]{:S(2)}) collective-permute-start(bf16[4,128,256]{2,1,0:T(8,128)(2,1)S(1)} %pad_maximum_fusion.5), channel_id=1, source_target_pairs={{8,0},{12,8},{4,12},{0,4},{24,16},{28,24},{20,28},{16,20},{9,1},{1... | collective-permute-start | bytes 786440 | tf_op jit(solution)/shard_map/ppermute | solution.py:282
  162.9 10.0 %collective-permute-start.18 = (bf16[4,128,256]{2,1,0:T(8,128)(2,1)S(1)}, bf16[4,128,256]{2,1,0:T(8,128)(2,1)S(1)}, u32[]{:S(2)}, u32[]{:S(2)}) collective-permute-start(bf16[4,128,256]{2,1,0:T(8,128)(2,1)S(1)} %add_convert_fusion.7), channel_id=1, source_target_pairs={{0,8},{8,16},{16,24},{24,28},{28,20},{20,12},{12,4},{4,0},{1,9},{9... | collective-permute-start | bytes 786440 | tf_op jit(solution)/shard_map/ppermute | solution.py:283
  166.3 10.6 %collective-permute-start.14 = (bf16[4,128,256]{2,1,0:T(8,128)(2,1)S(1)}, bf16[4,128,256]{2,1,0:T(8,128)(2,1)S(1)}, u32[]{:S(2)}, u32[]{:S(2)}) collective-permute-start(bf16[4,128,256]{2,1,0:T(8,128)(2,1)S(1)} %add_convert_fusion.9), channel_id=1, source_target_pairs={{8,0},{16,8},{24,16},{28,24},{20,28},{12,20},{4,12},{0,4},{9,1},{1... | collective-permute-start | bytes 786440 | tf_op jit(solution)/shard_map/ppermute | solution.py:282
  166.4 12.7 %collective-permute-start.23 = (bf16[4,128,256]{2,1,0:T(8,128)(2,1)S(1)}, bf16[4,128,256]{2,1,0:T(8,128)(2,1)S(1)}, u32[]{:S(2)}, u32[]{:S(2)}) collective-permute-start(bf16[4,128,256]{2,1,0:T(8,128)(2,1)S(1)} %pad_maximum_fusion.6), channel_id=1, source_target_pairs={{0,8},{8,12},{12,4},{4,0},{16,24},{24,28},{28,20},{20,16},{1,9},{9... | collective-permute-start | bytes 786440 | tf_op jit(solution)/shard_map/ppermute | solution.py:283
  177.0 7.9 %collective-permute-start.15 = (bf16[4,128,256]{2,1,0:T(8,128)(2,1)S(1)}, bf16[4,128,256]{2,1,0:T(8,128)(2,1)S(1)}, u32[]{:S(2)}, u32[]{:S(2)}) collective-permute-start(bf16[4,128,256]{2,1,0:T(8,128)(2,1)S(1)} %get-tuple-element.67), channel_id=1, source_target_pairs={{8,0},{16,8},{24,16},{28,24},{20,28},{12,20},{4,12},{0,4},{9,1},{1... | collective-permute-start | bytes 786440 | tf_op jit(solution)/shard_map/ppermute | solution.py:282
  177.1 7.9 %collective-permute-start.19 = (bf16[4,128,256]{2,1,0:T(8,128)(2,1)S(1)}, bf16[4,128,256]{2,1,0:T(8,128)(2,1)S(1)}, u32[]{:S(2)}, u32[]{:S(2)}) collective-permute-start(bf16[4,128,256]{2,1,0:T(8,128)(2,1)S(1)} %get-tuple-element.68), channel_id=1, source_target_pairs={{0,8},{8,16},{16,24},{24,28},{28,20},{20,12},{12,4},{4,0},{1,9},{9... | collective-permute-start | bytes 786440 | tf_op jit(solution)/shard_map/ppermute | solution.py:283
  185.2 4.2 %collective-permute-start.24 = (bf16[128,512]{1,0:T(8,128)(2,1)S(1)}, bf16[128,512]{1,0:T(8,128)(2,1)S(1)}, u32[]{:S(2)}, u32[]{:S(2)}) collective-permute-start(bf16[128,512]{1,0:T(8,128)(2,1)S(1)} %get-tuple-element.80), channel_id=1, source_target_pairs={{0,1},{1,0},{2,3},{3,2},{4,5},{5,4},{6,7},{7,6},{8,9},{9,8},{10,11... | collective-permute-start | bytes 393224 | tf_op jit(solution)/shard_map/ppermute | solution.py:310
  185.3 6.4 %collective-permute-start.25 = (bf16[128,512]{1,0:T(8,128)(2,1)S(1)}, bf16[128,512]{1,0:T(8,128)(2,1)S(1)}, u32[]{:S(2)}, u32[]{:S(2)}) collective-permute-start(bf16[128,512]{1,0:T(8,128)(2,1)S(1)} %get-tuple-element.81), channel_id=1, source_target_pairs={{0,2},{1,3},{2,0},{3,1},{4,6},{5,7},{6,4},{7,5},{8,10},{9,11},{10,... | collective-permute-start | bytes 393224 | tf_op jit(solution)/shard_map/ppermute | solution.py:310
  186.7 6.9 %collective-permute-start.26 = (bf16[128,512]{1,0:T(8,128)(2,1)S(1)}, bf16[128,512]{1,0:T(8,128)(2,1)S(1)}, u32[]{:S(2)}, u32[]{:S(2)}) collective-permute-start(bf16[128,512]{1,0:T(8,128)(2,1)S(1)} %get-tuple-element.82), channel_id=1, source_target_pairs={{0,3},{1,2},{2,1},{3,0},{4,7},{5,6},{6,5},{7,4},{8,11},{9,10},{10,... | collective-permute-start | bytes 393224 | tf_op jit(solution)/shard_map/ppermute | solution.py:310
  (11 other events, 46.1 us)
Sparse Core Ops, SparseCore 0:
  44.1 76.4 all-gather.1
